TPU v7x, 256 devices: a whole 4x4x8 slice. The times are simulated.
256 devices in a mesh: slide: 8 (over y, z_hi), tile: 32 (over x, z_lo, core).
Axes of the slice: x: 4, y: 4, z: 8 (z_hi: 2, z_lo: 4; z = z_hi * 4 + z_lo), core: 2. Of those that a mesh axis runs over, the one named last changes fastest.
Arguments:
- fine_level: bfloat16 [8, 256, 256, 256], P('slide', 'tile'), may hold values from -6 to 6
- coarse_level: bfloat16 [8, 128, 128, 256], P('slide', 'tile'), may hold values from -6 to 6
- fine_kernel: bfloat16 [256, 9, 128], replicated, may hold values from -0.125 to 0.125
- coarse_kernel: bfloat16 [256, 9, 128], replicated, may hold values from -0.125 to 0.125
- fine_gain: float32 [128], replicated, may hold values from 0.25 to 1.75
- fine_offset: float32 [128], replicated, may hold values from -3 to 3
- coarse_gain: float32 [128], replicated, may hold values from 0.25 to 1.75
- coarse_offset: float32 [128], replicated, may hold values from -3 to 3
- class_kernel: bfloat16 [8, 128], replicated
- class_offset: float32 [8], replicated, may hold values from -4 to 4
- tissue_labels: int32 [8, 256, 256], P('slide', 'tile'), may hold values from -1 to 7, as said below
Outputs:
- loss: float32 [], replicated
- head_grads: float32 [12, 128], replicated
- conv_grads: float32 [256, 2, 9, 128], P('tile')
Inputs may be any that keep to these rules, and one draw needn't show every extreme that they name: `tissue_labels`: -1 marks a pixel without tissue, other values are classes.
All inputs are finite; a program needn't handle non-finite values.
Results may differ from a plain program's by a relative error of at most 0.0033.
Values may be sent and summed in bfloat16 or wider, within the bound.
No kernel may reach another device: no remote copies, remote signals or barrier semaphores. Data moves between devices by JAX's collectives and lax.ppermute only.
A program may use at most 128 MiB of HBM per device.

v0:
```python
import jax
import jax.numpy as jnp
from jax import lax
from jax.sharding import PartitionSpec as P

GROUPS = 32


epsilon = 1e-05


def padded_2(cells, sides, width):
    for axis, dim in sides:
        count = lax.axis_size(axis)
        ends = count - 1
        head = lax.slice_in_dim(cells, 0, width, axis=dim)
        tail = lax.slice_in_dim(cells, cells.shape[dim] - width, cells.shape[dim], axis=dim)
        cells = jnp.concatenate(
            [
                lax.ppermute(tail, axis, [(i, (i + 1) % count) for i in range(ends)]),
                cells,
                lax.ppermute(head, axis, [((i + 1) % count, i) for i in range(ends)]),
            ],
            axis=dim,
        )
    return cells


def shifted(padded, height, width, position):
    row_step = position // 3
    col_step = position % 3
    return padded[row_step : row_step + height, col_step : col_step + width].reshape(
        height * width, -1
    )


def convolve(padded, kernel, height, width):
    total = jnp.zeros((height * width, kernel.shape[2]), jnp.float32)
    for position in range(9):
        total = total + jnp.dot(
            shifted(padded, height, width, position),
            kernel[:, position, :],
            preferred_element_type=jnp.float32,
        )
    return total


def group_sums(values, groups):
    return values.reshape(values.shape[0], groups, -1).sum(axis=(0, 2))


def spread(per_group, channels):
    return jnp.repeat(per_group, channels // per_group.shape[0])


def per_device(
    fine_level,
    coarse_level,
    fine_kernel,
    coarse_kernel,
    fine_gain,
    fine_offset,
    coarse_gain,
    coarse_offset,
    class_kernel,
    class_offset,
    tissue_labels,
):
    tiles = lax.axis_size("tile")
    channels = fine_kernel.shape[2]
    in_channels = fine_kernel.shape[0]
    height, width = (fine_level.shape[1], fine_level.shape[2])
    labels = tissue_labels[0].reshape(-1)
    tissue = (labels >= 0).astype(jnp.float32)
    total = lax.psum(jnp.sum(tissue), ("slide", "tile"))
    fine_rows = padded_2(fine_level[0], (("tile", 0),), 1)
    coarse_rows = padded_2(coarse_level[0], (("tile", 0),), 1)
    fine_pad = jnp.pad(fine_rows, ((0, 0), (1, 1), (0, 0)))
    coarse_pad = jnp.pad(coarse_rows, ((0, 0), (1, 1), (0, 0)))
    fine_conv = convolve(fine_pad, fine_kernel, height, width)
    coarse_conv = convolve(coarse_pad, coarse_kernel, height // 2, width // 2)
    stats = lax.psum(
        (
            group_sums(fine_conv, GROUPS),
            group_sums(fine_conv * fine_conv, GROUPS),
            group_sums(coarse_conv, GROUPS),
            group_sums(coarse_conv * coarse_conv, GROUPS),
        ),
        "tile",
    )
    fine_number = height * tiles * width * (channels // GROUPS)
    coarse_number = fine_number // 4

    def normalize(conv_out, first_sum, square_sum, number, gain, offset):
        mean = first_sum / number
        variance = square_sum / number - mean * mean
        scale = spread(lax.rsqrt(variance + epsilon), channels)
        normed = (conv_out - spread(mean, channels)) * scale
        return (normed, scale, normed * gain + offset)

    fine_normed, fine_scale, fine_pre = normalize(
        fine_conv, stats[0], stats[1], fine_number, fine_gain, fine_offset
    )
    coarse_normed, coarse_scale, coarse_pre = normalize(
        coarse_conv, stats[2], stats[3], coarse_number, coarse_gain, coarse_offset
    )
    act_coarse = jnp.maximum(coarse_pre, 0.0).reshape(height // 2, width // 2, channels)
    upsampled = jnp.repeat(jnp.repeat(act_coarse, 2, 0), 2, 1).reshape(height * width, channels)
    merged = (jnp.maximum(fine_pre, 0.0) + upsampled).astype(jnp.bfloat16)
    logits = (
        lax.dot_general(
            class_kernel, merged, (((1,), (1,)), ((), ())), preferred_element_type=jnp.float32
        )
        + class_offset[:, None]
    )
    onehot = (
        labels[None, :] == jnp.arange(class_kernel.shape[0], dtype=jnp.int32)[:, None]
    ).astype(jnp.float32)
    top = jnp.max(logits, axis=0)
    lse = top + jnp.log(jnp.sum(jnp.exp(logits - top[None, :]), axis=0))
    loss_local = jnp.sum((lse - jnp.sum(onehot * logits, axis=0)) * tissue)
    dlogits = ((jnp.exp(logits - lse[None, :]) - onehot) * tissue[None, :] / total).astype(
        jnp.bfloat16
    )
    class_grad = jnp.dot(dlogits, merged, preferred_element_type=jnp.float32)
    dmerged = lax.dot_general(
        dlogits, class_kernel, (((0,), (0,)), ((), ())), preferred_element_type=jnp.float32
    )
    dact_coarse = (
        dmerged.reshape(height // 2, 2, width // 2, 2, channels)
        .sum(axis=(1, 3))
        .reshape(-1, channels)
    )
    fine_dpre = dmerged * (fine_pre > 0).astype(jnp.float32)
    coarse_dpre = dact_coarse * (coarse_pre > 0).astype(jnp.float32)
    fine_dnorm = fine_dpre * fine_gain
    coarse_dnorm = coarse_dpre * coarse_gain
    back = lax.psum(
        (
            group_sums(fine_dnorm, GROUPS),
            group_sums(fine_dnorm * fine_normed, GROUPS),
            group_sums(coarse_dnorm, GROUPS),
            group_sums(coarse_dnorm * coarse_normed, GROUPS),
        ),
        "tile",
    )
    fine_dconv = (
        (
            fine_dnorm
            - spread(back[0] / fine_number, channels)
            - fine_normed * spread(back[1] / fine_number, channels)
        )
        * fine_scale
    ).astype(jnp.bfloat16)
    coarse_dconv = (
        (
            coarse_dnorm
            - spread(back[2] / coarse_number, channels)
            - coarse_normed * spread(back[3] / coarse_number, channels)
        )
        * coarse_scale
    ).astype(jnp.bfloat16)
    head_local = jnp.concatenate(
        [
            jnp.stack(
                [
                    jnp.sum(fine_dpre * fine_normed, axis=0),
                    jnp.sum(fine_dpre, axis=0),
                    jnp.sum(coarse_dpre * coarse_normed, axis=0),
                    jnp.sum(coarse_dpre, axis=0),
                ],
                0,
            ),
            class_grad,
        ],
        0,
    )
    head_grads, loss_total = lax.psum((head_local, loss_local), ("slide", "tile"))
    sections = []
    for padded, upstream, rows_here, cols_here in (
        (fine_pad, fine_dconv, height, width),
        (coarse_pad, coarse_dconv, height // 2, width // 2),
    ):
        stacked = jnp.concatenate(
            [shifted(padded, rows_here, cols_here, position) for position in range(9)], 1
        )
        product = lax.dot_general(
            stacked, upstream, (((0,), (0,)), ((), ())), preferred_element_type=jnp.float32
        )
        sections.append(product.reshape(9, in_channels, channels).transpose(1, 0, 2))
    whole = lax.psum(jnp.stack(sections, 1), "slide")
    conv_grads = lax.psum_scatter(whole, "tile", scatter_dimension=0, tiled=True)
    return (loss_total / total, head_grads, conv_grads)


def solution(mesh):
    return jax.shard_map(
        per_device,
        mesh=mesh,
        in_specs=(
            P("slide", "tile", None, None),
            P("slide", "tile", None, None),
            P(),
            P(),
            P(),
            P(),
            P(),
            P(),
            P(),
            P(),
            P("slide", "tile", None),
        ),
        out_specs=(P(), P(), P("tile", None, None, None)),
        check_vma=False,
    )
```

profile of v0, /device:TPU:32, one launch (start us, length us, event | category | flops | bytes accessed | tf_op | source)
XLA Modules:
  0.0 544.4 jit_solution(6351746061570303099)
XLA Ops:
  8.1 1.9 collective-permute-start.2
  10.0 3.6 collective-permute-start.3
  14.7 2.3 collective-permute-start
  17.0 3.4 collective-permute-start.1
  35.2 1.3 constant_dynamic-update-slice_fusion.8
  40.5 1.6 fusion.80
  42.5 66.5 %all-reduce.4 = (f32[32]{0:T(128)S(1)}, f32[32]{0:T(128)S(1)}, f32[32]{0:T(128)S(1)}, f32[32]{0:T(128)S(1)}) all-reduce(f32[32]{0:T(128)S(1)} %copy-done.30, f32[32]{0:T(128)S(1)} %copy-done.29, f32[32]{0:T(128)S(1)} %reduce_sum.178, f32[32]{0:T(128)S(1)} %reduce_sum.175), channel_id=1, replica_groups=mesh['slide'=8,'tile'=32] {'tile'}, use_global_device_ids=true, to_apply=%region_11.12 | all-reduce | flops 128 | bytes 1024 | tf_op jit(solution)/shard_map/psum | solution.py:82
  113.1 80.6 %psum.89 = f32[]{:T(128)} all-reduce(f32[]{:T(128)} %get-tuple-element.20), channel_id=1, replica_groups=mesh['slide'=8,'tile'=32] {'slide','tile'}, use_global_device_ids=true, to_apply=%region_18.19 | all-reduce | flops 1 | bytes 8 | tf_op jit(solution)/shard_map/psum | solution.py:75
  193.7 4.0 multiply_reduce_fusion.3
  198.2 2.7 reduce_sum.227
  200.9 1.8 multiply_reduce_fusion.4
  203.1 64.3 %all-reduce.3 = (f32[32]{0:T(128)S(1)}, f32[32]{0:T(128)S(1)}, f32[32]{0:T(128)S(1)}, f32[32]{0:T(128)S(1)}) all-reduce(f32[32]{0:T(128)S(1)} %reduce_sum.241, f32[32]{0:T(128)S(1)} %reduce_sum.238, f32[32]{0:T(128)S(1)} %reduce_sum.235, f32[32]{0:T(128)S(1)} %reduce_sum.232), channel_id=1, replica_groups=mesh['slide'=8,'tile'=32] {'tile'}, use_global_device_ids=true, to_apply=%region_36.37 | all-reduce | flops 128 | bytes 1024 | tf_op jit(solution)/shard_map/psum | solution.py:138
  268.1 2.5 constant_dynamic-update-slice_fusion.7
  272.8 1.1 constant_dynamic-update-slice_fusion.4
  275.0 1.2 constant_dynamic-update-slice_fusion.2
  276.3 1.1 constant_dynamic-update-slice_fusion.1
  277.4 1.2 constant_dynamic-update-slice_fusion
  278.6 5.4 fusion.9
  284.1 2.5 fusion.21
  286.5 1.6 pad_maximum_fusion
  288.3 141.8 %reduce-scatter.2.cloned.1.call-done = f32[8,2,9,128]{3,0,2,1:T(8,128)} async-done(((f32[256,2,9,128]{3,0,2,1:T(8,128)}), f32[8,2,9,128]{3,0,2,1:T(8,128)}) %reduce-scatter.2.cloned.1.call-update) | async-done | bytes 73744 | tf_op jit(solution)/shard_map/reduce_scatter | solution.py:192
  431.1 81.4 %all-reduce.2 = (f32[]{:T(128)}, f32[12,128]{1,0:T(8,128)}) all-reduce(f32[]{:T(128)} %get-tuple-element.21, f32[12,128]{1,0:T(8,128)S(1)} %concatenate.33), channel_id=1, replica_groups=mesh['slide'=8,'tile'=32] {'slide','tile'}, use_global_device_ids=true, to_apply=%region_16.17 | all-reduce | flops 1537 | bytes 12296 | tf_op jit(solution)/shard_map/psum | solution.py:178
  513.8 21.1 %all-reduce.7.cloned.1.call-done = f32[8,2,9,128]{3,0,2,1:T(8,128)} async-done(((f32[8,2,9,128]{3,0,2,1:T(8,128)}), f32[8,2,9,128]{3,0,2,1:T(8,128)}) %all-reduce.7.cloned.1.call-update) | async-done | bytes 73744 | tf_op jit(solution)/shard_map/psum | solution.py:191
  534.8 1.6 copy.16
  (173 shorter events, 30.7 us)
Async XLA Ops:
  7.2 104.9 %copy-start = (bf16[8,128]{1,0:T(8,128)(2,1)S(1)}, bf16[8,128]{1,0:T(8,128)(2,1)}, u32[]{:S(2)}) copy-start(bf16[8,128]{1,0:T(8,128)(2,1)} %param.19) | copy-start | bytes 6148
  7.2 422.9 %reduce-scatter.2.cloned.1.call-start = ((), (), s32[]{:S(2)}) async-start(), calls=%async_computation.1 | async-start | bytes 2433024 | tf_op jit(solution)/shard_map/reduce_scatter | solution.py:192
  8.1 13.6 %collective-permute-start.2 = (bf16[1,128,256]{2,1,0:T(8,128)(2,1)S(1)}, bf16[1,128,256]{2,1,0:T(8,128)(2,1)S(1)}, u32[]{:S(2)}, u32[]{:S(2)}) collective-permute-start(bf16[1,128,256]{2,1,0:T(8,128)(2,1)S(1)} %get-tuple-element.53), channel_id=1, source_target_pairs={{0,1},{1,2},{2,3},{3,4},{4,5},{5,6},{6,7},{7,8},{8,9},{9,10},{10,1... | collective-permute-start | bytes 196616 | tf_op jit(solution)/shard_map/ppermute | solution.py:20
  10.0 11.7 %collective-permute-start.3 = (bf16[1,128,256]{2,1,0:T(8,128)(2,1)S(1)}, bf16[1,128,256]{2,1,0:T(8,128)(2,1)S(1)}, u32[]{:S(2)}, u32[]{:S(2)}) collective-permute-start(bf16[1,128,256]{2,1,0:T(8,128)(2,1)S(1)} %get-tuple-element.54), channel_id=1, source_target_pairs={{1,0},{2,1},{3,2},{4,3},{5,4},{6,5},{7,6},{8,7},{9,8},{10,9},{11,1... | collective-permute-start | bytes 196616 | tf_op jit(solution)/shard_map/ppermute | solution.py:22
  14.7 9.1 %copy-start.19 = (bf16[256,9,128]{2,0,1:T(8,128)(2,1)S(1)}, bf16[256,9,128]{2,0,1:T(8,128)(2,1)}, u32[]{:S(2)}) copy-start(bf16[256,9,128]{2,0,1:T(8,128)(2,1)} %param.14) | copy-start | bytes 1769476
  14.7 18.8 %collective-permute-start = (bf16[1,256,256]{2,1,0:T(8,128)(2,1)S(1)}, bf16[1,256,256]{2,1,0:T(8,128)(2,1)S(1)}, u32[]{:S(2)}, u32[]{:S(2)}) collective-permute-start(bf16[1,256,256]{2,1,0:T(8,128)(2,1)S(1)} %get-tuple-element.43), channel_id=1, source_target_pairs={{0,1},{1,2},{2,3},{3,4},{4,5},{5,6},{6,7},{7,8},{8,9},{9,10},{10,1... | collective-permute-start | bytes 393224 | tf_op jit(solution)/shard_map/ppermute | solution.py:20
  17.0 16.5 %collective-permute-start.1 = (bf16[1,256,256]{2,1,0:T(8,128)(2,1)S(1)}, bf16[1,256,256]{2,1,0:T(8,128)(2,1)S(1)}, u32[]{:S(2)}, u32[]{:S(2)}) collective-permute-start(bf16[1,256,256]{2,1,0:T(8,128)(2,1)S(1)} %get-tuple-element.44), channel_id=1, source_target_pairs={{1,0},{2,1},{3,2},{4,3},{5,4},{6,5},{7,6},{8,7},{9,8},{10,9},{11,1... | collective-permute-start | bytes 393224 | tf_op jit(solution)/shard_map/ppermute | solution.py:22
  28.2 5.9 %copy-start.1 = (bf16[1,8,256,256]{3,2,1,0:T(8,128)(2,1)S(1)}, bf16[1,8,256,256]{3,2,1,0:T(8,128)(2,1)}, u32[]{:S(2)}) copy-start(bf16[1,8,256,256]{3,2,1,0:T(8,128)(2,1)} %param.11) | copy-start | bytes 3145732
  35.2 3.0 copy-start.4
  35.2 3.5 copy-start.2
  37.7 2.8 copy-start.8
  40.5 69.3 %copy-start.24 = (f32[128]{0:T(128)S(1)}, f32[128]{0:T(128)}, u32[]{:S(2)}) copy-start(f32[128]{0:T(128)} %param.17) | copy-start | bytes 1540
  40.5 69.3 %copy-start.31 = (f32[128]{0:T(128)S(1)}, f32[128]{0:T(128)}, u32[]{:S(2)}) copy-start(f32[128]{0:T(128)} %param.18) | copy-start | bytes 1540
  42.1 68.3 %copy-start.32 = (f32[128]{0:T(128)S(1)}, f32[128]{0:T(128)}, u32[]{:S(2)}) copy-start(f32[128]{0:T(128)} %param.16) | copy-start | bytes 1540
  42.1 68.3 %copy-start.34 = (f32[128]{0:T(128)S(1)}, f32[128]{0:T(128)}, u32[]{:S(2)}) copy-start(f32[128]{0:T(128)} %param.15) | copy-start | bytes 1540
  109.9 2.5 copy-start.23
  110.0 83.8 %copy-start.22 = (f32[2048]{0:T(1024)S(1)}, f32[2048]{0:T(1024)}, u32[]{:S(2)}) copy-start(f32[2048]{0:T(1024)} %compare_convert_fusion) | copy-start | bytes 24580
  268.1 2.5 copy-start.5
  268.1 3.6 copy-start.3
  278.6 5.4 copy-start.16
  288.2 141.9 %copy-start.13 = (bf16[2048,128]{1,0:T(8,128)(2,1)S(1)}, bf16[2048,128]{1,0:T(8,128)(2,1)}, u32[]{:S(2)}) copy-start(bf16[2048,128]{1,0:T(8,128)(2,1)} %copy-done.12) | copy-start | bytes 1572868
  288.2 142.8 %copy-start.36 = (f32[128]{0:T(128)S(1)}, f32[128]{0:T(128)}, u32[]{:S(2)}) copy-start(f32[128]{0:T(128)} %get-tuple-element.7) | copy-start | bytes 1540
  288.2 142.8 %copy-start.37 = (f32[128]{0:T(128)S(1)}, f32[128]{0:T(128)}, u32[]{:S(2)}) copy-start(f32[128]{0:T(128)} %get-tuple-element.8) | copy-start | bytes 1540
  288.2 246.6 %all-reduce.7.cloned.1.call-start = ((), (), s32[]{:S(2)}) async-start(), calls=%async_computation.2 | async-start | bytes 147456 | tf_op jit(solution)/shard_map/psum | solution.py:191
  (21 other events, 38.6 us)
Sparse Core Ops, SparseCore 0:
  288.3 141.7 reduce-scatter.1
  432.7 102.0 all-reduce.6
where the time goes:
time: 546 us; the launch traced here: 544 us
  blocking collectives  293 us (54%)
  waiting for transfers between devices  163 us (30%)
  local copies, waits for them, and re-layouts  28.8 us (5%)
  matrix products  20 us (4%)
  between operations  17.2 us (3%)
  starting transfers between devices  11.3 us (2%)
  other arithmetic  11.3 us (2%)
    reduce_scatter x1, waiting for transfers between devices, per_device(): lax.psum_scatter(whole, 'tile', scatter_dimension=0, tiled=True)  142 us
    psum x1, blocking collectives, per_device(): lax.psum((head_local, loss_local), ('slide', 'tile'))  81.4 us
    psum x1, blocking collectives, per_device(): total = lax.psum(jnp.sum(tissue), ('slide', 'tile'))  80.6 us
    psum x1, blocking collectives, per_device(): lax.psum((group_sums(fine_conv, GROUPS), group_sums(fine_conv * fine_conv...  66.5 us
    psum x1, blocking collectives, per_device(): lax.psum((group_sums(fine_dnorm, GROUPS), group_sums(fine_dnorm * fine_no...  64.3 us
    unnamed x96, local copies, waits for them, and re-layouts  21.4 us
    psum x1, waiting for transfers between devices, per_device(): whole = lax.psum(jnp.stack(sections, 1), 'slide')  21.1 us
  transfers between devices with their start and end apart: 6, of which 2 were waited for; matrix products, arithmetic and copies ran while one was open for 3% of the time, Pallas kernels for 0%

commit v1 on v0

v1 whole, which is shorter than its diff:
```python
import functools

import jax
import jax.numpy as jnp
from jax import lax
from jax.experimental import pallas as pl
from jax.experimental.pallas import tpu as pltpu
from jax.sharding import PartitionSpec as P

GROUPS = 32
epsilon = 1e-05
F32 = jnp.float32
BF16 = jnp.bfloat16
VMEM_BYTES = 48 * 1024 * 1024


def call(kernel, outs, scratch=(), **more):
    return pl.pallas_call(
        kernel,
        out_shape=outs,
        scratch_shapes=list(scratch),
        compiler_params=pltpu.CompilerParams(vmem_limit_bytes=VMEM_BYTES),
        **more,
    )


def shape(*dims, dtype=F32):
    return jax.ShapeDtypeStruct(dims, dtype)


def moved(values, step):
    count = values.shape[0]
    rows = lax.broadcasted_iota(jnp.int32, values.shape, 0)
    edge = 0 if step > 0 else count - 1
    return jnp.where(rows == edge, 0.0, pltpu.roll(values, step % count, 0))


def taps_of(kernel_ref, row_step):
    return jnp.concatenate([kernel_ref[3 * row_step + b] for b in range(3)], axis=1)


def joined(products, channels):
    left = products[:, :channels]
    middle = products[:, channels : 2 * channels]
    right = products[:, 2 * channels :]
    return moved(left, 1) + middle + moved(right, -1)


def interior_kernel(rows_fine, rows_coarse, fine_ref, coarse_ref, fk_ref, ck_ref, fconv_ref, cconv_ref):
    for x_ref, k_ref, out_ref, rows in (
        (coarse_ref, ck_ref, cconv_ref, rows_coarse),
        (fine_ref, fk_ref, fconv_ref, rows_fine),
    ):
        cols = x_ref.shape[0] // rows
        channels = k_ref.shape[2]
        for row in range(rows):
            total = None
            for a in range(3):
                source = row + a - 1
                if 0 <= source < rows:
                    part = jnp.dot(
                        x_ref[source * cols : (source + 1) * cols, :],
                        taps_of(k_ref, a),
                        preferred_element_type=F32,
                    )
                    total = part if total is None else total + part
            out_ref[row * cols : (row + 1) * cols, :] = joined(total, channels)


def edges_kernel(
    rows_fine,
    rows_coarse,
    fpart_ref,
    cpart_ref,
    above_ref,
    below_ref,
    fk_ref,
    ck_ref,
    fconv_ref,
    cconv_ref,
    stats_ref,
):
    stats_ref[...] = jnp.zeros_like(stats_ref)
    start = 0
    for level, (part_ref, k_ref, out_ref, rows) in enumerate(
        ((fpart_ref, fk_ref, fconv_ref, rows_fine), (cpart_ref, ck_ref, cconv_ref, rows_coarse))
    ):
        cols = part_ref.shape[0] // rows
        channels = k_ref.shape[2]
        first = jnp.zeros((1, channels), F32)
        second = jnp.zeros((1, channels), F32)
        for row in range(rows):
            value = part_ref[row * cols : (row + 1) * cols, :]
            for edge, halo_ref, a in ((0, above_ref, 0), (rows - 1, below_ref, 2)):
                if row == edge:
                    value = value + joined(
                        jnp.dot(
                            halo_ref[start : start + cols, :],
                            taps_of(k_ref, a),
                            preferred_element_type=F32,
                        ),
                        channels,
                    )
            out_ref[row * cols : (row + 1) * cols, :] = value
            first = first + jnp.sum(value, axis=0, keepdims=True)
            second = second + jnp.sum(value * value, axis=0, keepdims=True)
        stats_ref[2 * level : 2 * level + 1, :] = first
        stats_ref[2 * level + 1 : 2 * level + 2, :] = second
        start += cols


def turned_kernel(fine_ref, coarse_ref, above_ref, below_ref, fturn_ref, cturn_ref):
    channels = fine_ref.shape[1]
    tile = lax.axis_index("tile")
    core, z, x = tile % 2, (tile // 2) % 4, tile // 8
    row = lax.broadcasted_iota(jnp.int32, (channels, channels), 0)
    col = lax.broadcasted_iota(jnp.int32, (channels, channels), 1)
    to_core = lax.rem(core + row // 128, 2)
    to_x = lax.rem(x + lax.rem(row // 32, 4), 4)
    to_z = lax.rem(z + lax.rem(row // 8, 4), 4)
    channel = (to_x * 8 + to_z * 2 + to_core) * 8 + lax.rem(row, 8)
    order = (col == channel).astype(F32).astype(BF16)
    start = 0
    for x_ref, out_ref, cols in (
        (fine_ref, fturn_ref, above_ref.shape[0] * 2 // 3),
        (coarse_ref, cturn_ref, above_ref.shape[0] // 3),
    ):
        inner = x_ref.shape[0]
        for ref, at, size, to in (
            (above_ref, start, cols, 0),
            (x_ref, 0, inner, cols),
            (below_ref, start, cols, cols + inner),
        ):
            out_ref[:, to : to + size] = lax.dot_general(
                order, ref[at : at + size, :], (((1,), (1,)), ((), ())), preferred_element_type=F32
            ).astype(BF16)
        start += cols


def same_group(channels):
    per_group = channels // GROUPS
    row = lax.broadcasted_iota(jnp.int32, (channels, channels), 0)
    col = lax.broadcasted_iota(jnp.int32, (channels, channels), 1)
    return (row // per_group == col // per_group).astype(F32)


def over_group(rows, members):
    return jnp.dot(rows, members, precision=lax.Precision.HIGHEST, preferred_element_type=F32)


def norm_terms(sums, level, number):
    mean = sums[2 * level : 2 * level + 1, :] / number
    variance = sums[2 * level + 1 : 2 * level + 2, :] / number - mean * mean
    return mean, lax.rsqrt(variance + epsilon)


def loss_kernel(
    rows_fine,
    numbers,
    fconv_ref,
    cconv_ref,
    stats_ref,
    fgain_ref,
    foffset_ref,
    cgain_ref,
    coffset_ref,
    class_ref,
    bias_ref,
    labels_ref,
    fdpre_ref,
    cdpre_ref,
    head_ref,
    wide_ref,
    sum_ref,
):
    channels = fconv_ref.shape[1]
    cols = fconv_ref.shape[0] // rows_fine
    half = cols // 2
    classes = class_ref.shape[0]
    sums = over_group(stats_ref[...], same_group(channels))
    fmean, fscale = norm_terms(sums, 0, numbers[0])
    cmean, cscale = norm_terms(sums, 1, numbers[1])
    weights = class_ref[...]
    bias = bias_ref[...]
    rows_sum = [jnp.zeros((1, channels), F32) for _ in range(4)]
    class_sum = jnp.zeros((classes, channels), F32)
    loss_sum = jnp.zeros((1, cols), F32)
    tissue_sum = jnp.zeros((1, cols), F32)
    class_id = lax.broadcasted_iota(jnp.int32, (classes, cols), 0)
    for pair in range(rows_fine // 2):
        cnormed = (cconv_ref[pair * half : (pair + 1) * half, :] - cmean) * cscale
        cpre = cnormed * cgain_ref[...] + coffset_ref[...]
        cact = jnp.maximum(cpre, 0.0)
        wide_ref[pl.ds(0, half, stride=2), :] = cact
        wide_ref[pl.ds(1, half, stride=2), :] = cact
        up = wide_ref[...]
        both = None
        for row in (2 * pair, 2 * pair + 1):
            here = slice(row * cols, (row + 1) * cols)
            normed = (fconv_ref[here, :] - fmean) * fscale
            pre = normed * fgain_ref[...] + foffset_ref[...]
            merged = (jnp.maximum(pre, 0.0) + up).astype(BF16)
            logits = (
                lax.dot_general(
                    weights, merged, (((1,), (1,)), ((), ())), preferred_element_type=F32
                )
                + bias
            )
            top = jnp.max(logits, axis=0, keepdims=True)
            lse = top + jnp.log(jnp.sum(jnp.exp(logits - top), axis=0, keepdims=True))
            label = labels_ref[row : row + 1, :]
            tissue = (label >= 0).astype(F32)
            onehot = (label == class_id).astype(F32)
            loss_sum = loss_sum + (lse - jnp.sum(onehot * logits, axis=0, keepdims=True)) * tissue
            tissue_sum = tissue_sum + tissue
            dlogits = (jnp.exp(logits - lse) - onehot) * tissue
            class_sum = class_sum + jnp.dot(
                dlogits.astype(BF16), merged, preferred_element_type=F32
            )
            dmerged = lax.dot_general(
                dlogits.astype(BF16), weights, (((0,), (0,)), ((), ())), preferred_element_type=F32
            )
            dpre = jnp.where(pre > 0, dmerged, 0.0)
            fdpre_ref[here, :] = dpre
            rows_sum[0] = rows_sum[0] + jnp.sum(dpre * normed, axis=0, keepdims=True)
            rows_sum[1] = rows_sum[1] + jnp.sum(dpre, axis=0, keepdims=True)
            both = dmerged if both is None else both + dmerged
        sum_ref[...] = both
        dact = sum_ref[pl.ds(0, half, stride=2), :] + sum_ref[pl.ds(1, half, stride=2), :]
        dpre = jnp.where(cpre > 0, dact, 0.0)
        cdpre_ref[pair * half : (pair + 1) * half, :] = dpre
        rows_sum[2] = rows_sum[2] + jnp.sum(dpre * cnormed, axis=0, keepdims=True)
        rows_sum[3] = rows_sum[3] + jnp.sum(dpre, axis=0, keepdims=True)
    head_ref[...] = jnp.zeros_like(head_ref)
    for at in range(4):
        head_ref[at : at + 1, :] = rows_sum[at]
    head_ref[4 : 4 + classes, :] = class_sum
    lane = lax.broadcasted_iota(jnp.int32, (1, channels), 1)
    loss_all = jnp.sum(loss_sum, axis=1, keepdims=True)
    tissue_all = jnp.sum(tissue_sum, axis=1, keepdims=True)
    head_ref[4 + classes : 5 + classes, :] = jnp.where(
        lane == 0, loss_all, jnp.where(lane == 1, tissue_all, 0.0)
    )


def weights_kernel(
    rows_fine,
    numbers,
    fconv_ref,
    cconv_ref,
    fdpre_ref,
    cdpre_ref,
    stats_ref,
    back_ref,
    fgain_ref,
    cgain_ref,
    fturn_ref,
    cturn_ref,
    keep_ref,
    send_ref,
    fd_ref,
    cd_ref,
):
    channels = fconv_ref.shape[1]
    members = same_group(channels)
    sums = over_group(stats_ref[...], members)
    kept = keep_ref.shape[0] // 16
    for level, (conv_ref, dpre_ref, gain_ref, turn_ref, d_ref, rows) in enumerate(
        (
            (fconv_ref, fdpre_ref, fgain_ref, fturn_ref, fd_ref, rows_fine),
            (cconv_ref, cdpre_ref, cgain_ref, cturn_ref, cd_ref, rows_fine // 2),
        )
    ):
        cols = conv_ref.shape[0] // rows
        mean, scale = norm_terms(sums, level, numbers[level])
        gain = gain_ref[...]
        means = over_group(back_ref[2 * level : 2 * level + 2, :] * gain, members) / numbers[level]
        with_normed, plain = means[0:1, :], means[1:2, :]
        for row in range(rows):
            here = slice(row * cols, (row + 1) * cols)
            normed = (conv_ref[here, :] - mean) * scale
            dconv = (dpre_ref[here, :] * gain - plain - normed * with_normed) * scale
            d_ref[here, :channels] = moved(dconv, -1).astype(BF16)
            d_ref[here, channels : 2 * channels] = dconv.astype(BF16)
            d_ref[here, 2 * channels :] = moved(dconv, 1).astype(BF16)
        for a in range(3):
            product = jnp.dot(
                turn_ref[:, a * cols : a * cols + rows * cols], d_ref[...], preferred_element_type=F32
            )
            wide = product.shape[1]
            span = slice(a * wide, (a + 1) * wide)
            for block in range(product.shape[0] // 8):
                piece = product[8 * block : 8 * block + 8, :]
                at = 16 * (block % kept) + 8 * level
                if block < kept:
                    keep_ref[at : at + 8, span] = piece
                else:
                    send_ref[at : at + 8, span] = piece


def first_sum_kernel(keep_ref, sent_ref, own_ref, *out_refs):
    size = own_ref.shape[0]
    own_ref[...] = keep_ref[:size, :] + sent_ref[:size, :].astype(F32)
    for at, out_ref in enumerate(out_refs):
        here = slice((at + 1) * size, (at + 2) * size)
        out_ref[...] = (keep_ref[here, :] + sent_ref[here, :].astype(F32)).astype(BF16)


def next_sum_kernel(keep_ref, one_ref, two_ref, three_ref, own_ref, *out_refs):
    size = own_ref.shape[0]
    for at, out_ref in enumerate((own_ref, *out_refs)):
        here = slice(at * size, (at + 1) * size)
        out_ref[...] = (
            (keep_ref[here, :] + one_ref[here, :].astype(F32))
            + (two_ref[here, :].astype(F32) + three_ref[here, :].astype(F32))
        ).astype(out_ref.dtype)


def last_tile_kernel(keep_ref, one_ref, two_ref, three_ref, head_ref, out_ref):
    wide = keep_ref.shape[1]
    out_ref[:, :wide] = (keep_ref[...] + one_ref[...].astype(F32)) + (
        two_ref[...].astype(F32) + three_ref[...].astype(F32)
    )
    out_ref[:, wide:] = head_ref[...]


def final_kernel(own_ref, one_ref, two_ref, three_ref, loss_ref, head_ref, grads_ref):
    whole = (own_ref[...] + two_ref[...]) + (one_ref[...] + three_ref[...])
    rows = head_ref.shape[0]
    channels = head_ref.shape[1]
    wide = whole.shape[1] - channels
    head = whole[:, wide:]
    total = head[rows : rows + 1, 1:2]
    loss_ref[...] = head[rows : rows + 1, 0:1] / total
    head_ref[...] = head[:rows, :] / total
    taps = wide // channels
    for level in range(2):
        for tap in range(taps):
            grads_ref[pl.ds(2 * tap + level, 8, stride=2 * taps), :] = (
                whole[8 * level : 8 * level + 8, tap * channels : (tap + 1) * channels] / total
            )


def core_pairs():
    return [(i, i ^ 1) for i in range(32)]


def x_pairs(step):
    return [(i, (i // 8 + step) % 4 * 8 + i % 8) for i in range(32)]


def z_pairs(step):
    return [(i, i // 8 * 8 + (i // 2 + step) % 4 * 2 + i % 2) for i in range(32)]


def tile_sum(values):
    values = values + lax.ppermute(values, "tile", core_pairs())
    for pairs in (x_pairs, z_pairs):
        one, two, three = [lax.ppermute(values, "tile", pairs(step)) for step in (1, 2, 3)]
        values = (values + two) + (one + three)
    return values


def per_device(
    fine_level,
    coarse_level,
    fine_kernel,
    coarse_kernel,
    fine_gain,
    fine_offset,
    coarse_gain,
    coarse_offset,
    class_kernel,
    class_offset,
    tissue_labels,
):
    tiles = lax.axis_size("tile")
    in_channels, _, channels = fine_kernel.shape
    _, height, width, _ = fine_level.shape
    classes = class_kernel.shape[0]
    numbers = (
        float(height * tiles * width * (channels // GROUPS)),
        float(height * tiles * width * (channels // GROUPS) // 4),
    )
    fine_size, coarse_size = height * width, height * width // 4
    fine = fine_level.reshape(fine_size, in_channels)
    coarse = coarse_level.reshape(coarse_size, in_channels)
    fk = fine_kernel.transpose(1, 0, 2)
    ck = coarse_kernel.transpose(1, 0, 2)
    fgain, foffset = fine_gain[None, :], fine_offset[None, :]
    cgain, coffset = coarse_gain[None, :], coarse_offset[None, :]
    labels = tissue_labels[0]

    with jax.named_scope("halo"):
        down = jnp.concatenate([fine[-width:], coarse[-(width // 2) :]], 0)
        up = jnp.concatenate([fine[:width], coarse[: width // 2]], 0)
        above = lax.ppermute(down, "tile", [(i, i + 1) for i in range(tiles - 1)])
        below = lax.ppermute(up, "tile", [(i + 1, i) for i in range(tiles - 1)])
    with jax.named_scope("forward"):
        fpart, cpart = call(
            functools.partial(interior_kernel, height, height // 2),
            (shape(fine_size, channels), shape(coarse_size, channels)),
        )(fine, coarse, fk, ck)
        fconv, cconv, stats = call(
            functools.partial(edges_kernel, height, height // 2),
            (shape(fine_size, channels), shape(coarse_size, channels), shape(8, channels)),
        )(fpart, cpart, above, below, fk, ck)
    with jax.named_scope("turned"):
        fturn, cturn = call(
            turned_kernel,
            (
                shape(in_channels, fine_size + 2 * width, dtype=BF16),
                shape(in_channels, coarse_size + width, dtype=BF16),
            ),
        )(fine, coarse, above, below)
    with jax.named_scope("forward_sums"):
        stats = tile_sum(stats)
    with jax.named_scope("loss_and_head"):
        fdpre, cdpre, head = call(
            functools.partial(loss_kernel, height, numbers),
            (shape(fine_size, channels), shape(coarse_size, channels), shape(16, channels)),
            (pltpu.VMEM((width, channels), F32), pltpu.VMEM((width, channels), F32)),
        )(
            fconv,
            cconv,
            stats,
            fgain,
            foffset,
            cgain,
            coffset,
            class_kernel,
            class_offset[:, None],
            labels,
        )
    with jax.named_scope("backward_sums"):
        head = tile_sum(head)
    with jax.named_scope("weight_grads"):
        wide = 9 * channels
        keep, send = call(
            functools.partial(weights_kernel, height, numbers),
            (shape(in_channels, wide), shape(in_channels, wide)),
            (
                pltpu.VMEM((fine_size, 3 * channels), BF16),
                pltpu.VMEM((coarse_size, 3 * channels), BF16),
            ),
        )(fconv, cconv, fdpre, cdpre, stats, head, fgain, cgain, fturn, cturn)
    with jax.named_scope("over_tiles"):
        sent = lax.ppermute(send.astype(BF16), "tile", core_pairs())
        size = in_channels // 4
        parts = call(
            first_sum_kernel, (shape(size, wide),) + (shape(size, wide, dtype=BF16),) * 3
        )(keep, sent)
        got = [lax.ppermute(parts[step], "tile", x_pairs(step)) for step in (1, 2, 3)]
        size = size // 4
        parts = call(
            next_sum_kernel, (shape(size, wide),) + (shape(size, wide, dtype=BF16),) * 3
        )(parts[0], *got)
        got = [lax.ppermute(parts[step], "tile", z_pairs(step)) for step in (1, 2, 3)]
        own = call(last_tile_kernel, shape(size, wide + channels))(parts[0], *got, head)
    with jax.named_scope("over_slides"):
        slides = lax.axis_size("slide")
        own = own + lax.ppermute(own, "slide", [(i, i ^ 1) for i in range(slides)])
        got = [
            lax.ppermute(own, "slide", [(i, (i + 2 * step) % slides) for i in range(slides)])
            for step in (1, 2, 3)
        ]
        loss, head_grads, grads = call(
            final_kernel,
            (shape(1, 1), shape(4 + classes, channels), shape(in_channels // tiles * 18, channels)),
        )(own, *got)
    conv_grads = grads.reshape(in_channels // tiles, 9, 2, channels).transpose(0, 2, 1, 3)
    return (loss.reshape(()), head_grads, conv_grads)


def solution(mesh):
    return jax.shard_map(
        per_device,
        mesh=mesh,
        in_specs=(
            P("slide", "tile", None, None),
            P("slide", "tile", None, None),
            P(),
            P(),
            P(),
            P(),
            P(),
            P(),
            P(),
            P(),
            P("slide", "tile", None),
        ),
        out_specs=(P(), P(), P("tile", None, None, None)),
        check_vma=False,
    )
```

time: 546 us -> 99.4 us (0.18)
  the two profiles are of different devices: /device:TPU:32 before, /device:TPU:4 now
where the time goes in v1:
time: 99.4 us; the launch traced here: 99.1 us
  starting transfers between devices  42.5 us (43%)
  waiting for transfers between devices  39.2 us (39%)
  Pallas kernels  10.9 us (11%)
  local copies, waits for them, and re-layouts  5.33 us (5%)
    ppermute x12, waiting for transfers between devices, tile_sum(): lax.ppermute(values, 'tile', pairs(step))  15.6 us
    ppermute x12, starting transfers between devices, tile_sum(): lax.ppermute(values, 'tile', pairs(step))  13.9 us
    ppermute x1, starting transfers between devices, per_device(): own = own + lax.ppermute(own, 'slide', [(i, i ^ 1) for i in range(slides)])  7.68 us
    ppermute x3, waiting for transfers between devices, per_device(): lax.ppermute(parts[step], 'tile', x_pairs(step))  7.1 us
    ppermute x1, starting transfers between devices, per_device(): below = lax.ppermute(up, 'tile', [(i + 1, i) for i in range(tiles - 1)])  6.34 us
    ppermute x3, waiting for transfers between devices, per_device(): lax.ppermute(own, 'slide', [(i, (i + 2 * step) % slides) for i in range(s...  5.22 us
    ppermute x3, starting transfers between devices, per_device(): lax.ppermute(own, 'slide', [(i, (i + 2 * step) % slides) for i in range(s...  4.69 us
    pallas_call x1, Pallas kernels, per_device(): call(functools.partial(weights_kernel, height, numbers), (shape(in_channe...  4.34 us
  transfers between devices with their start and end apart: 27, of which 22 were waited for; matrix products, arithmetic and copies ran while one was open for 0% of the time, Pallas kernels for 3%

profile of v1, /device:TPU:4, one launch (start us, length us, event | category | flops | bytes accessed | tf_op | source)
XLA Modules:
  0.0 99.1 jit_solution(17653506536852557280)
XLA Ops:
  2.7 1.9 %collective-permute-start = (bf16[384,256]{1,0:T(8,128)(2,1)S(1)}, bf16[384,256]{1,0:T(8,128)(2,1)S(1)}, u32[]{:S(2)}, u32[]{:S(2)}) collective-permute-start(bf16[384,256]{1,0:T(8,128)(2,1)S(1)} %pad_maximum_fusion), channel_id=1, source_target_pairs={{0,1},{1,2},{2,3},{3,4},{4,5},{5,6},{6,7},{7,8},{8,9},{9,10},{10,1... | collective-permute-start | bytes 589832 | tf_op jit(solution)/shard_map/halo/ppermute | solution.py:397
  4.6 6.3 %collective-permute-start.1 = (bf16[384,256]{1,0:T(8,128)(2,1)S(1)}, bf16[384,256]{1,0:T(8,128)(2,1)S(1)}, u32[]{:S(2)}, u32[]{:S(2)}) collective-permute-start(bf16[384,256]{1,0:T(8,128)(2,1)S(1)} %pad_maximum_fusion.1), channel_id=1, source_target_pairs={{1,0},{2,1},{3,2},{4,3},{5,4},{6,5},{7,6},{8,7},{9,8},{10,9},{11,1... | collective-permute-start | bytes 589832 | tf_op jit(solution)/shard_map/halo/ppermute | solution.py:398
  13.1 2.0 %forward.2 = (f32[2048,128]{1,0:T(8,128)S(1)}, f32[512,128]{1,0:T(8,128)S(1)}) custom-call(bf16[2048,256]{1,0:T(8,128)(2,1)S(1)} %bitcast.22, bf16[512,256]{1,0:T(8,128)(2,1)S(1)} %bitcast.28, bf16[9,256,128]{2,1,0:T(8,128)(2,1)S(1)} %bitcast.24, bf16[9,256,128]{2,1,0:T(8,128)(2,1)S(1)} %bitcast.26), custom_call_target="tpu_custom_call" | custom-call | tf_op jit(solution)/shard_map/forward/pallas_call | solution.py:400
  17.5 1.5 %collective-permute-start.4 = (f32[8,128]{1,0:T(8,128)S(1)}, f32[8,128]{1,0:T(8,128)S(1)}, u32[]{:S(2)}, u32[]{:S(2)}) collective-permute-start(f32[8,128]{1,0:T(8,128)S(1)} %add.45), channel_id=1, source_target_pairs={{0,8},{1,9},{2,10},{3,11},{4,12},{5,13},{6,14},{7,15},{8,16},{9,17... | collective-permute-start | bytes 12296 | tf_op jit(solution)/shard_map/forward_sums/ppermute | solution.py:359
  21.1 3.0 %collective-permute-done.3 = f32[8,128]{1,0:T(8,128)S(1)} collective-permute-done((f32[8,128]{1,0:T(8,128)S(1)}, f32[8,128]{1,0:T(8,128)S(1)}, u32[]{:S(2)}, u32[]{:S(2)}) %collective-permute-start.3) | collective-permute-done | bytes 4128 | tf_op jit(solution)/shard_map/forward_sums/ppermute | solution.py:359
  24.1 3.3 %collective-permute-start.8 = (f32[8,128]{1,0:T(8,128)S(1)}, f32[8,128]{1,0:T(8,128)S(1)}, u32[]{:S(2)}, u32[]{:S(2)}) collective-permute-start(f32[8,128]{1,0:T(8,128)S(1)} %add_add_fusion.3), channel_id=1, source_target_pairs={{0,6},{1,7},{2,0},{3,1},{4,2},{5,3},{6,4},{7,5},{8,14},{9,15},{10,... | collective-permute-start | bytes 12296 | tf_op jit(solution)/shard_map/forward_sums/ppermute | solution.py:359
  28.8 4.1 %collective-permute-done.7 = f32[8,128]{1,0:T(8,128)S(1)} collective-permute-done((f32[8,128]{1,0:T(8,128)S(1)}, f32[8,128]{1,0:T(8,128)S(1)}, u32[]{:S(2)}, u32[]{:S(2)}) %collective-permute-start.7) | collective-permute-done | bytes 4128 | tf_op jit(solution)/shard_map/forward_sums/ppermute | solution.py:359
  33.0 2.4 %loss_and_head.1 = (f32[2048,128]{1,0:T(8,128)S(1)}, f32[512,128]{1,0:T(8,128)S(1)}, f32[16,128]{1,0:T(8,128)S(1)}) custom-call(f32[2048,128]{1,0:T(8,128)S(1)} %get-tuple-element.28.fconv_ref, f32[512,128]{1,0:T(8,128)S(1)} %get-tuple-element.29.cconv_ref, f32[8,128]{1,0:T(8,128)S(1)} %add_add_fusion.2.stats_ref, f32[1,128]{1,0:T(1,128)S(1)} %bitcast.31, ...), custom_call_target="tpu_custom_call" | custom-call | tf_op jit(solution)/shard_map/loss_and_head/pallas_call | solution.py:419
  41.1 2.7 %collective-permute-done.10 = f32[16,128]{1,0:T(8,128)S(1)} collective-permute-done((f32[16,128]{1,0:T(8,128)S(1)}, f32[16,128]{1,0:T(8,128)S(1)}, u32[]{:S(2)}, u32[]{:S(2)}) %collective-permute-start.10) | collective-permute-done | bytes 8224 | tf_op jit(solution)/shard_map/backward_sums/ppermute | solution.py:359
  43.8 2.9 %collective-permute-start.15 = (f32[16,128]{1,0:T(8,128)S(1)}, f32[16,128]{1,0:T(8,128)S(1)}, u32[]{:S(2)}, u32[]{:S(2)}) collective-permute-start(f32[16,128]{1,0:T(8,128)S(1)} %add_add_fusion.1), channel_id=1, source_target_pairs={{0,6},{1,7},{2,0},{3,1},{4,2},{5,3},{6,4},{7,5},{8,14},{9,15},{10,... | collective-permute-start | bytes 24584 | tf_op jit(solution)/shard_map/backward_sums/ppermute | solution.py:359
  49.2 3.0 %collective-permute-done.14 = f32[16,128]{1,0:T(8,128)S(1)} collective-permute-done((f32[16,128]{1,0:T(8,128)S(1)}, f32[16,128]{1,0:T(8,128)S(1)}, u32[]{:S(2)}, u32[]{:S(2)}) %collective-permute-start.14) | collective-permute-done | bytes 8224 | tf_op jit(solution)/shard_map/backward_sums/ppermute | solution.py:359
  52.2 4.3 %weight_grads.1 = (f32[256,1152]{1,0:T(8,128)S(1)}, f32[256,1152]{1,0:T(8,128)S(1)}) custom-call(f32[2048,128]{1,0:T(8,128)S(1)} %get-tuple-element.28.fconv_ref, f32[512,128]{1,0:T(8,128)S(1)} %get-tuple-element.29.cconv_ref, f32[2048,128]{1,0:T(8,128)S(1)} %get-tuple-element.31.fdpre_ref, f32[512,128]{1,0:T(8,128)S(1)} %get-tuple-element.32.cdpre_ref, ...), custom_call_target="tpu_custom_call" | custom-call | tf_op jit(solution)/shard_map/weight_grads/pallas_call | solution.py:439
  56.7 2.0 %collective-permute-done.16.sent_ref = bf16[256,1152]{1,0:T(8,128)(2,1)S(1)} collective-permute-done((bf16[256,1152]{1,0:T(8,128)(2,1)S(1)}, bf16[256,1152]{1,0:T(8,128)(2,1)S(1)}, u32[]{:S(2)}, u32[]{:S(2)}) %collective-permute-start.16) | collective-permute-done | bytes 589856 | tf_op jit(solution)/shard_map/over_tiles/ppermute | solution.py:448
  58.8 2.3 %collective-permute-start.17 = (bf16[64,1152]{1,0:T(8,128)(2,1)S(1)}, bf16[64,1152]{1,0:T(8,128)(2,1)S(1)}, u32[]{:S(2)}, u32[]{:S(2)}) collective-permute-start(bf16[64,1152]{1,0:T(8,128)(2,1)S(1)} %get-tuple-element.39), channel_id=1, source_target_pairs={{0,8},{1,9},{2,10},{3,11},{4,12},{5,13},{6,14},{7,15},{8,16},{9,17... | collective-permute-start | bytes 442376 | tf_op jit(solution)/shard_map/over_tiles/ppermute | solution.py:453
  61.2 1.5 %collective-permute-start.19 = (bf16[64,1152]{1,0:T(8,128)(2,1)S(1)}, bf16[64,1152]{1,0:T(8,128)(2,1)S(1)}, u32[]{:S(2)}, u32[]{:S(2)}) collective-permute-start(bf16[64,1152]{1,0:T(8,128)(2,1)S(1)} %get-tuple-element.41), channel_id=1, source_target_pairs={{0,24},{1,25},{2,26},{3,27},{4,28},{5,29},{6,30},{7,31},{8,0},{9,1... | collective-permute-start | bytes 442376 | tf_op jit(solution)/shard_map/over_tiles/ppermute | solution.py:453
  62.7 2.6 %collective-permute-done.17.one_ref = bf16[64,1152]{1,0:T(8,128)(2,1)S(1)} collective-permute-done((bf16[64,1152]{1,0:T(8,128)(2,1)S(1)}, bf16[64,1152]{1,0:T(8,128)(2,1)S(1)}, u32[]{:S(2)}, u32[]{:S(2)}) %collective-permute-start.17) | collective-permute-done | bytes 147488 | tf_op jit(solution)/shard_map/over_tiles/ppermute | solution.py:453
  65.3 2.9 %collective-permute-done.18.two_ref = bf16[64,1152]{1,0:T(8,128)(2,1)S(1)} collective-permute-done((bf16[64,1152]{1,0:T(8,128)(2,1)S(1)}, bf16[64,1152]{1,0:T(8,128)(2,1)S(1)}, u32[]{:S(2)}, u32[]{:S(2)}) %collective-permute-start.18) | collective-permute-done | bytes 147488 | tf_op jit(solution)/shard_map/over_tiles/ppermute | solution.py:453
  68.2 1.6 %collective-permute-done.19.three_ref = bf16[64,1152]{1,0:T(8,128)(2,1)S(1)} collective-permute-done((bf16[64,1152]{1,0:T(8,128)(2,1)S(1)}, bf16[64,1152]{1,0:T(8,128)(2,1)S(1)}, u32[]{:S(2)}, u32[]{:S(2)}) %collective-permute-start.19) | collective-permute-done | bytes 147488 | tf_op jit(solution)/shard_map/over_tiles/ppermute | solution.py:453
  70.7 2.7 %collective-permute-start.21 = (bf16[16,1152]{1,0:T(8,128)(2,1)S(1)}, bf16[16,1152]{1,0:T(8,128)(2,1)S(1)}, u32[]{:S(2)}, u32[]{:S(2)}) collective-permute-start(bf16[16,1152]{1,0:T(8,128)(2,1)S(1)} %get-tuple-element.44), channel_id=1, source_target_pairs={{0,4},{1,5},{2,6},{3,7},{4,0},{5,1},{6,2},{7,3},{8,12},{9,13},{10,... | collective-permute-start | bytes 110600 | tf_op jit(solution)/shard_map/over_tiles/ppermute | solution.py:458
  73.8 2.0 %collective-permute-done.20.one_ref = bf16[16,1152]{1,0:T(8,128)(2,1)S(1)} collective-permute-done((bf16[16,1152]{1,0:T(8,128)(2,1)S(1)}, bf16[16,1152]{1,0:T(8,128)(2,1)S(1)}, u32[]{:S(2)}, u32[]{:S(2)}) %collective-permute-start.20) | collective-permute-done | bytes 36896 | tf_op jit(solution)/shard_map/over_tiles/ppermute | solution.py:458
  77.4 7.7 %collective-permute-start.23 = (f32[16,1280]{1,0:T(8,128)S(1)}, f32[16,1280]{1,0:T(8,128)S(1)}, u32[]{:S(2)}, u32[]{:S(2)}) collective-permute-start(f32[16,1280]{1,0:T(8,128)S(1)} %over_tiles.5), channel_id=1, source_target_pairs={{0,32},{32,0},{64,96},{96,64},{128,160},{160,128},{192,224},{224,1... | collective-permute-start | bytes 245768 | tf_op jit(solution)/shard_map/over_slides/ppermute | solution.py:462
  85.1 3.3 %collective-permute-done.23 = f32[16,1280]{1,0:T(8,128)S(1)} collective-permute-done((f32[16,1280]{1,0:T(8,128)S(1)}, f32[16,1280]{1,0:T(8,128)S(1)}, u32[]{:S(2)}, u32[]{:S(2)}) %collective-permute-start.23) | collective-permute-done | bytes 81952 | tf_op jit(solution)/shard_map/over_slides/ppermute | solution.py:462
  88.4 3.1 %collective-permute-start.26 = (f32[16,1280]{1,0:T(8,128)S(1)}, f32[16,1280]{1,0:T(8,128)S(1)}, u32[]{:S(2)}, u32[]{:S(2)}) collective-permute-start(f32[16,1280]{1,0:T(8,128)S(1)} %add.59.own_ref), channel_id=1, source_target_pairs={{0,192},{32,224},{64,0},{96,32},{128,64},{160,96},{192,128},{224,1... | collective-permute-start | bytes 245768 | tf_op jit(solution)/shard_map/over_slides/ppermute | solution.py:464
  93.5 3.9 %collective-permute-done.25.two_ref = f32[16,1280]{1,0:T(8,128)S(1)} collective-permute-done((f32[16,1280]{1,0:T(8,128)S(1)}, f32[16,1280]{1,0:T(8,128)S(1)}, u32[]{:S(2)}, u32[]{:S(2)}) %collective-permute-start.25) | collective-permute-done | bytes 81952 | tf_op jit(solution)/shard_map/over_slides/ppermute | solution.py:464
  (80 shorter events, 25.0 us)
Async XLA Ops:
  2.7 12.5 %collective-permute-start = (bf16[384,256]{1,0:T(8,128)(2,1)S(1)}, bf16[384,256]{1,0:T(8,128)(2,1)S(1)}, u32[]{:S(2)}, u32[]{:S(2)}) collective-permute-start(bf16[384,256]{1,0:T(8,128)(2,1)S(1)} %pad_maximum_fusion), channel_id=1, source_target_pairs={{0,1},{1,2},{2,3},{3,4},{4,5},{5,6},{6,7},{7,8},{8,9},{9,10},{10,1... | collective-permute-start | bytes 589832 | tf_op jit(solution)/shard_map/halo/ppermute | solution.py:397
  4.6 10.5 %collective-permute-start.1 = (bf16[384,256]{1,0:T(8,128)(2,1)S(1)}, bf16[384,256]{1,0:T(8,128)(2,1)S(1)}, u32[]{:S(2)}, u32[]{:S(2)}) collective-permute-start(bf16[384,256]{1,0:T(8,128)(2,1)S(1)} %pad_maximum_fusion.1), channel_id=1, source_target_pairs={{1,0},{2,1},{3,2},{4,3},{5,4},{6,5},{7,6},{8,7},{9,8},{10,9},{11,1... | collective-permute-start | bytes 589832 | tf_op jit(solution)/shard_map/halo/ppermute | solution.py:398
  17.0 3.6 %collective-permute-start.5 = (f32[8,128]{1,0:T(8,128)S(1)}, f32[8,128]{1,0:T(8,128)S(1)}, u32[]{:S(2)}, u32[]{:S(2)}) collective-permute-start(f32[8,128]{1,0:T(8,128)S(1)} %add.45), channel_id=1, source_target_pairs={{0,24},{1,25},{2,26},{3,27},{4,28},{5,29},{6,30},{7,31},{8,0},{9,1... | collective-permute-start | bytes 12296 | tf_op jit(solution)/shard_map/forward_sums/ppermute | solution.py:359
  17.5 3.6 %collective-permute-start.4 = (f32[8,128]{1,0:T(8,128)S(1)}, f32[8,128]{1,0:T(8,128)S(1)}, u32[]{:S(2)}, u32[]{:S(2)}) collective-permute-start(f32[8,128]{1,0:T(8,128)S(1)} %add.45), channel_id=1, source_target_pairs={{0,8},{1,9},{2,10},{3,11},{4,12},{5,13},{6,14},{7,15},{8,16},{9,17... | collective-permute-start | bytes 12296 | tf_op jit(solution)/shard_map/forward_sums/ppermute | solution.py:359
  19.0 5.1 %collective-permute-start.3 = (f32[8,128]{1,0:T(8,128)S(1)}, f32[8,128]{1,0:T(8,128)S(1)}, u32[]{:S(2)}, u32[]{:S(2)}) collective-permute-start(f32[8,128]{1,0:T(8,128)S(1)} %add.45), channel_id=1, source_target_pairs={{0,16},{1,17},{2,18},{3,19},{4,20},{5,21},{6,22},{7,23},{8,24},{9,... | collective-permute-start | bytes 12296 | tf_op jit(solution)/shard_map/forward_sums/ppermute | solution.py:359
  24.1 4.7 %collective-permute-start.8 = (f32[8,128]{1,0:T(8,128)S(1)}, f32[8,128]{1,0:T(8,128)S(1)}, u32[]{:S(2)}, u32[]{:S(2)}) collective-permute-start(f32[8,128]{1,0:T(8,128)S(1)} %add_add_fusion.3), channel_id=1, source_target_pairs={{0,6},{1,7},{2,0},{3,1},{4,2},{5,3},{6,4},{7,5},{8,14},{9,15},{10,... | collective-permute-start | bytes 12296 | tf_op jit(solution)/shard_map/forward_sums/ppermute | solution.py:359
  27.5 5.4 %collective-permute-start.7 = (f32[8,128]{1,0:T(8,128)S(1)}, f32[8,128]{1,0:T(8,128)S(1)}, u32[]{:S(2)}, u32[]{:S(2)}) collective-permute-start(f32[8,128]{1,0:T(8,128)S(1)} %add_add_fusion.3), channel_id=1, source_target_pairs={{0,2},{1,3},{2,4},{3,5},{4,6},{5,7},{6,0},{7,1},{8,10},{9,11},{10,... | collective-permute-start | bytes 12296 | tf_op jit(solution)/shard_map/forward_sums/ppermute | solution.py:359
  27.5 5.4 %collective-permute-start.6 = (f32[8,128]{1,0:T(8,128)S(1)}, f32[8,128]{1,0:T(8,128)S(1)}, u32[]{:S(2)}, u32[]{:S(2)}) collective-permute-start(f32[8,128]{1,0:T(8,128)S(1)} %add_add_fusion.3), channel_id=1, source_target_pairs={{0,4},{1,5},{2,6},{3,7},{4,0},{5,1},{6,2},{7,3},{8,12},{9,13},{10,... | collective-permute-start | bytes 12296 | tf_op jit(solution)/shard_map/forward_sums/ppermute | solution.py:359
  36.6 3.7 %collective-permute-start.12 = (f32[16,128]{1,0:T(8,128)S(1)}, f32[16,128]{1,0:T(8,128)S(1)}, u32[]{:S(2)}, u32[]{:S(2)}) collective-permute-start(f32[16,128]{1,0:T(8,128)S(1)} %add.52), channel_id=1, source_target_pairs={{0,24},{1,25},{2,26},{3,27},{4,28},{5,29},{6,30},{7,31},{8,0},{9,1... | collective-permute-start | bytes 24584 | tf_op jit(solution)/shard_map/backward_sums/ppermute | solution.py:359
  37.5 3.7 %collective-permute-start.11 = (f32[16,128]{1,0:T(8,128)S(1)}, f32[16,128]{1,0:T(8,128)S(1)}, u32[]{:S(2)}, u32[]{:S(2)}) collective-permute-start(f32[16,128]{1,0:T(8,128)S(1)} %add.52), channel_id=1, source_target_pairs={{0,8},{1,9},{2,10},{3,11},{4,12},{5,13},{6,14},{7,15},{8,16},{9,17... | collective-permute-start | bytes 24584 | tf_op jit(solution)/shard_map/backward_sums/ppermute | solution.py:359
  38.7 5.2 %collective-permute-start.10 = (f32[16,128]{1,0:T(8,128)S(1)}, f32[16,128]{1,0:T(8,128)S(1)}, u32[]{:S(2)}, u32[]{:S(2)}) collective-permute-start(f32[16,128]{1,0:T(8,128)S(1)} %add.52), channel_id=1, source_target_pairs={{0,16},{1,17},{2,18},{3,19},{4,20},{5,21},{6,22},{7,23},{8,24},{9,... | collective-permute-start | bytes 24584 | tf_op jit(solution)/shard_map/backward_sums/ppermute | solution.py:359
  43.8 5.4 %collective-permute-start.15 = (f32[16,128]{1,0:T(8,128)S(1)}, f32[16,128]{1,0:T(8,128)S(1)}, u32[]{:S(2)}, u32[]{:S(2)}) collective-permute-start(f32[16,128]{1,0:T(8,128)S(1)} %add_add_fusion.1), channel_id=1, source_target_pairs={{0,6},{1,7},{2,0},{3,1},{4,2},{5,3},{6,4},{7,5},{8,14},{9,15},{10,... | collective-permute-start | bytes 24584 | tf_op jit(solution)/shard_map/backward_sums/ppermute | solution.py:359
  46.7 5.4 %collective-permute-start.14 = (f32[16,128]{1,0:T(8,128)S(1)}, f32[16,128]{1,0:T(8,128)S(1)}, u32[]{:S(2)}, u32[]{:S(2)}) collective-permute-start(f32[16,128]{1,0:T(8,128)S(1)} %add_add_fusion.1), channel_id=1, source_target_pairs={{0,2},{1,3},{2,4},{3,5},{4,6},{5,7},{6,0},{7,1},{8,10},{9,11},{10,... | collective-permute-start | bytes 24584 | tf_op jit(solution)/shard_map/backward_sums/ppermute | solution.py:359
  46.7 5.4 %collective-permute-start.13 = (f32[16,128]{1,0:T(8,128)S(1)}, f32[16,128]{1,0:T(8,128)S(1)}, u32[]{:S(2)}, u32[]{:S(2)}) collective-permute-start(f32[16,128]{1,0:T(8,128)S(1)} %add_add_fusion.1), channel_id=1, source_target_pairs={{0,4},{1,5},{2,6},{3,7},{4,0},{5,1},{6,2},{7,3},{8,12},{9,13},{10,... | collective-permute-start | bytes 24584 | tf_op jit(solution)/shard_map/backward_sums/ppermute | solution.py:359
  58.8 6.5 %collective-permute-start.17 = (bf16[64,1152]{1,0:T(8,128)(2,1)S(1)}, bf16[64,1152]{1,0:T(8,128)(2,1)S(1)}, u32[]{:S(2)}, u32[]{:S(2)}) collective-permute-start(bf16[64,1152]{1,0:T(8,128)(2,1)S(1)} %get-tuple-element.39), channel_id=1, source_target_pairs={{0,8},{1,9},{2,10},{3,11},{4,12},{5,13},{6,14},{7,15},{8,16},{9,17... | collective-permute-start | bytes 442376 | tf_op jit(solution)/shard_map/over_tiles/ppermute | solution.py:453
  61.1 7.1 %collective-permute-start.18 = (bf16[64,1152]{1,0:T(8,128)(2,1)S(1)}, bf16[64,1152]{1,0:T(8,128)(2,1)S(1)}, u32[]{:S(2)}, u32[]{:S(2)}) collective-permute-start(bf16[64,1152]{1,0:T(8,128)(2,1)S(1)} %get-tuple-element.40), channel_id=1, source_target_pairs={{0,16},{1,17},{2,18},{3,19},{4,20},{5,21},{6,22},{7,23},{8,24},{9,... | collective-permute-start | bytes 442376 | tf_op jit(solution)/shard_map/over_tiles/ppermute | solution.py:453
  61.2 8.6 %collective-permute-start.19 = (bf16[64,1152]{1,0:T(8,128)(2,1)S(1)}, bf16[64,1152]{1,0:T(8,128)(2,1)S(1)}, u32[]{:S(2)}, u32[]{:S(2)}) collective-permute-start(bf16[64,1152]{1,0:T(8,128)(2,1)S(1)} %get-tuple-element.41), channel_id=1, source_target_pairs={{0,24},{1,25},{2,26},{3,27},{4,28},{5,29},{6,30},{7,31},{8,0},{9,1... | collective-permute-start | bytes 442376 | tf_op jit(solution)/shard_map/over_tiles/ppermute | solution.py:453
  69.9 5.9 %collective-permute-start.20 = (bf16[16,1152]{1,0:T(8,128)(2,1)S(1)}, bf16[16,1152]{1,0:T(8,128)(2,1)S(1)}, u32[]{:S(2)}, u32[]{:S(2)}) collective-permute-start(bf16[16,1152]{1,0:T(8,128)(2,1)S(1)} %get-tuple-element.43), channel_id=1, source_target_pairs={{0,2},{1,3},{2,4},{3,5},{4,6},{5,7},{6,0},{7,1},{8,10},{9,11},{10,... | collective-permute-start | bytes 110600 | tf_op jit(solution)/shard_map/over_tiles/ppermute | solution.py:458
  70.7 5.6 %collective-permute-start.21 = (bf16[16,1152]{1,0:T(8,128)(2,1)S(1)}, bf16[16,1152]{1,0:T(8,128)(2,1)S(1)}, u32[]{:S(2)}, u32[]{:S(2)}) collective-permute-start(bf16[16,1152]{1,0:T(8,128)(2,1)S(1)} %get-tuple-element.44), channel_id=1, source_target_pairs={{0,4},{1,5},{2,6},{3,7},{4,0},{5,1},{6,2},{7,3},{8,12},{9,13},{10,... | collective-permute-start | bytes 110600 | tf_op jit(solution)/shard_map/over_tiles/ppermute | solution.py:458
  73.4 4.0 %collective-permute-start.22 = (bf16[16,1152]{1,0:T(8,128)(2,1)S(1)}, bf16[16,1152]{1,0:T(8,128)(2,1)S(1)}, u32[]{:S(2)}, u32[]{:S(2)}) collective-permute-start(bf16[16,1152]{1,0:T(8,128)(2,1)S(1)} %get-tuple-element.45), channel_id=1, source_target_pairs={{0,6},{1,7},{2,0},{3,1},{4,2},{5,3},{6,4},{7,5},{8,14},{9,15},{10,... | collective-permute-start | bytes 110600 | tf_op jit(solution)/shard_map/over_tiles/ppermute | solution.py:458
  77.4 11.0 %collective-permute-start.23 = (f32[16,1280]{1,0:T(8,128)S(1)}, f32[16,1280]{1,0:T(8,128)S(1)}, u32[]{:S(2)}, u32[]{:S(2)}) collective-permute-start(f32[16,1280]{1,0:T(8,128)S(1)} %over_tiles.5), channel_id=1, source_target_pairs={{0,32},{32,0},{64,96},{96,64},{128,160},{160,128},{192,224},{224,1... | collective-permute-start | bytes 245768 | tf_op jit(solution)/shard_map/over_slides/ppermute | solution.py:462
  88.4 5.2 %collective-permute-start.26 = (f32[16,1280]{1,0:T(8,128)S(1)}, f32[16,1280]{1,0:T(8,128)S(1)}, u32[]{:S(2)}, u32[]{:S(2)}) collective-permute-start(f32[16,1280]{1,0:T(8,128)S(1)} %add.59.own_ref), channel_id=1, source_target_pairs={{0,192},{32,224},{64,0},{96,32},{128,64},{160,96},{192,128},{224,1... | collective-permute-start | bytes 245768 | tf_op jit(solution)/shard_map/over_slides/ppermute | solution.py:464
  91.5 6.0 %collective-permute-start.25 = (f32[16,1280]{1,0:T(8,128)S(1)}, f32[16,1280]{1,0:T(8,128)S(1)}, u32[]{:S(2)}, u32[]{:S(2)}) collective-permute-start(f32[16,1280]{1,0:T(8,128)S(1)} %add.59.own_ref), channel_id=1, source_target_pairs={{0,128},{32,160},{64,192},{96,224},{128,0},{160,32},{192,64},{224,... | collective-permute-start | bytes 245768 | tf_op jit(solution)/shard_map/over_slides/ppermute | solution.py:464
  92.1 6.2 %collective-permute-start.24 = (f32[16,1280]{1,0:T(8,128)S(1)}, f32[16,1280]{1,0:T(8,128)S(1)}, u32[]{:S(2)}, u32[]{:S(2)}) collective-permute-start(f32[16,1280]{1,0:T(8,128)S(1)} %add.59.own_ref), channel_id=1, source_target_pairs={{0,64},{32,96},{64,128},{96,160},{128,192},{160,224},{192,0},{224,... | collective-permute-start | bytes 245768 | tf_op jit(solution)/shard_map/over_slides/ppermute | solution.py:464
  (17 other events, 151.9 us)

commit v2 on v1

--- a/solution.py
+++ b/solution.py
@@ -11,7 +11,7 @@
 epsilon = 1e-05
 F32 = jnp.float32
 BF16 = jnp.bfloat16
-VMEM_BYTES = 48 * 1024 * 1024
+VMEM_BYTES = 24 * 1024 * 1024
 
 
 def call(kernel, outs, scratch=(), **more):
@@ -46,44 +46,118 @@
     return moved(left, 1) + middle + moved(right, -1)
 
 
-def interior_kernel(rows_fine, rows_coarse, fine_ref, coarse_ref, fk_ref, ck_ref, fconv_ref, cconv_ref):
-    for x_ref, k_ref, out_ref, rows in (
-        (coarse_ref, ck_ref, cconv_ref, rows_coarse),
-        (fine_ref, fk_ref, fconv_ref, rows_fine),
-    ):
-        cols = x_ref.shape[0] // rows
-        channels = k_ref.shape[2]
-        for row in range(rows):
-            total = None
-            for a in range(3):
-                source = row + a - 1
-                if 0 <= source < rows:
-                    part = jnp.dot(
-                        x_ref[source * cols : (source + 1) * cols, :],
-                        taps_of(k_ref, a),
-                        preferred_element_type=F32,
-                    )
-                    total = part if total is None else total + part
-            out_ref[row * cols : (row + 1) * cols, :] = joined(total, channels)
+def ends_kernel(fine_ref, coarse_ref, first_ref, last_ref, sems):
+    wide = first_ref.shape[0] * 2 // 3
+    half = first_ref.shape[0] // 3
+    fine_end, coarse_end = fine_ref.shape[0] - wide, coarse_ref.shape[0] - half
+    copies = [
+        pltpu.make_async_copy(source, target, sems.at[at])
+        for at, (source, target) in enumerate(
+            (
+                (fine_ref.at[pl.ds(fine_end, wide)], last_ref.at[pl.ds(0, wide)]),
+                (fine_ref.at[pl.ds(0, wide)], first_ref.at[pl.ds(0, wide)]),
+                (coarse_ref.at[pl.ds(coarse_end, half)], last_ref.at[pl.ds(wide, half)]),
+                (coarse_ref.at[pl.ds(0, half)], first_ref.at[pl.ds(wide, half)]),
+            )
+        )
+    ]
+    for copy in copies:
+        copy.start()
+    for copy in copies:
+        copy.wait()
+
+
+def levels(ref, size, axis=0):
+    rest = ref.shape[axis] - size
+    parts = (pl.ds(0, size), pl.ds(size, rest))
+    return [ref.at[part] if axis == 0 else ref.at[:, part] for part in parts]
+
+
+def channel_order(channels):
+    tile = lax.axis_index("tile")
+    core, z, x = tile % 2, (tile // 2) % 4, tile // 8
+    row = lax.broadcasted_iota(jnp.int32, (channels, channels), 0)
+    col = lax.broadcasted_iota(jnp.int32, (channels, channels), 1)
+    to_core = lax.rem(core + row // 128, 2)
+    to_x = lax.rem(x + lax.rem(row // 32, 4), 4)
+    to_z = lax.rem(z + lax.rem(row // 8, 4), 4)
+    channel = (to_x * 8 + to_z * 2 + to_core) * 8 + lax.rem(row, 8)
+    return (col == channel).astype(F32).astype(BF16)
+
+
+def turn(order, pixels):
+    return lax.dot_general(
+        order, pixels, (((1,), (1,)), ((), ())), preferred_element_type=F32
+    ).astype(BF16)
+
+
+def interior_kernel(
+    rows_fine,
+    rows_coarse,
+    fine_ref,
+    coarse_ref,
+    fk_ref,
+    ck_ref,
+    fgain_ref,
+    foffset_ref,
+    cgain_ref,
+    coffset_ref,
+    bias_ref,
+    conv_ref,
+    turn_ref,
+    vectors_ref,
+):
+    for at, ref in enumerate((fgain_ref, foffset_ref, cgain_ref, coffset_ref)):
+        vectors_ref[at : at + 1, :] = ref[...]
+        vectors_ref[4 + at : 5 + at, :] = ref[...]
+    for at in range(bias_ref.shape[0]):
+        vectors_ref[8 + at : 9 + at, :] = jnp.full((1, vectors_ref.shape[1]), bias_ref[at], F32)
+    fine_size = fine_ref.shape[0]
+    fconv_ref, cconv_ref = levels(conv_ref, fine_size)
+    fturn_ref, cturn_ref = levels(turn_ref, fine_size, 1)
+    level_products(coarse_ref, ck_ref, cconv_ref, rows_coarse)
+    level_products(fine_ref, fk_ref, fconv_ref, rows_fine)
+    order = channel_order(fine_ref.shape[1])
+    cturn_ref[...] = turn(order, coarse_ref[...])
+    fturn_ref[...] = turn(order, fine_ref[...])
+
+
+def level_products(x_ref, k_ref, out_ref, rows):
+    cols = x_ref.shape[0] // rows
+    channels = k_ref.shape[2]
+    for row in range(rows):
+        total = None
+        for a in range(3):
+            source = row + a - 1
+            if 0 <= source < rows:
+                part = jnp.dot(
+                    x_ref[source * cols : (source + 1) * cols, :],
+                    taps_of(k_ref, a),
+                    preferred_element_type=F32,
+                )
+                total = part if total is None else total + part
+        out_ref[row * cols : (row + 1) * cols, :] = joined(total, channels)
 
 
 def edges_kernel(
     rows_fine,
     rows_coarse,
-    fpart_ref,
-    cpart_ref,
+    part_ref,
     above_ref,
     below_ref,
     fk_ref,
     ck_ref,
-    fconv_ref,
-    cconv_ref,
+    conv_ref,
     stats_ref,
 ):
-    stats_ref[...] = jnp.zeros_like(stats_ref)
+    fine_size = part_ref.shape[0] * 4 // 5
+    fpart_ref, cpart_ref = levels(part_ref, fine_size)
+    fconv_ref, cconv_ref = levels(conv_ref, fine_size)
     start = 0
-    for level, (part_ref, k_ref, out_ref, rows) in enumerate(
-        ((fpart_ref, fk_ref, fconv_ref, rows_fine), (cpart_ref, ck_ref, cconv_ref, rows_coarse))
+    found = []
+    for part_ref, k_ref, out_ref, rows in (
+        (fpart_ref, fk_ref, fconv_ref, rows_fine),
+        (cpart_ref, ck_ref, cconv_ref, rows_coarse),
     ):
         cols = part_ref.shape[0] // rows
         channels = k_ref.shape[2]
@@ -104,37 +178,11 @@
             out_ref[row * cols : (row + 1) * cols, :] = value
             first = first + jnp.sum(value, axis=0, keepdims=True)
             second = second + jnp.sum(value * value, axis=0, keepdims=True)
-        stats_ref[2 * level : 2 * level + 1, :] = first
-        stats_ref[2 * level + 1 : 2 * level + 2, :] = second
+        found += [first, second]
         start += cols
-
-
-def turned_kernel(fine_ref, coarse_ref, above_ref, below_ref, fturn_ref, cturn_ref):
-    channels = fine_ref.shape[1]
-    tile = lax.axis_index("tile")
-    core, z, x = tile % 2, (tile // 2) % 4, tile // 8
-    row = lax.broadcasted_iota(jnp.int32, (channels, channels), 0)
-    col = lax.broadcasted_iota(jnp.int32, (channels, channels), 1)
-    to_core = lax.rem(core + row // 128, 2)
-    to_x = lax.rem(x + lax.rem(row // 32, 4), 4)
-    to_z = lax.rem(z + lax.rem(row // 8, 4), 4)
-    channel = (to_x * 8 + to_z * 2 + to_core) * 8 + lax.rem(row, 8)
-    order = (col == channel).astype(F32).astype(BF16)
-    start = 0
-    for x_ref, out_ref, cols in (
-        (fine_ref, fturn_ref, above_ref.shape[0] * 2 // 3),
-        (coarse_ref, cturn_ref, above_ref.shape[0] // 3),
-    ):
-        inner = x_ref.shape[0]
-        for ref, at, size, to in (
-            (above_ref, start, cols, 0),
-            (x_ref, 0, inner, cols),
-            (below_ref, start, cols, cols + inner),
-        ):
-            out_ref[:, to : to + size] = lax.dot_general(
-                order, ref[at : at + size, :], (((1,), (1,)), ((), ())), preferred_element_type=F32
-            ).astype(BF16)
-        start += cols
+    found = jnp.concatenate(found + [jnp.zeros_like(found[0])] * 4, axis=0)
+    for tile in range(stats_ref.shape[0] // 8):
+        stats_ref[8 * tile : 8 * tile + 8, :] = found
 
 
 def same_group(channels):
@@ -144,6 +192,10 @@
     return (row // per_group == col // per_group).astype(F32)
 
 
+def over_tiles(all_ref, count):
+    return jnp.sum(all_ref[...].reshape(-1, count, all_ref.shape[1]), axis=0)
+
+
 def over_group(rows, members):
     return jnp.dot(rows, members, precision=lax.Precision.HIGHEST, preferred_element_type=F32)
 
@@ -157,31 +209,31 @@
 def loss_kernel(
     rows_fine,
     numbers,
-    fconv_ref,
-    cconv_ref,
+    conv_ref,
     stats_ref,
-    fgain_ref,
-    foffset_ref,
-    cgain_ref,
-    coffset_ref,
+    vectors_ref,
     class_ref,
-    bias_ref,
     labels_ref,
-    fdpre_ref,
-    cdpre_ref,
+    dpre_ref,
     head_ref,
     wide_ref,
     sum_ref,
 ):
-    channels = fconv_ref.shape[1]
+    fine_size = conv_ref.shape[0] * 4 // 5
+    fconv_ref, cconv_ref = levels(conv_ref, fine_size)
+    fdpre_ref, cdpre_ref = levels(dpre_ref, fine_size)
+    channels = conv_ref.shape[1]
     cols = fconv_ref.shape[0] // rows_fine
     half = cols // 2
     classes = class_ref.shape[0]
-    sums = over_group(stats_ref[...], same_group(channels))
+    sums = over_group(over_tiles(stats_ref, 8), same_group(channels))
     fmean, fscale = norm_terms(sums, 0, numbers[0])
     cmean, cscale = norm_terms(sums, 1, numbers[1])
     weights = class_ref[...]
-    bias = bias_ref[...]
+    bias = vectors_ref[8 : 8 + classes, 0:1]
+    fgain, foffset = vectors_ref[0:1, :], vectors_ref[1:2, :]
+    cgain, coffset = vectors_ref[2:3, :], vectors_ref[3:4, :]
+    twice = jnp.concatenate([weights.astype(F32)] * 2, axis=0).astype(BF16)
     rows_sum = [jnp.zeros((1, channels), F32) for _ in range(4)]
     class_sum = jnp.zeros((classes, channels), F32)
     loss_sum = jnp.zeros((1, cols), F32)
@@ -189,7 +241,7 @@
     class_id = lax.broadcasted_iota(jnp.int32, (classes, cols), 0)
     for pair in range(rows_fine // 2):
         cnormed = (cconv_ref[pair * half : (pair + 1) * half, :] - cmean) * cscale
-        cpre = cnormed * cgain_ref[...] + coffset_ref[...]
+        cpre = cnormed * cgain + coffset
         cact = jnp.maximum(cpre, 0.0)
         wide_ref[pl.ds(0, half, stride=2), :] = cact
         wide_ref[pl.ds(1, half, stride=2), :] = cact
@@ -198,7 +250,7 @@
         for row in (2 * pair, 2 * pair + 1):
             here = slice(row * cols, (row + 1) * cols)
             normed = (fconv_ref[here, :] - fmean) * fscale
-            pre = normed * fgain_ref[...] + foffset_ref[...]
+            pre = normed * fgain + foffset
             merged = (jnp.maximum(pre, 0.0) + up).astype(BF16)
             logits = (
                 lax.dot_general(
@@ -214,11 +266,12 @@
             loss_sum = loss_sum + (lse - jnp.sum(onehot * logits, axis=0, keepdims=True)) * tissue
             tissue_sum = tissue_sum + tissue
             dlogits = (jnp.exp(logits - lse) - onehot) * tissue
-            class_sum = class_sum + jnp.dot(
-                dlogits.astype(BF16), merged, preferred_element_type=F32
-            )
+            high = dlogits.astype(BF16).astype(F32)
+            parts = jnp.concatenate([high, dlogits - high], axis=0).astype(BF16)
+            class_part = jnp.dot(parts, merged, preferred_element_type=F32)
+            class_sum = class_sum + (class_part[:classes] + class_part[classes:])
             dmerged = lax.dot_general(
-                dlogits.astype(BF16), weights, (((0,), (0,)), ((), ())), preferred_element_type=F32
+                parts, twice, (((0,), (0,)), ((), ())), preferred_element_type=F32
             )
             dpre = jnp.where(pre > 0, dmerged, 0.0)
             fdpre_ref[here, :] = dpre
@@ -231,50 +284,58 @@
         cdpre_ref[pair * half : (pair + 1) * half, :] = dpre
         rows_sum[2] = rows_sum[2] + jnp.sum(dpre * cnormed, axis=0, keepdims=True)
         rows_sum[3] = rows_sum[3] + jnp.sum(dpre, axis=0, keepdims=True)
-    head_ref[...] = jnp.zeros_like(head_ref)
-    for at in range(4):
-        head_ref[at : at + 1, :] = rows_sum[at]
-    head_ref[4 : 4 + classes, :] = class_sum
     lane = lax.broadcasted_iota(jnp.int32, (1, channels), 1)
     loss_all = jnp.sum(loss_sum, axis=1, keepdims=True)
     tissue_all = jnp.sum(tissue_sum, axis=1, keepdims=True)
-    head_ref[4 + classes : 5 + classes, :] = jnp.where(
-        lane == 0, loss_all, jnp.where(lane == 1, tissue_all, 0.0)
-    )
+    counts = jnp.where(lane == 0, loss_all, jnp.where(lane == 1, tissue_all, 0.0))
+    blank = jnp.zeros((11 - classes, channels), F32)
+    head = jnp.concatenate(rows_sum + [class_sum, counts, blank], axis=0)
+    for tile in range(head_ref.shape[0] // 16):
+        head_ref[16 * tile : 16 * tile + 16, :] = head
 
 
 def weights_kernel(
     rows_fine,
     numbers,
-    fconv_ref,
-    cconv_ref,
-    fdpre_ref,
-    cdpre_ref,
+    all_conv_ref,
+    all_dpre_ref,
     stats_ref,
     back_ref,
-    fgain_ref,
-    cgain_ref,
-    fturn_ref,
-    cturn_ref,
+    vectors_ref,
+    all_turn_ref,
+    above_ref,
+    below_ref,
     keep_ref,
     send_ref,
+    head_ref,
     fd_ref,
     cd_ref,
+    wide_ref,
 ):
-    channels = fconv_ref.shape[1]
+    fine_size = fd_ref.shape[0]
+    fconv_ref, cconv_ref = levels(all_conv_ref, fine_size)
+    fdpre_ref, cdpre_ref = levels(all_dpre_ref, fine_size)
+    fturn_ref, cturn_ref = levels(all_turn_ref, fine_size, 1)
+    channels = all_conv_ref.shape[1]
     members = same_group(channels)
-    sums = over_group(stats_ref[...], members)
+    sums = over_group(over_tiles(stats_ref, 8), members)
+    back = over_tiles(back_ref, 16)
+    head_ref[...] = back
     kept = keep_ref.shape[0] // 16
-    for level, (conv_ref, dpre_ref, gain_ref, turn_ref, d_ref, rows) in enumerate(
+    order = channel_order(above_ref.shape[1])
+    above, below = turn(order, above_ref[...]), turn(order, below_ref[...])
+    start = 0
+    for level, (conv_ref, dpre_ref, turn_ref, d_ref, rows) in enumerate(
         (
-            (fconv_ref, fdpre_ref, fgain_ref, fturn_ref, fd_ref, rows_fine),
-            (cconv_ref, cdpre_ref, cgain_ref, cturn_ref, cd_ref, rows_fine // 2),
+            (fconv_ref, fdpre_ref, fturn_ref, fd_ref, rows_fine),
+            (cconv_ref, cdpre_ref, cturn_ref, cd_ref, rows_fine // 2),
         )
     ):
-        cols = conv_ref.shape[0] // rows
+        size = conv_ref.shape[0]
+        cols = size // rows
         mean, scale = norm_terms(sums, level, numbers[level])
-        gain = gain_ref[...]
-        means = over_group(back_ref[2 * level : 2 * level + 2, :] * gain, members) / numbers[level]
+        gain = vectors_ref[2 * level : 2 * level + 1, :]
+        means = over_group(back[2 * level : 2 * level + 2, :] * gain, members) / numbers[level]
         with_normed, plain = means[0:1, :], means[1:2, :]
         for row in range(rows):
             here = slice(row * cols, (row + 1) * cols)
@@ -284,18 +345,31 @@
             d_ref[here, channels : 2 * channels] = dconv.astype(BF16)
             d_ref[here, 2 * channels :] = moved(dconv, 1).astype(BF16)
         for a in range(3):
-            product = jnp.dot(
-                turn_ref[:, a * cols : a * cols + rows * cols], d_ref[...], preferred_element_type=F32
-            )
+            if a == 0:
+                product = jnp.dot(
+                    turn_ref[:, : size - cols], d_ref[cols:, :], preferred_element_type=F32
+                ) + jnp.dot(
+                    above[:, start : start + cols], d_ref[:cols, :], preferred_element_type=F32
+                )
+            elif a == 1:
+                product = jnp.dot(turn_ref[...], d_ref[...], preferred_element_type=F32)
+            else:
+                product = jnp.dot(
+                    turn_ref[:, cols:], d_ref[: size - cols, :], preferred_element_type=F32
+                ) + jnp.dot(
+                    below[:, start : start + cols],
+                    d_ref[size - cols :, :],
+                    preferred_element_type=F32,
+                )
             wide = product.shape[1]
             span = slice(a * wide, (a + 1) * wide)
             for block in range(product.shape[0] // 8):
                 piece = product[8 * block : 8 * block + 8, :]
                 at = 16 * (block % kept) + 8 * level
-                if block < kept:
-                    keep_ref[at : at + 8, span] = piece
-                else:
-                    send_ref[at : at + 8, span] = piece
+                to_ref = keep_ref if block < kept else wide_ref
+                to_ref[at : at + 8, span] = piece
+        start += cols
+    send_ref[...] = wide_ref[...].astype(BF16)
 
 
 def first_sum_kernel(keep_ref, sent_ref, own_ref, *out_refs):
@@ -351,14 +425,6 @@
 
 def z_pairs(step):
     return [(i, i // 8 * 8 + (i // 2 + step) % 4 * 2 + i % 2) for i in range(32)]
-
-
-def tile_sum(values):
-    values = values + lax.ppermute(values, "tile", core_pairs())
-    for pairs in (x_pairs, z_pairs):
-        one, two, three = [lax.ppermute(values, "tile", pairs(step)) for step in (1, 2, 3)]
-        values = (values + two) + (one + three)
-    return values
 
 
 def per_device(
@@ -383,69 +449,68 @@
         float(height * tiles * width * (channels // GROUPS) // 4),
     )
     fine_size, coarse_size = height * width, height * width // 4
+    pixels = fine_size + coarse_size
     fine = fine_level.reshape(fine_size, in_channels)
     coarse = coarse_level.reshape(coarse_size, in_channels)
     fk = fine_kernel.transpose(1, 0, 2)
     ck = coarse_kernel.transpose(1, 0, 2)
-    fgain, foffset = fine_gain[None, :], fine_offset[None, :]
-    cgain, coffset = coarse_gain[None, :], coarse_offset[None, :]
     labels = tissue_labels[0]
+    vectors = [fine_gain, fine_offset, coarse_gain, coarse_offset]
+    vectors = [vector[None, :] for vector in vectors]
 
     with jax.named_scope("halo"):
-        down = jnp.concatenate([fine[-width:], coarse[-(width // 2) :]], 0)
-        up = jnp.concatenate([fine[:width], coarse[: width // 2]], 0)
+        ends = shape(width + width // 2, in_channels, dtype=BF16)
+        up, down = call(
+            ends_kernel,
+            (ends, ends),
+            (pltpu.SemaphoreType.DMA((4,)),),
+            in_specs=[pl.BlockSpec(memory_space=pltpu.HBM)] * 2,
+        )(fine, coarse)
         above = lax.ppermute(down, "tile", [(i, i + 1) for i in range(tiles - 1)])
         below = lax.ppermute(up, "tile", [(i + 1, i) for i in range(tiles - 1)])
     with jax.named_scope("forward"):
-        fpart, cpart = call(
+        whole = pl.BlockSpec(memory_space=pltpu.VMEM)
+        part, turned, vectors = call(
             functools.partial(interior_kernel, height, height // 2),
-            (shape(fine_size, channels), shape(coarse_size, channels)),
-        )(fine, coarse, fk, ck)
-        fconv, cconv, stats = call(
+            (
+                shape(pixels, channels),
+                shape(in_channels, pixels, dtype=BF16),
+                shape(8 + classes, channels),
+            ),
+            in_specs=[whole] * 8 + [pl.BlockSpec(memory_space=pltpu.SMEM)],
+        )(fine, coarse, fk, ck, *vectors, class_offset)
+        conv, stats = call(
             functools.partial(edges_kernel, height, height // 2),
-            (shape(fine_size, channels), shape(coarse_size, channels), shape(8, channels)),
-        )(fpart, cpart, above, below, fk, ck)
-    with jax.named_scope("turned"):
-        fturn, cturn = call(
-            turned_kernel,
-            (
-                shape(in_channels, fine_size + 2 * width, dtype=BF16),
-                shape(in_channels, coarse_size + width, dtype=BF16),
-            ),
-        )(fine, coarse, above, below)
+            (shape(pixels, channels), shape(8 * tiles, channels)),
+            input_output_aliases={0: 0},
+        )(part, above, below, fk, ck)
     with jax.named_scope("forward_sums"):
-        stats = tile_sum(stats)
+        stats = lax.all_to_all(stats, "tile", 0, 0, tiled=True)
     with jax.named_scope("loss_and_head"):
-        fdpre, cdpre, head = call(
+        dpre, head = call(
             functools.partial(loss_kernel, height, numbers),
-            (shape(fine_size, channels), shape(coarse_size, channels), shape(16, channels)),
+            (shape(pixels, channels), shape(16 * tiles, channels)),
             (pltpu.VMEM((width, channels), F32), pltpu.VMEM((width, channels), F32)),
-        )(
-            fconv,
-            cconv,
-            stats,
-            fgain,
-            foffset,
-            cgain,
-            coffset,
-            class_kernel,
-            class_offset[:, None],
-            labels,
-        )
+        )(conv, stats, vectors, class_kernel, labels)
     with jax.named_scope("backward_sums"):
-        head = tile_sum(head)
+        head = lax.all_to_all(head, "tile", 0, 0, tiled=True)
     with jax.named_scope("weight_grads"):
         wide = 9 * channels
-        keep, send = call(
+        keep, send, head = call(
             functools.partial(weights_kernel, height, numbers),
-            (shape(in_channels, wide), shape(in_channels, wide)),
+            (
+                shape(in_channels, wide),
+                shape(in_channels, wide, dtype=BF16),
+                shape(16, channels),
+            ),
             (
                 pltpu.VMEM((fine_size, 3 * channels), BF16),
                 pltpu.VMEM((coarse_size, 3 * channels), BF16),
+                pltpu.VMEM((in_channels, wide), F32),
             ),
-        )(fconv, cconv, fdpre, cdpre, stats, head, fgain, cgain, fturn, cturn)
+        )(conv, dpre, stats, head, vectors, turned, above, below)
     with jax.named_scope("over_tiles"):
-        sent = lax.ppermute(send.astype(BF16), "tile", core_pairs())
+        sent = lax.ppermute(send, "tile", core_pairs())
         size = in_channels // 4
         parts = call(
             first_sum_kernel, (shape(size, wide),) + (shape(size, wide, dtype=BF16),) * 3

time: 99.4 us -> 94.1 us (0.947)
  the two profiles are of different devices: /device:TPU:4 before, /device:TPU:32 now
where the time goes in v2:
time: 94.1 us; the launch traced here: 93.5 us
  blocking collectives  31.6 us (34%)
  starting transfers between devices  26.9 us (29%)
  waiting for transfers between devices  21 us (22%)
  Pallas kernels  11 us (12%)
  local copies, waits for them, and re-layouts  2.23 us (2%)
    all_to_all x1, blocking collectives, per_device(): stats = lax.all_to_all(stats, 'tile', 0, 0, tiled=True)  17.4 us
    all_to_all x1, blocking collectives, per_device(): head = lax.all_to_all(head, 'tile', 0, 0, tiled=True)  14.2 us
    ppermute x1, starting transfers between devices, per_device(): own = own + lax.ppermute(own, 'slide', [(i, i ^ 1) for i in range(slides)])  7.28 us
    ppermute x3, waiting for transfers between devices, per_device(): lax.ppermute(parts[step], 'tile', x_pairs(step))  6.83 us
    ppermute x3, waiting for transfers between devices, per_device(): lax.ppermute(own, 'slide', [(i, (i + 2 * step) % slides) for i in range(s...  5.22 us
    ppermute x3, starting transfers between devices, per_device(): lax.ppermute(parts[step], 'tile', z_pairs(step))  4.76 us
    ppermute x3, starting transfers between devices, per_device(): lax.ppermute(own, 'slide', [(i, (i + 2 * step) % slides) for i in range(s...  4.69 us
    ppermute x3, starting transfers between devices, per_device(): lax.ppermute(parts[step], 'tile', x_pairs(step))  4.24 us
  transfers between devices with their start and end apart: 13, of which 10 were waited for; matrix products, arithmetic and copies ran while one was open for 0% of the time, Pallas kernels for 3%

profile of v2, /device:TPU:32, one launch (start us, length us, event | category | flops | bytes accessed | tf_op | source)
XLA Modules:
  0.0 93.5 jit_solution(2730337325745086698)
XLA Ops:
  0.7 1.2 %copy-done = bf16[1,8,256,256]{3,2,1,0:T(8,128)(2,1)S(1)} copy-done((bf16[1,8,256,256]{3,2,1,0:T(8,128)(2,1)S(1)}, bf16[1,8,256,256]{3,2,1,0:T(8,128)(2,1)}, u32[]{:S(2)}) %copy-start) | copy-done | bytes 1048600
  1.9 0.9 %copy-done.3 = bf16[1,4,128,256]{3,2,1,0:T(8,128)(2,1)S(1)} copy-done((bf16[1,4,128,256]{3,2,1,0:T(8,128)(2,1)S(1)}, bf16[1,4,128,256]{3,2,1,0:T(8,128)(2,1)}, u32[]{:S(2)}) %copy-start.3) | copy-done | bytes 262168
  3.4 1.9 %collective-permute-start = (bf16[384,256]{1,0:T(8,128)(2,1)S(1)}, bf16[384,256]{1,0:T(8,128)(2,1)S(1)}, u32[]{:S(2)}, u32[]{:S(2)}) collective-permute-start(bf16[384,256]{1,0:T(8,128)(2,1)S(1)} %get-tuple-element.27), channel_id=1, source_target_pairs={{0,1},{1,2},{2,3},{3,4},{4,5},{5,6},{6,7},{7,8},{8,9},{9,10},{10,1... | collective-permute-start | bytes 589832 | tf_op jit(solution)/shard_map/halo/ppermute | solution.py:469
  5.4 3.6 %collective-permute-start.1 = (bf16[384,256]{1,0:T(8,128)(2,1)S(1)}, bf16[384,256]{1,0:T(8,128)(2,1)S(1)}, u32[]{:S(2)}, u32[]{:S(2)}) collective-permute-start(bf16[384,256]{1,0:T(8,128)(2,1)S(1)} %get-tuple-element.28), channel_id=1, source_target_pairs={{1,0},{2,1},{3,2},{4,3},{5,4},{6,5},{7,6},{8,7},{9,8},{10,9},{11,1... | collective-permute-start | bytes 589832 | tf_op jit(solution)/shard_map/halo/ppermute | solution.py:470
  9.1 3.0 %forward.2 = (f32[2560,128]{1,0:T(8,128)S(1)}, bf16[256,2560]{1,0:T(8,128)(2,1)S(1)}, f32[16,128]{1,0:T(8,128)S(1)}) custom-call(bf16[2048,256]{1,0:T(8,128)(2,1)S(1)} %bitcast.18, bf16[512,256]{1,0:T(8,128)(2,1)S(1)} %bitcast.26, bf16[9,256,128]{2,1,0:T(8,128)(2,1)S(1)} %bitcast.19, bf16[9,256,128]{2,1,0:T(8,128)(2,1)S(1)} %bitcast.21, ...), custom_call_target="tpu_custom_call" | custom-call | tf_op jit(solution)/shard_map/forward/pallas_call | solution.py:473
  12.1 0.8 collective-permute-done.1.below_ref
  13.7 17.4 %all_to_all.22 = f32[32,8,128]{2,1,0:T(8,128)S(1)} all-to-all(f32[32,8,128]{2,1,0:T(8,128)S(1)} %bitcast.29), channel_id=1, replica_groups=mesh['slide'=8,'tile'=32] {'tile'}, dimensions={0} | all-to-all | bytes 262144 | tf_op jit(solution)/shard_map/forward_sums/all_to_all | solution.py:488
  31.1 2.5 %loss_and_head.1 = (f32[2560,128]{1,0:T(8,128)S(1)}, f32[512,128]{1,0:T(8,128)S(1)}) custom-call(f32[2560,128]{1,0:T(8,128)S(1)} %get-tuple-element.29.conv_ref.all_conv_ref, f32[256,128]{1,0:T(8,128)S(1)} %bitcast.23, f32[16,128]{1,0:T(8,128)S(1)} %get-tuple-element.31.vectors_ref, bf16[8,128]{1,0:T(8,128)(2,1)S(1)} %copy-done.5, s32[8,256]{1,0:T(8,128)S(1)} %bitcast.30), custom_call_target="tpu_custom_call" | custom-call | tf_op jit(solution)/shard_map/loss_and_head/pallas_call | solution.py:490
  33.6 14.2 %all_to_all.23 = f32[32,16,128]{2,1,0:T(8,128)S(1)} all-to-all(f32[32,16,128]{2,1,0:T(8,128)S(1)} %bitcast.28), channel_id=1, replica_groups=mesh['slide'=8,'tile'=32] {'tile'}, dimensions={0} | all-to-all | bytes 524288 | tf_op jit(solution)/shard_map/backward_sums/all_to_all | solution.py:496
  47.8 3.2 %weight_grads.1 = (f32[256,1152]{1,0:T(8,128)S(1)}, bf16[256,1152]{1,0:T(8,128)(2,1)S(1)}, f32[16,128]{1,0:T(8,128)S(1)}) custom-call(f32[2560,128]{1,0:T(8,128)S(1)} %get-tuple-element.29.conv_ref.all_conv_ref, f32[2560,128]{1,0:T(8,128)S(1)} %get-tuple-element.32.all_dpre_ref, f32[256,128]{1,0:T(8,128)S(1)} %bitcast.24, f32[512,128]{1,0:T(8,128)S(1)} %bitcast.27, ...), custom_call_target="tpu_custom_call" | custom-call | tf_op jit(solution)/shard_map/weight_grads/pallas_call | solution.py:499
  51.4 1.7 %collective-permute-done.2.sent_ref = bf16[256,1152]{1,0:T(8,128)(2,1)S(1)} collective-permute-done((bf16[256,1152]{1,0:T(8,128)(2,1)S(1)}, bf16[256,1152]{1,0:T(8,128)(2,1)S(1)}, u32[]{:S(2)}, u32[]{:S(2)}) %collective-permute-start.2) | collective-permute-done | bytes 589856 | tf_op jit(solution)/shard_map/over_tiles/ppermute | solution.py:513
  53.8 2.0 %collective-permute-start.4 = (bf16[64,1152]{1,0:T(8,128)(2,1)S(1)}, bf16[64,1152]{1,0:T(8,128)(2,1)S(1)}, u32[]{:S(2)}, u32[]{:S(2)}) collective-permute-start(bf16[64,1152]{1,0:T(8,128)(2,1)S(1)} %get-tuple-element.39), channel_id=1, source_target_pairs={{0,16},{1,17},{2,18},{3,19},{4,20},{5,21},{6,22},{7,23},{8,24},{9,... | collective-permute-start | bytes 442376 | tf_op jit(solution)/shard_map/over_tiles/ppermute | solution.py:518
  55.8 1.6 %collective-permute-start.5 = (bf16[64,1152]{1,0:T(8,128)(2,1)S(1)}, bf16[64,1152]{1,0:T(8,128)(2,1)S(1)}, u32[]{:S(2)}, u32[]{:S(2)}) collective-permute-start(bf16[64,1152]{1,0:T(8,128)(2,1)S(1)} %get-tuple-element.40), channel_id=1, source_target_pairs={{0,24},{1,25},{2,26},{3,27},{4,28},{5,29},{6,30},{7,31},{8,0},{9,1... | collective-permute-start | bytes 442376 | tf_op jit(solution)/shard_map/over_tiles/ppermute | solution.py:518
  57.5 6.2 %collective-permute-done.3.one_ref = bf16[64,1152]{1,0:T(8,128)(2,1)S(1)} collective-permute-done((bf16[64,1152]{1,0:T(8,128)(2,1)S(1)}, bf16[64,1152]{1,0:T(8,128)(2,1)S(1)}, u32[]{:S(2)}, u32[]{:S(2)}) %collective-permute-start.3) | collective-permute-done | bytes 147488 | tf_op jit(solution)/shard_map/over_tiles/ppermute | solution.py:518
  64.4 1.3 %collective-permute-start.6 = (bf16[16,1152]{1,0:T(8,128)(2,1)S(1)}, bf16[16,1152]{1,0:T(8,128)(2,1)S(1)}, u32[]{:S(2)}, u32[]{:S(2)}) collective-permute-start(bf16[16,1152]{1,0:T(8,128)(2,1)S(1)} %get-tuple-element.42), channel_id=1, source_target_pairs={{0,2},{1,3},{2,4},{3,5},{4,6},{5,7},{6,0},{7,1},{8,10},{9,11},{10,... | collective-permute-start | bytes 110600 | tf_op jit(solution)/shard_map/over_tiles/ppermute | solution.py:523
  65.6 3.5 %collective-permute-start.7 = (bf16[16,1152]{1,0:T(8,128)(2,1)S(1)}, bf16[16,1152]{1,0:T(8,128)(2,1)S(1)}, u32[]{:S(2)}, u32[]{:S(2)}) collective-permute-start(bf16[16,1152]{1,0:T(8,128)(2,1)S(1)} %get-tuple-element.43), channel_id=1, source_target_pairs={{0,4},{1,5},{2,6},{3,7},{4,0},{5,1},{6,2},{7,3},{8,12},{9,13},{10,... | collective-permute-start | bytes 110600 | tf_op jit(solution)/shard_map/over_tiles/ppermute | solution.py:523
  69.2 2.4 %collective-permute-done.7.two_ref = bf16[16,1152]{1,0:T(8,128)(2,1)S(1)} collective-permute-done((bf16[16,1152]{1,0:T(8,128)(2,1)S(1)}, bf16[16,1152]{1,0:T(8,128)(2,1)S(1)}, u32[]{:S(2)}, u32[]{:S(2)}) %collective-permute-start.7) | collective-permute-done | bytes 36896 | tf_op jit(solution)/shard_map/over_tiles/ppermute | solution.py:523
  71.6 1.5 %collective-permute-done.8.three_ref = bf16[16,1152]{1,0:T(8,128)(2,1)S(1)} collective-permute-done((bf16[16,1152]{1,0:T(8,128)(2,1)S(1)}, bf16[16,1152]{1,0:T(8,128)(2,1)S(1)}, u32[]{:S(2)}, u32[]{:S(2)}) %collective-permute-start.8) | collective-permute-done | bytes 36896 | tf_op jit(solution)/shard_map/over_tiles/ppermute | solution.py:523
  73.1 7.3 %collective-permute-start.9 = (f32[16,1280]{1,0:T(8,128)S(1)}, f32[16,1280]{1,0:T(8,128)S(1)}, u32[]{:S(2)}, u32[]{:S(2)}) collective-permute-start(f32[16,1280]{1,0:T(8,128)S(1)} %over_tiles.5), channel_id=1, source_target_pairs={{0,32},{32,0},{64,96},{96,64},{128,160},{160,128},{192,224},{224,1... | collective-permute-start | bytes 245768 | tf_op jit(solution)/shard_map/over_slides/ppermute | solution.py:527
  80.4 2.4 %collective-permute-done.9 = f32[16,1280]{1,0:T(8,128)S(1)} collective-permute-done((f32[16,1280]{1,0:T(8,128)S(1)}, f32[16,1280]{1,0:T(8,128)S(1)}, u32[]{:S(2)}, u32[]{:S(2)}) %collective-permute-start.9) | collective-permute-done | bytes 81952 | tf_op jit(solution)/shard_map/over_slides/ppermute | solution.py:527
  82.8 3.1 %collective-permute-start.12 = (f32[16,1280]{1,0:T(8,128)S(1)}, f32[16,1280]{1,0:T(8,128)S(1)}, u32[]{:S(2)}, u32[]{:S(2)}) collective-permute-start(f32[16,1280]{1,0:T(8,128)S(1)} %add.3.own_ref), channel_id=1, source_target_pairs={{0,192},{32,224},{64,0},{96,32},{128,64},{160,96},{192,128},{224,1... | collective-permute-start | bytes 245768 | tf_op jit(solution)/shard_map/over_slides/ppermute | solution.py:529
  86.6 1.0 %collective-permute-start.10 = (f32[16,1280]{1,0:T(8,128)S(1)}, f32[16,1280]{1,0:T(8,128)S(1)}, u32[]{:S(2)}, u32[]{:S(2)}) collective-permute-start(f32[16,1280]{1,0:T(8,128)S(1)} %add.3.own_ref), channel_id=1, source_target_pairs={{0,64},{32,96},{64,128},{96,160},{128,192},{160,224},{192,0},{224,... | collective-permute-start | bytes 245768 | tf_op jit(solution)/shard_map/over_slides/ppermute | solution.py:529
  88.1 3.9 %collective-permute-done.11.two_ref = f32[16,1280]{1,0:T(8,128)S(1)} collective-permute-done((f32[16,1280]{1,0:T(8,128)S(1)}, f32[16,1280]{1,0:T(8,128)S(1)}, u32[]{:S(2)}, u32[]{:S(2)}) %collective-permute-start.11) | collective-permute-done | bytes 81952 | tf_op jit(solution)/shard_map/over_slides/ppermute | solution.py:529
  91.9 0.8 collective-permute-done.10.one_ref
  (36 shorter events, 5.1 us)
Async XLA Ops:
  0.6 8.4 %copy-start.10 = (f32[8]{0:T(128)S(1)}, f32[8]{0:T(128)}, u32[]{:S(2)}) copy-start(f32[8]{0:T(128)} %bias_ref.1) | copy-start | bytes 100
  0.6 8.4 %copy-start.9 = (f32[128]{0:T(128)S(1)}, f32[128]{0:T(128)}, u32[]{:S(2)}) copy-start(f32[128]{0:T(128)} %param.18) | copy-start | bytes 1540
  0.7 8.4 %copy-start.8 = (f32[128]{0:T(128)S(1)}, f32[128]{0:T(128)}, u32[]{:S(2)}) copy-start(f32[128]{0:T(128)} %param.17) | copy-start | bytes 1540
  0.7 8.4 %copy-start.7 = (f32[128]{0:T(128)S(1)}, f32[128]{0:T(128)}, u32[]{:S(2)}) copy-start(f32[128]{0:T(128)} %param.16) | copy-start | bytes 1540
  0.7 8.4 %copy-start.6 = (f32[128]{0:T(128)S(1)}, f32[128]{0:T(128)}, u32[]{:S(2)}) copy-start(f32[128]{0:T(128)} %param.15) | copy-start | bytes 1540
  0.7 1.3 %copy-start = (bf16[1,8,256,256]{3,2,1,0:T(8,128)(2,1)S(1)}, bf16[1,8,256,256]{3,2,1,0:T(8,128)(2,1)}, u32[]{:S(2)}) copy-start(bf16[1,8,256,256]{3,2,1,0:T(8,128)(2,1)} %param.11) | copy-start | bytes 3145732
  1.9 0.9 %copy-start.3 = (bf16[1,4,128,256]{3,2,1,0:T(8,128)(2,1)S(1)}, bf16[1,4,128,256]{3,2,1,0:T(8,128)(2,1)}, u32[]{:S(2)}) copy-start(bf16[1,4,128,256]{3,2,1,0:T(8,128)(2,1)} %param.12) | copy-start | bytes 786436
  2.9 6.2 %copy-start.1 = (bf16[256,9,128]{2,0,1:T(8,128)(2,1)S(1)}, bf16[256,9,128]{2,0,1:T(8,128)(2,1)}, u32[]{:S(2)}) copy-start(bf16[256,9,128]{2,0,1:T(8,128)(2,1)} %param.13) | copy-start | bytes 1769476
  2.9 6.2 %copy-start.2 = (bf16[256,9,128]{2,0,1:T(8,128)(2,1)S(1)}, bf16[256,9,128]{2,0,1:T(8,128)(2,1)}, u32[]{:S(2)}) copy-start(bf16[256,9,128]{2,0,1:T(8,128)(2,1)} %param.14) | copy-start | bytes 1769476
  3.4 8.6 %collective-permute-start = (bf16[384,256]{1,0:T(8,128)(2,1)S(1)}, bf16[384,256]{1,0:T(8,128)(2,1)S(1)}, u32[]{:S(2)}, u32[]{:S(2)}) collective-permute-start(bf16[384,256]{1,0:T(8,128)(2,1)S(1)} %get-tuple-element.27), channel_id=1, source_target_pairs={{0,1},{1,2},{2,3},{3,4},{4,5},{5,6},{6,7},{7,8},{8,9},{9,10},{10,1... | collective-permute-start | bytes 589832 | tf_op jit(solution)/shard_map/halo/ppermute | solution.py:469
  5.4 7.5 %collective-permute-start.1 = (bf16[384,256]{1,0:T(8,128)(2,1)S(1)}, bf16[384,256]{1,0:T(8,128)(2,1)S(1)}, u32[]{:S(2)}, u32[]{:S(2)}) collective-permute-start(bf16[384,256]{1,0:T(8,128)(2,1)S(1)} %get-tuple-element.28), channel_id=1, source_target_pairs={{1,0},{2,1},{3,2},{4,3},{5,4},{6,5},{7,6},{8,7},{9,8},{10,9},{11,1... | collective-permute-start | bytes 589832 | tf_op jit(solution)/shard_map/halo/ppermute | solution.py:470
  12.9 18.2 %copy-start.4 = (s32[1,8,256]{2,1,0:T(8,128)S(1)}, s32[1,8,256]{2,1,0:T(8,128)}, u32[]{:S(2)}) copy-start(s32[1,8,256]{2,1,0:T(8,128)} %param.21) | copy-start | bytes 24580
  12.9 18.2 %copy-start.5 = (bf16[8,128]{1,0:T(8,128)(2,1)S(1)}, bf16[8,128]{1,0:T(8,128)(2,1)}, u32[]{:S(2)}) copy-start(bf16[8,128]{1,0:T(8,128)(2,1)} %class_ref.1) | copy-start | bytes 6148
  51.0 2.1 %collective-permute-start.2 = (bf16[256,1152]{1,0:T(8,128)(2,1)S(1)}, bf16[256,1152]{1,0:T(8,128)(2,1)S(1)}, u32[]{:S(2)}, u32[]{:S(2)}) collective-permute-start(bf16[256,1152]{1,0:T(8,128)(2,1)S(1)} %get-tuple-element.36), channel_id=1, source_target_pairs={{0,1},{1,0},{2,3},{3,2},{4,5},{5,4},{6,7},{7,6},{8,9},{9,8},{10,11... | collective-permute-start | bytes 1769480 | tf_op jit(solution)/shard_map/over_tiles/ppermute | solution.py:513
  53.2 10.5 %collective-permute-start.3 = (bf16[64,1152]{1,0:T(8,128)(2,1)S(1)}, bf16[64,1152]{1,0:T(8,128)(2,1)S(1)}, u32[]{:S(2)}, u32[]{:S(2)}) collective-permute-start(bf16[64,1152]{1,0:T(8,128)(2,1)S(1)} %get-tuple-element.38), channel_id=1, source_target_pairs={{0,8},{1,9},{2,10},{3,11},{4,12},{5,13},{6,14},{7,15},{8,16},{9,17... | collective-permute-start | bytes 442376 | tf_op jit(solution)/shard_map/over_tiles/ppermute | solution.py:518
  53.8 9.9 %collective-permute-start.4 = (bf16[64,1152]{1,0:T(8,128)(2,1)S(1)}, bf16[64,1152]{1,0:T(8,128)(2,1)S(1)}, u32[]{:S(2)}, u32[]{:S(2)}) collective-permute-start(bf16[64,1152]{1,0:T(8,128)(2,1)S(1)} %get-tuple-element.39), channel_id=1, source_target_pairs={{0,16},{1,17},{2,18},{3,19},{4,20},{5,21},{6,22},{7,23},{8,24},{9,... | collective-permute-start | bytes 442376 | tf_op jit(solution)/shard_map/over_tiles/ppermute | solution.py:518
  55.8 8.5 %collective-permute-start.5 = (bf16[64,1152]{1,0:T(8,128)(2,1)S(1)}, bf16[64,1152]{1,0:T(8,128)(2,1)S(1)}, u32[]{:S(2)}, u32[]{:S(2)}) collective-permute-start(bf16[64,1152]{1,0:T(8,128)(2,1)S(1)} %get-tuple-element.40), channel_id=1, source_target_pairs={{0,24},{1,25},{2,26},{3,27},{4,28},{5,29},{6,30},{7,31},{8,0},{9,1... | collective-permute-start | bytes 442376 | tf_op jit(solution)/shard_map/over_tiles/ppermute | solution.py:518
  64.4 4.8 %collective-permute-start.6 = (bf16[16,1152]{1,0:T(8,128)(2,1)S(1)}, bf16[16,1152]{1,0:T(8,128)(2,1)S(1)}, u32[]{:S(2)}, u32[]{:S(2)}) collective-permute-start(bf16[16,1152]{1,0:T(8,128)(2,1)S(1)} %get-tuple-element.42), channel_id=1, source_target_pairs={{0,2},{1,3},{2,4},{3,5},{4,6},{5,7},{6,0},{7,1},{8,10},{9,11},{10,... | collective-permute-start | bytes 110600 | tf_op jit(solution)/shard_map/over_tiles/ppermute | solution.py:523
  65.6 5.9 %collective-permute-start.7 = (bf16[16,1152]{1,0:T(8,128)(2,1)S(1)}, bf16[16,1152]{1,0:T(8,128)(2,1)S(1)}, u32[]{:S(2)}, u32[]{:S(2)}) collective-permute-start(bf16[16,1152]{1,0:T(8,128)(2,1)S(1)} %get-tuple-element.43), channel_id=1, source_target_pairs={{0,4},{1,5},{2,6},{3,7},{4,0},{5,1},{6,2},{7,3},{8,12},{9,13},{10,... | collective-permute-start | bytes 110600 | tf_op jit(solution)/shard_map/over_tiles/ppermute | solution.py:523
  69.1 4.0 %collective-permute-start.8 = (bf16[16,1152]{1,0:T(8,128)(2,1)S(1)}, bf16[16,1152]{1,0:T(8,128)(2,1)S(1)}, u32[]{:S(2)}, u32[]{:S(2)}) collective-permute-start(bf16[16,1152]{1,0:T(8,128)(2,1)S(1)} %get-tuple-element.44), channel_id=1, source_target_pairs={{0,6},{1,7},{2,0},{3,1},{4,2},{5,3},{6,4},{7,5},{8,14},{9,15},{10,... | collective-permute-start | bytes 110600 | tf_op jit(solution)/shard_map/over_tiles/ppermute | solution.py:523
  73.1 9.7 %collective-permute-start.9 = (f32[16,1280]{1,0:T(8,128)S(1)}, f32[16,1280]{1,0:T(8,128)S(1)}, u32[]{:S(2)}, u32[]{:S(2)}) collective-permute-start(f32[16,1280]{1,0:T(8,128)S(1)} %over_tiles.5), channel_id=1, source_target_pairs={{0,32},{32,0},{64,96},{96,64},{128,160},{160,128},{192,224},{224,1... | collective-permute-start | bytes 245768 | tf_op jit(solution)/shard_map/over_slides/ppermute | solution.py:527
  82.8 5.2 %collective-permute-start.12 = (f32[16,1280]{1,0:T(8,128)S(1)}, f32[16,1280]{1,0:T(8,128)S(1)}, u32[]{:S(2)}, u32[]{:S(2)}) collective-permute-start(f32[16,1280]{1,0:T(8,128)S(1)} %add.3.own_ref), channel_id=1, source_target_pairs={{0,192},{32,224},{64,0},{96,32},{128,64},{160,96},{192,128},{224,1... | collective-permute-start | bytes 245768 | tf_op jit(solution)/shard_map/over_slides/ppermute | solution.py:529
  85.9 6.0 %collective-permute-start.11 = (f32[16,1280]{1,0:T(8,128)S(1)}, f32[16,1280]{1,0:T(8,128)S(1)}, u32[]{:S(2)}, u32[]{:S(2)}) collective-permute-start(f32[16,1280]{1,0:T(8,128)S(1)} %add.3.own_ref), channel_id=1, source_target_pairs={{0,128},{32,160},{64,192},{96,224},{128,0},{160,32},{192,64},{224,... | collective-permute-start | bytes 245768 | tf_op jit(solution)/shard_map/over_slides/ppermute | solution.py:529
  86.6 6.2 %collective-permute-start.10 = (f32[16,1280]{1,0:T(8,128)S(1)}, f32[16,1280]{1,0:T(8,128)S(1)}, u32[]{:S(2)}, u32[]{:S(2)}) collective-permute-start(f32[16,1280]{1,0:T(8,128)S(1)} %add.3.own_ref), channel_id=1, source_target_pairs={{0,64},{32,96},{64,128},{96,160},{128,192},{160,224},{192,0},{224,... | collective-permute-start | bytes 245768 | tf_op jit(solution)/shard_map/over_slides/ppermute | solution.py:529

commit v3 on v2

--- a/solution.py
+++ b/solution.py
@@ -46,25 +46,10 @@
     return moved(left, 1) + middle + moved(right, -1)
 
 
-def ends_kernel(fine_ref, coarse_ref, first_ref, last_ref, sems):
-    wide = first_ref.shape[0] * 2 // 3
-    half = first_ref.shape[0] // 3
-    fine_end, coarse_end = fine_ref.shape[0] - wide, coarse_ref.shape[0] - half
-    copies = [
-        pltpu.make_async_copy(source, target, sems.at[at])
-        for at, (source, target) in enumerate(
-            (
-                (fine_ref.at[pl.ds(fine_end, wide)], last_ref.at[pl.ds(0, wide)]),
-                (fine_ref.at[pl.ds(0, wide)], first_ref.at[pl.ds(0, wide)]),
-                (coarse_ref.at[pl.ds(coarse_end, half)], last_ref.at[pl.ds(wide, half)]),
-                (coarse_ref.at[pl.ds(0, half)], first_ref.at[pl.ds(wide, half)]),
-            )
-        )
-    ]
-    for copy in copies:
-        copy.start()
-    for copy in copies:
-        copy.wait()
+def above_below(off_ref, on_ref):
+    odd = lax.axis_index("tile") % 2 == 1
+    off, on = off_ref[...].astype(F32), on_ref[...].astype(F32)
+    return jnp.where(odd, on, off).astype(BF16), jnp.where(odd, off, on).astype(BF16)
 
 
 def levels(ref, size, axis=0):
@@ -143,8 +128,8 @@
     rows_fine,
     rows_coarse,
     part_ref,
-    above_ref,
-    below_ref,
+    off_ref,
+    on_ref,
     fk_ref,
     ck_ref,
     conv_ref,
@@ -153,6 +138,7 @@
     fine_size = part_ref.shape[0] * 4 // 5
     fpart_ref, cpart_ref = levels(part_ref, fine_size)
     fconv_ref, cconv_ref = levels(conv_ref, fine_size)
+    above, below = above_below(off_ref, on_ref)
     start = 0
     found = []
     for part_ref, k_ref, out_ref, rows in (
@@ -165,11 +151,11 @@
         second = jnp.zeros((1, channels), F32)
         for row in range(rows):
             value = part_ref[row * cols : (row + 1) * cols, :]
-            for edge, halo_ref, a in ((0, above_ref, 0), (rows - 1, below_ref, 2)):
+            for edge, halo, a in ((0, above, 0), (rows - 1, below, 2)):
                 if row == edge:
                     value = value + joined(
                         jnp.dot(
-                            halo_ref[start : start + cols, :],
+                            halo[start : start + cols, :],
                             taps_of(k_ref, a),
                             preferred_element_type=F32,
                         ),
@@ -236,9 +222,9 @@
     twice = jnp.concatenate([weights.astype(F32)] * 2, axis=0).astype(BF16)
     rows_sum = [jnp.zeros((1, channels), F32) for _ in range(4)]
     class_sum = jnp.zeros((classes, channels), F32)
-    loss_sum = jnp.zeros((1, cols), F32)
-    tissue_sum = jnp.zeros((1, cols), F32)
-    class_id = lax.broadcasted_iota(jnp.int32, (classes, cols), 0)
+    loss_sum = jnp.zeros((1, 2 * cols), F32)
+    tissue_sum = jnp.zeros((1, 2 * cols), F32)
+    class_id = lax.broadcasted_iota(jnp.int32, (classes, 2 * cols), 0)
     for pair in range(rows_fine // 2):
         cnormed = (cconv_ref[pair * half : (pair + 1) * half, :] - cmean) * cscale
         cpre = cnormed * cgain + coffset
@@ -246,38 +232,38 @@
         wide_ref[pl.ds(0, half, stride=2), :] = cact
         wide_ref[pl.ds(1, half, stride=2), :] = cact
         up = wide_ref[...]
-        both = None
-        for row in (2 * pair, 2 * pair + 1):
-            here = slice(row * cols, (row + 1) * cols)
-            normed = (fconv_ref[here, :] - fmean) * fscale
-            pre = normed * fgain + foffset
-            merged = (jnp.maximum(pre, 0.0) + up).astype(BF16)
-            logits = (
-                lax.dot_general(
-                    weights, merged, (((1,), (1,)), ((), ())), preferred_element_type=F32
-                )
-                + bias
-            )
-            top = jnp.max(logits, axis=0, keepdims=True)
-            lse = top + jnp.log(jnp.sum(jnp.exp(logits - top), axis=0, keepdims=True))
-            label = labels_ref[row : row + 1, :]
-            tissue = (label >= 0).astype(F32)
-            onehot = (label == class_id).astype(F32)
-            loss_sum = loss_sum + (lse - jnp.sum(onehot * logits, axis=0, keepdims=True)) * tissue
-            tissue_sum = tissue_sum + tissue
-            dlogits = (jnp.exp(logits - lse) - onehot) * tissue
-            high = dlogits.astype(BF16).astype(F32)
-            parts = jnp.concatenate([high, dlogits - high], axis=0).astype(BF16)
-            class_part = jnp.dot(parts, merged, preferred_element_type=F32)
-            class_sum = class_sum + (class_part[:classes] + class_part[classes:])
-            dmerged = lax.dot_general(
-                parts, twice, (((0,), (0,)), ((), ())), preferred_element_type=F32
-            )
-            dpre = jnp.where(pre > 0, dmerged, 0.0)
-            fdpre_ref[here, :] = dpre
-            rows_sum[0] = rows_sum[0] + jnp.sum(dpre * normed, axis=0, keepdims=True)
-            rows_sum[1] = rows_sum[1] + jnp.sum(dpre, axis=0, keepdims=True)
-            both = dmerged if both is None else both + dmerged
+        up = jnp.concatenate([up, up], axis=0)
+        here = slice(2 * pair * cols, 2 * (pair + 1) * cols)
+        normed = (fconv_ref[here, :] - fmean) * fscale
+        pre = normed * fgain + foffset
+        merged = (jnp.maximum(pre, 0.0) + up).astype(BF16)
+        logits = (
+            lax.dot_general(weights, merged, (((1,), (1,)), ((), ())), preferred_element_type=F32)
+            + bias
+        )
+        top = jnp.max(logits, axis=0, keepdims=True)
+        lse = top + jnp.log(jnp.sum(jnp.exp(logits - top), axis=0, keepdims=True))
+        label = jnp.concatenate(
+            [labels_ref[2 * pair : 2 * pair + 1, :], labels_ref[2 * pair + 1 : 2 * pair + 2, :]],
+            axis=1,
+        )
+        tissue = (label >= 0).astype(F32)
+        onehot = (label == class_id).astype(F32)
+        loss_sum = loss_sum + (lse - jnp.sum(onehot * logits, axis=0, keepdims=True)) * tissue
+        tissue_sum = tissue_sum + tissue
+        dlogits = (jnp.exp(logits - lse) - onehot) * tissue
+        high = dlogits.astype(BF16).astype(F32)
+        parts = jnp.concatenate([high, dlogits - high], axis=0).astype(BF16)
+        class_part = jnp.dot(parts, merged, preferred_element_type=F32)
+        class_sum = class_sum + (class_part[:classes] + class_part[classes:])
+        dmerged = lax.dot_general(
+            parts, twice, (((0,), (0,)), ((), ())), preferred_element_type=F32
+        )
+        dpre = jnp.where(pre > 0, dmerged, 0.0)
+        fdpre_ref[here, :] = dpre
+        rows_sum[0] = rows_sum[0] + jnp.sum(dpre * normed, axis=0, keepdims=True)
+        rows_sum[1] = rows_sum[1] + jnp.sum(dpre, axis=0, keepdims=True)
+        both = dmerged[:cols] + dmerged[cols:]
         sum_ref[...] = both
         dact = sum_ref[pl.ds(0, half, stride=2), :] + sum_ref[pl.ds(1, half, stride=2), :]
         dpre = jnp.where(cpre > 0, dact, 0.0)
@@ -303,8 +289,8 @@
     back_ref,
     vectors_ref,
     all_turn_ref,
-    above_ref,
-    below_ref,
+    off_ref,
+    on_ref,
     keep_ref,
     send_ref,
     head_ref,
@@ -322,8 +308,8 @@
     back = over_tiles(back_ref, 16)
     head_ref[...] = back
     kept = keep_ref.shape[0] // 16
-    order = channel_order(above_ref.shape[1])
-    above, below = turn(order, above_ref[...]), turn(order, below_ref[...])
+    order = channel_order(off_ref.shape[1])
+    above, below = [turn(order, rows) for rows in above_below(off_ref, on_ref)]
     start = 0
     for level, (conv_ref, dpre_ref, turn_ref, d_ref, rows) in enumerate(
         (
@@ -415,6 +401,10 @@
             )
 
 
+def swaps(firsts):
+    return [pair for i in firsts for pair in ((i, i + 1), (i + 1, i))]
+
+
 def core_pairs():
     return [(i, i ^ 1) for i in range(32)]
 
@@ -459,15 +449,18 @@
     vectors = [vector[None, :] for vector in vectors]
 
     with jax.named_scope("halo"):
-        ends = shape(width + width // 2, in_channels, dtype=BF16)
-        up, down = call(
-            ends_kernel,
-            (ends, ends),
-            (pltpu.SemaphoreType.DMA((4,)),),
-            in_specs=[pl.BlockSpec(memory_space=pltpu.HBM)] * 2,
-        )(fine, coarse)
-        above = lax.ppermute(down, "tile", [(i, i + 1) for i in range(tiles - 1)])
-        below = lax.ppermute(up, "tile", [(i + 1, i) for i in range(tiles - 1)])
+        odd = (lax.axis_index("tile") & 1).astype(jnp.uint32)
+
+        def edge_rows(last):
+            parts = []
+            for rows, size in ((fine, width), (coarse, width // 2)):
+                start = last * jnp.uint32(rows.shape[0] - size)
+                parts.append(lax.dynamic_slice(rows, (start, jnp.uint32(0)), (size, in_channels)))
+            return jnp.concatenate(parts)
+
+        off, on = edge_rows(odd), edge_rows(1 - odd)
+        off = lax.ppermute(off, "tile", swaps(range(1, tiles - 1, 2)))
+        on = lax.ppermute(on, "tile", swaps(range(0, tiles, 2)))
     with jax.named_scope("forward"):
         whole = pl.BlockSpec(memory_space=pltpu.VMEM)
         part, turned, vectors = call(
@@ -483,7 +476,7 @@
             functools.partial(edges_kernel, height, height // 2),
             (shape(pixels, channels), shape(8 * tiles, channels)),
             input_output_aliases={0: 0},
-        )(part, above, below, fk, ck)
+        )(part, off, on, fk, ck)
     with jax.named_scope("forward_sums"):
         stats = lax.all_to_all(stats, "tile", 0, 0, tiled=True)
     with jax.named_scope("loss_and_head"):
@@ -508,7 +501,7 @@
                 pltpu.VMEM((coarse_size, 3 * channels), BF16),
                 pltpu.VMEM((in_channels, wide), F32),
             ),
-        )(conv, dpre, stats, head, vectors, turned, above, below)
+        )(conv, dpre, stats, head, vectors, turned, off, on)
     with jax.named_scope("over_tiles"):
         sent = lax.ppermute(send, "tile", core_pairs())
         size = in_channels // 4

time: 94.1 us -> 88.9 us (0.945)
  starting transfers between devices: 26.9 us -> 23.4 us
  Pallas kernels: 11 us -> 9.68 us
  local copies, waits for them, and re-layouts: 2.23 us -> 3.25 us
    dynamic_slice x0 -> x2, local copies, waits for them, and re-layouts: none -> 1.99 us  [edge_rows(): lax.dynamic_slice(rows, (start, jnp.uint32(0)), (size, in_channels))]
    ppermute x1, starting transfers between devices: 7.28 us -> 5.47 us  [per_device(): own = own + lax.ppermute(own, 'slide', [(i, i ^ 1) for i in range(slides)])]
    ppermute x2, starting transfers between devices: 5.56 us -> 4.03 us  [the longest x1 2.11 us: per_device(): on = lax.ppermute(on, 'tile', swaps(range(0, tiles, 2)))]
    unnamed x22, local copies, waits for them, and re-layouts: 2.23 us -> 1.27 us
  transfers between devices with their start and end apart: 13 -> 13, of which waited for: 10 -> 9; matrix products, arithmetic and copies ran while one was open for 0% -> 0% of each run, Pallas kernels for 3% -> 3%
where the time goes in v3:
time: 88.9 us; the launch traced here: 88.6 us
  blocking collectives  30.7 us (35%)
  starting transfers between devices  23.4 us (26%)
  waiting for transfers between devices  20.7 us (23%)
  Pallas kernels  9.68 us (11%)
  local copies, waits for them, and re-layouts  3.25 us (4%)
    all_to_all x1, blocking collectives, per_device(): stats = lax.all_to_all(stats, 'tile', 0, 0, tiled=True)  16.5 us
    all_to_all x1, blocking collectives, per_device(): head = lax.all_to_all(head, 'tile', 0, 0, tiled=True)  14.2 us
    ppermute x3, waiting for transfers between devices, per_device(): lax.ppermute(parts[step], 'tile', x_pairs(step))  6.83 us
    ppermute x1, starting transfers between devices, per_device(): own = own + lax.ppermute(own, 'slide', [(i, i ^ 1) for i in range(slides)])  5.47 us
    ppermute x3, waiting for transfers between devices, per_device(): lax.ppermute(own, 'slide', [(i, (i + 2 * step) % slides) for i in range(s...  5.22 us
    ppermute x3, starting transfers between devices, per_device(): lax.ppermute(own, 'slide', [(i, (i + 2 * step) % slides) for i in range(s...  4.69 us
    ppermute x3, starting transfers between devices, per_device(): lax.ppermute(parts[step], 'tile', z_pairs(step))  4.59 us
    ppermute x3, starting transfers between devices, per_device(): lax.ppermute(parts[step], 'tile', x_pairs(step))  4.24 us
  transfers between devices with their start and end apart: 13, of which 9 were waited for; matrix products, arithmetic and copies ran while one was open for 0% of the time, Pallas kernels for 3%

profile of v3, /device:TPU:32, one launch (start us, length us, event | category | flops | bytes accessed | tf_op | source)
XLA Modules:
  0.0 88.6 jit_solution(16134609989627640691)
XLA Ops:
  0.7 1.0 %constant_dynamic-slice_fusion = (bf16[128,256]{1,0:T(8,128)(2,1)S(1)}, bf16[128,256]{1,0:T(8,128)(2,1)S(1)}) fusion(bf16[512,256]{1,0:T(8,128)(2,1)} %bitcast.26, u32[]{:T(128)S(6)} %mul.15, u32[]{:T(128)S(6)} %mul.13), kind=kLoop, calls=%fused_computation.2 | loop fusion | bytes 262152 | tf_op jit(solution)/shard_map/halo/dynamic_slice | solution.py:458
  1.7 1.0 %constant_dynamic-slice_fusion.1 = (bf16[256,256]{1,0:T(8,128)(2,1)S(1)}, bf16[256,256]{1,0:T(8,128)(2,1)S(1)}) fusion(bf16[2048,256]{1,0:T(8,128)(2,1)} %bitcast.21, u32[]{:T(128)S(6)} %mul.14, u32[]{:T(128)S(6)} %mul.12), kind=kLoop, calls=%fused_computation.3 | loop fusion | bytes 524296 | tf_op jit(solution)/shard_map/halo/dynamic_slice | solution.py:458
  2.7 1.9 %collective-permute-start = (bf16[384,256]{1,0:T(8,128)(2,1)S(1)}, bf16[384,256]{1,0:T(8,128)(2,1)S(1)}, u32[]{:S(2)}, u32[]{:S(2)}) collective-permute-start(bf16[384,256]{1,0:T(8,128)(2,1)S(1)} %pad_maximum_fusion), channel_id=1, source_target_pairs={{1,2},{2,1},{3,4},{4,3},{5,6},{6,5},{7,8},{8,7},{9,10},{10,9},{11,... | collective-permute-start | bytes 589832 | tf_op jit(solution)/shard_map/halo/ppermute | solution.py:462
  4.7 2.1 %collective-permute-start.1 = (bf16[384,256]{1,0:T(8,128)(2,1)S(1)}, bf16[384,256]{1,0:T(8,128)(2,1)S(1)}, u32[]{:S(2)}, u32[]{:S(2)}) collective-permute-start(bf16[384,256]{1,0:T(8,128)(2,1)S(1)} %pad_maximum_fusion.1), channel_id=1, source_target_pairs={{0,1},{1,0},{2,3},{3,2},{4,5},{5,4},{6,7},{7,6},{8,9},{9,8},{10,11... | collective-permute-start | bytes 589832 | tf_op jit(solution)/shard_map/halo/ppermute | solution.py:463
  6.9 1.2 %copy-done.2 = bf16[1,8,256,256]{3,2,1,0:T(8,128)(2,1)S(1)} copy-done((bf16[1,8,256,256]{3,2,1,0:T(8,128)(2,1)S(1)}, bf16[1,8,256,256]{3,2,1,0:T(8,128)(2,1)}, u32[]{:S(2)}) %copy-start.2) | copy-done | bytes 1048600
  8.1 3.0 %forward.2 = (f32[2560,128]{1,0:T(8,128)S(1)}, bf16[256,2560]{1,0:T(8,128)(2,1)S(1)}, f32[16,128]{1,0:T(8,128)S(1)}) custom-call(bf16[2048,256]{1,0:T(8,128)(2,1)S(1)} %bitcast.22, bf16[512,256]{1,0:T(8,128)(2,1)S(1)} %bitcast.27, bf16[9,256,128]{2,1,0:T(8,128)(2,1)S(1)} %bitcast.17, bf16[9,256,128]{2,1,0:T(8,128)(2,1)S(1)} %bitcast.19, ...), custom_call_target="tpu_custom_call" | custom-call | tf_op jit(solution)/shard_map/forward/pallas_call | solution.py:466
  11.9 16.5 %all_to_all.22 = f32[32,8,128]{2,1,0:T(8,128)S(1)} all-to-all(f32[32,8,128]{2,1,0:T(8,128)S(1)} %bitcast.29), channel_id=1, replica_groups=mesh['slide'=8,'tile'=32] {'tile'}, dimensions={0} | all-to-all | bytes 262144 | tf_op jit(solution)/shard_map/forward_sums/all_to_all | solution.py:481
  28.4 1.6 %loss_and_head.1 = (f32[2560,128]{1,0:T(8,128)S(1)}, f32[512,128]{1,0:T(8,128)S(1)}) custom-call(f32[2560,128]{1,0:T(8,128)S(1)} %get-tuple-element.25.conv_ref.all_conv_ref, f32[256,128]{1,0:T(8,128)S(1)} %bitcast.23, f32[16,128]{1,0:T(8,128)S(1)} %get-tuple-element.27.vectors_ref, bf16[8,128]{1,0:T(8,128)(2,1)S(1)} %copy-done.5, s32[8,256]{1,0:T(8,128)S(1)} %bitcast.30), custom_call_target="tpu_custom_call" | custom-call | tf_op jit(solution)/shard_map/loss_and_head/pallas_call | solution.py:483
  30.0 14.2 %all_to_all.23 = f32[32,16,128]{2,1,0:T(8,128)S(1)} all-to-all(f32[32,16,128]{2,1,0:T(8,128)S(1)} %bitcast.28), channel_id=1, replica_groups=mesh['slide'=8,'tile'=32] {'tile'}, dimensions={0} | all-to-all | bytes 524288 | tf_op jit(solution)/shard_map/backward_sums/all_to_all | solution.py:489
  44.2 3.3 %weight_grads.1 = (f32[256,1152]{1,0:T(8,128)S(1)}, bf16[256,1152]{1,0:T(8,128)(2,1)S(1)}, f32[16,128]{1,0:T(8,128)S(1)}) custom-call(f32[2560,128]{1,0:T(8,128)S(1)} %get-tuple-element.25.conv_ref.all_conv_ref, f32[2560,128]{1,0:T(8,128)S(1)} %get-tuple-element.28.all_dpre_ref, f32[256,128]{1,0:T(8,128)S(1)} %bitcast.24, f32[512,128]{1,0:T(8,128)S(1)} %bitcast.25, ...), custom_call_target="tpu_custom_call" | custom-call | tf_op jit(solution)/shard_map/weight_grads/pallas_call | solution.py:492
  47.9 1.7 %collective-permute-done.2.sent_ref = bf16[256,1152]{1,0:T(8,128)(2,1)S(1)} collective-permute-done((bf16[256,1152]{1,0:T(8,128)(2,1)S(1)}, bf16[256,1152]{1,0:T(8,128)(2,1)S(1)}, u32[]{:S(2)}, u32[]{:S(2)}) %collective-permute-start.2) | collective-permute-done | bytes 589856 | tf_op jit(solution)/shard_map/over_tiles/ppermute | solution.py:506
  50.4 2.0 %collective-permute-start.4 = (bf16[64,1152]{1,0:T(8,128)(2,1)S(1)}, bf16[64,1152]{1,0:T(8,128)(2,1)S(1)}, u32[]{:S(2)}, u32[]{:S(2)}) collective-permute-start(bf16[64,1152]{1,0:T(8,128)(2,1)S(1)} %get-tuple-element.35), channel_id=1, source_target_pairs={{0,16},{1,17},{2,18},{3,19},{4,20},{5,21},{6,22},{7,23},{8,24},{9,... | collective-permute-start | bytes 442376 | tf_op jit(solution)/shard_map/over_tiles/ppermute | solution.py:511
  52.4 1.6 %collective-permute-start.5 = (bf16[64,1152]{1,0:T(8,128)(2,1)S(1)}, bf16[64,1152]{1,0:T(8,128)(2,1)S(1)}, u32[]{:S(2)}, u32[]{:S(2)}) collective-permute-start(bf16[64,1152]{1,0:T(8,128)(2,1)S(1)} %get-tuple-element.36), channel_id=1, source_target_pairs={{0,24},{1,25},{2,26},{3,27},{4,28},{5,29},{6,30},{7,31},{8,0},{9,1... | collective-permute-start | bytes 442376 | tf_op jit(solution)/shard_map/over_tiles/ppermute | solution.py:511
  54.0 6.2 %collective-permute-done.3.one_ref = bf16[64,1152]{1,0:T(8,128)(2,1)S(1)} collective-permute-done((bf16[64,1152]{1,0:T(8,128)(2,1)S(1)}, bf16[64,1152]{1,0:T(8,128)(2,1)S(1)}, u32[]{:S(2)}, u32[]{:S(2)}) %collective-permute-start.3) | collective-permute-done | bytes 147488 | tf_op jit(solution)/shard_map/over_tiles/ppermute | solution.py:511
  60.9 1.1 %collective-permute-start.6 = (bf16[16,1152]{1,0:T(8,128)(2,1)S(1)}, bf16[16,1152]{1,0:T(8,128)(2,1)S(1)}, u32[]{:S(2)}, u32[]{:S(2)}) collective-permute-start(bf16[16,1152]{1,0:T(8,128)(2,1)S(1)} %get-tuple-element.38), channel_id=1, source_target_pairs={{0,2},{1,3},{2,4},{3,5},{4,6},{5,7},{6,0},{7,1},{8,10},{9,11},{10,... | collective-permute-start | bytes 110600 | tf_op jit(solution)/shard_map/over_tiles/ppermute | solution.py:516
  62.0 3.5 %collective-permute-start.7 = (bf16[16,1152]{1,0:T(8,128)(2,1)S(1)}, bf16[16,1152]{1,0:T(8,128)(2,1)S(1)}, u32[]{:S(2)}, u32[]{:S(2)}) collective-permute-start(bf16[16,1152]{1,0:T(8,128)(2,1)S(1)} %get-tuple-element.39), channel_id=1, source_target_pairs={{0,4},{1,5},{2,6},{3,7},{4,0},{5,1},{6,2},{7,3},{8,12},{9,13},{10,... | collective-permute-start | bytes 110600 | tf_op jit(solution)/shard_map/over_tiles/ppermute | solution.py:516
  65.5 2.4 %collective-permute-done.7.two_ref = bf16[16,1152]{1,0:T(8,128)(2,1)S(1)} collective-permute-done((bf16[16,1152]{1,0:T(8,128)(2,1)S(1)}, bf16[16,1152]{1,0:T(8,128)(2,1)S(1)}, u32[]{:S(2)}, u32[]{:S(2)}) %collective-permute-start.7) | collective-permute-done | bytes 36896 | tf_op jit(solution)/shard_map/over_tiles/ppermute | solution.py:516
  67.9 1.5 %collective-permute-done.8.three_ref = bf16[16,1152]{1,0:T(8,128)(2,1)S(1)} collective-permute-done((bf16[16,1152]{1,0:T(8,128)(2,1)S(1)}, bf16[16,1152]{1,0:T(8,128)(2,1)S(1)}, u32[]{:S(2)}, u32[]{:S(2)}) %collective-permute-start.8) | collective-permute-done | bytes 36896 | tf_op jit(solution)/shard_map/over_tiles/ppermute | solution.py:516
  69.5 5.5 %collective-permute-start.9 = (f32[16,1280]{1,0:T(8,128)S(1)}, f32[16,1280]{1,0:T(8,128)S(1)}, u32[]{:S(2)}, u32[]{:S(2)}) collective-permute-start(f32[16,1280]{1,0:T(8,128)S(1)} %over_tiles.5), channel_id=1, source_target_pairs={{0,32},{32,0},{64,96},{96,64},{128,160},{160,128},{192,224},{224,1... | collective-permute-start | bytes 245768 | tf_op jit(solution)/shard_map/over_slides/ppermute | solution.py:520
  75.0 3.0 %collective-permute-done.9 = f32[16,1280]{1,0:T(8,128)S(1)} collective-permute-done((f32[16,1280]{1,0:T(8,128)S(1)}, f32[16,1280]{1,0:T(8,128)S(1)}, u32[]{:S(2)}, u32[]{:S(2)}) %collective-permute-start.9) | collective-permute-done | bytes 81952 | tf_op jit(solution)/shard_map/over_slides/ppermute | solution.py:520
  77.9 3.1 %collective-permute-start.12 = (f32[16,1280]{1,0:T(8,128)S(1)}, f32[16,1280]{1,0:T(8,128)S(1)}, u32[]{:S(2)}, u32[]{:S(2)}) collective-permute-start(f32[16,1280]{1,0:T(8,128)S(1)} %add.3.own_ref), channel_id=1, source_target_pairs={{0,192},{32,224},{64,0},{96,32},{128,64},{160,96},{192,128},{224,1... | collective-permute-start | bytes 245768 | tf_op jit(solution)/shard_map/over_slides/ppermute | solution.py:522
  81.7 1.0 %collective-permute-start.10 = (f32[16,1280]{1,0:T(8,128)S(1)}, f32[16,1280]{1,0:T(8,128)S(1)}, u32[]{:S(2)}, u32[]{:S(2)}) collective-permute-start(f32[16,1280]{1,0:T(8,128)S(1)} %add.3.own_ref), channel_id=1, source_target_pairs={{0,64},{32,96},{64,128},{96,160},{128,192},{160,224},{192,0},{224,... | collective-permute-start | bytes 245768 | tf_op jit(solution)/shard_map/over_slides/ppermute | solution.py:522
  83.1 3.9 %collective-permute-done.11.two_ref = f32[16,1280]{1,0:T(8,128)S(1)} collective-permute-done((f32[16,1280]{1,0:T(8,128)S(1)}, f32[16,1280]{1,0:T(8,128)S(1)}, u32[]{:S(2)}, u32[]{:S(2)}) %collective-permute-start.11) | collective-permute-done | bytes 81952 | tf_op jit(solution)/shard_map/over_slides/ppermute | solution.py:522
  87.0 0.8 collective-permute-done.10.one_ref
  (39 shorter events, 4.5 us)
Async XLA Ops:
  0.6 6.2 %copy-start.3 = (bf16[1,4,128,256]{3,2,1,0:T(8,128)(2,1)S(1)}, bf16[1,4,128,256]{3,2,1,0:T(8,128)(2,1)}, u32[]{:S(2)}) copy-start(bf16[1,4,128,256]{3,2,1,0:T(8,128)(2,1)} %param.12) | copy-start | bytes 786436
  0.6 6.2 %copy-start.10 = (f32[8]{0:T(128)S(1)}, f32[8]{0:T(128)}, u32[]{:S(2)}) copy-start(f32[8]{0:T(128)} %bias_ref.1) | copy-start | bytes 100
  0.7 6.2 %copy-start.9 = (f32[128]{0:T(128)S(1)}, f32[128]{0:T(128)}, u32[]{:S(2)}) copy-start(f32[128]{0:T(128)} %param.18) | copy-start | bytes 1540
  0.7 6.1 %copy-start.8 = (f32[128]{0:T(128)S(1)}, f32[128]{0:T(128)}, u32[]{:S(2)}) copy-start(f32[128]{0:T(128)} %param.17) | copy-start | bytes 1540
  0.7 6.1 %copy-start.7 = (f32[128]{0:T(128)S(1)}, f32[128]{0:T(128)}, u32[]{:S(2)}) copy-start(f32[128]{0:T(128)} %param.16) | copy-start | bytes 1540
  0.7 6.1 %copy-start.6 = (f32[128]{0:T(128)S(1)}, f32[128]{0:T(128)}, u32[]{:S(2)}) copy-start(f32[128]{0:T(128)} %param.15) | copy-start | bytes 1540
  0.7 6.1 %copy-start.1 = (bf16[256,9,128]{2,0,1:T(8,128)(2,1)S(1)}, bf16[256,9,128]{2,0,1:T(8,128)(2,1)}, u32[]{:S(2)}) copy-start(bf16[256,9,128]{2,0,1:T(8,128)(2,1)} %param.14) | copy-start | bytes 1769476
  0.7 6.1 %copy-start = (bf16[256,9,128]{2,0,1:T(8,128)(2,1)S(1)}, bf16[256,9,128]{2,0,1:T(8,128)(2,1)}, u32[]{:S(2)}) copy-start(bf16[256,9,128]{2,0,1:T(8,128)(2,1)} %param.13) | copy-start | bytes 1769476
  2.7 8.3 %collective-permute-start = (bf16[384,256]{1,0:T(8,128)(2,1)S(1)}, bf16[384,256]{1,0:T(8,128)(2,1)S(1)}, u32[]{:S(2)}, u32[]{:S(2)}) collective-permute-start(bf16[384,256]{1,0:T(8,128)(2,1)S(1)} %pad_maximum_fusion), channel_id=1, source_target_pairs={{1,2},{2,1},{3,4},{4,3},{5,6},{6,5},{7,8},{8,7},{9,10},{10,9},{11,... | collective-permute-start | bytes 589832 | tf_op jit(solution)/shard_map/halo/ppermute | solution.py:462
  4.7 6.4 %collective-permute-start.1 = (bf16[384,256]{1,0:T(8,128)(2,1)S(1)}, bf16[384,256]{1,0:T(8,128)(2,1)S(1)}, u32[]{:S(2)}, u32[]{:S(2)}) collective-permute-start(bf16[384,256]{1,0:T(8,128)(2,1)S(1)} %pad_maximum_fusion.1), channel_id=1, source_target_pairs={{0,1},{1,0},{2,3},{3,2},{4,5},{5,4},{6,7},{7,6},{8,9},{9,8},{10,11... | collective-permute-start | bytes 589832 | tf_op jit(solution)/shard_map/halo/ppermute | solution.py:463
  6.9 1.2 %copy-start.2 = (bf16[1,8,256,256]{3,2,1,0:T(8,128)(2,1)S(1)}, bf16[1,8,256,256]{3,2,1,0:T(8,128)(2,1)}, u32[]{:S(2)}) copy-start(bf16[1,8,256,256]{3,2,1,0:T(8,128)(2,1)} %param.11) | copy-start | bytes 3145732
  11.1 17.3 %copy-start.4 = (s32[1,8,256]{2,1,0:T(8,128)S(1)}, s32[1,8,256]{2,1,0:T(8,128)}, u32[]{:S(2)}) copy-start(s32[1,8,256]{2,1,0:T(8,128)} %param.21) | copy-start | bytes 24580
  11.1 17.3 %copy-start.5 = (bf16[8,128]{1,0:T(8,128)(2,1)S(1)}, bf16[8,128]{1,0:T(8,128)(2,1)}, u32[]{:S(2)}) copy-start(bf16[8,128]{1,0:T(8,128)(2,1)} %class_ref.1) | copy-start | bytes 6148
  47.5 2.1 %collective-permute-start.2 = (bf16[256,1152]{1,0:T(8,128)(2,1)S(1)}, bf16[256,1152]{1,0:T(8,128)(2,1)S(1)}, u32[]{:S(2)}, u32[]{:S(2)}) collective-permute-start(bf16[256,1152]{1,0:T(8,128)(2,1)S(1)} %get-tuple-element.32), channel_id=1, source_target_pairs={{0,1},{1,0},{2,3},{3,2},{4,5},{5,4},{6,7},{7,6},{8,9},{9,8},{10,11... | collective-permute-start | bytes 1769480 | tf_op jit(solution)/shard_map/over_tiles/ppermute | solution.py:506
  49.8 10.5 %collective-permute-start.3 = (bf16[64,1152]{1,0:T(8,128)(2,1)S(1)}, bf16[64,1152]{1,0:T(8,128)(2,1)S(1)}, u32[]{:S(2)}, u32[]{:S(2)}) collective-permute-start(bf16[64,1152]{1,0:T(8,128)(2,1)S(1)} %get-tuple-element.34), channel_id=1, source_target_pairs={{0,8},{1,9},{2,10},{3,11},{4,12},{5,13},{6,14},{7,15},{8,16},{9,17... | collective-permute-start | bytes 442376 | tf_op jit(solution)/shard_map/over_tiles/ppermute | solution.py:511
  50.4 9.9 %collective-permute-start.4 = (bf16[64,1152]{1,0:T(8,128)(2,1)S(1)}, bf16[64,1152]{1,0:T(8,128)(2,1)S(1)}, u32[]{:S(2)}, u32[]{:S(2)}) collective-permute-start(bf16[64,1152]{1,0:T(8,128)(2,1)S(1)} %get-tuple-element.35), channel_id=1, source_target_pairs={{0,16},{1,17},{2,18},{3,19},{4,20},{5,21},{6,22},{7,23},{8,24},{9,... | collective-permute-start | bytes 442376 | tf_op jit(solution)/shard_map/over_tiles/ppermute | solution.py:511
  52.4 8.5 %collective-permute-start.5 = (bf16[64,1152]{1,0:T(8,128)(2,1)S(1)}, bf16[64,1152]{1,0:T(8,128)(2,1)S(1)}, u32[]{:S(2)}, u32[]{:S(2)}) collective-permute-start(bf16[64,1152]{1,0:T(8,128)(2,1)S(1)} %get-tuple-element.36), channel_id=1, source_target_pairs={{0,24},{1,25},{2,26},{3,27},{4,28},{5,29},{6,30},{7,31},{8,0},{9,1... | collective-permute-start | bytes 442376 | tf_op jit(solution)/shard_map/over_tiles/ppermute | solution.py:511
  60.9 4.6 %collective-permute-start.6 = (bf16[16,1152]{1,0:T(8,128)(2,1)S(1)}, bf16[16,1152]{1,0:T(8,128)(2,1)S(1)}, u32[]{:S(2)}, u32[]{:S(2)}) collective-permute-start(bf16[16,1152]{1,0:T(8,128)(2,1)S(1)} %get-tuple-element.38), channel_id=1, source_target_pairs={{0,2},{1,3},{2,4},{3,5},{4,6},{5,7},{6,0},{7,1},{8,10},{9,11},{10,... | collective-permute-start | bytes 110600 | tf_op jit(solution)/shard_map/over_tiles/ppermute | solution.py:516
  62.0 5.9 %collective-permute-start.7 = (bf16[16,1152]{1,0:T(8,128)(2,1)S(1)}, bf16[16,1152]{1,0:T(8,128)(2,1)S(1)}, u32[]{:S(2)}, u32[]{:S(2)}) collective-permute-start(bf16[16,1152]{1,0:T(8,128)(2,1)S(1)} %get-tuple-element.39), channel_id=1, source_target_pairs={{0,4},{1,5},{2,6},{3,7},{4,0},{5,1},{6,2},{7,3},{8,12},{9,13},{10,... | collective-permute-start | bytes 110600 | tf_op jit(solution)/shard_map/over_tiles/ppermute | solution.py:516
  65.5 4.0 %collective-permute-start.8 = (bf16[16,1152]{1,0:T(8,128)(2,1)S(1)}, bf16[16,1152]{1,0:T(8,128)(2,1)S(1)}, u32[]{:S(2)}, u32[]{:S(2)}) collective-permute-start(bf16[16,1152]{1,0:T(8,128)(2,1)S(1)} %get-tuple-element.40), channel_id=1, source_target_pairs={{0,6},{1,7},{2,0},{3,1},{4,2},{5,3},{6,4},{7,5},{8,14},{9,15},{10,... | collective-permute-start | bytes 110600 | tf_op jit(solution)/shard_map/over_tiles/ppermute | solution.py:516
  69.5 8.4 %collective-permute-start.9 = (f32[16,1280]{1,0:T(8,128)S(1)}, f32[16,1280]{1,0:T(8,128)S(1)}, u32[]{:S(2)}, u32[]{:S(2)}) collective-permute-start(f32[16,1280]{1,0:T(8,128)S(1)} %over_tiles.5), channel_id=1, source_target_pairs={{0,32},{32,0},{64,96},{96,64},{128,160},{160,128},{192,224},{224,1... | collective-permute-start | bytes 245768 | tf_op jit(solution)/shard_map/over_slides/ppermute | solution.py:520
  77.9 5.1 %collective-permute-start.12 = (f32[16,1280]{1,0:T(8,128)S(1)}, f32[16,1280]{1,0:T(8,128)S(1)}, u32[]{:S(2)}, u32[]{:S(2)}) collective-permute-start(f32[16,1280]{1,0:T(8,128)S(1)} %add.3.own_ref), channel_id=1, source_target_pairs={{0,192},{32,224},{64,0},{96,32},{128,64},{160,96},{192,128},{224,1... | collective-permute-start | bytes 245768 | tf_op jit(solution)/shard_map/over_slides/ppermute | solution.py:522
  81.0 6.0 %collective-permute-start.11 = (f32[16,1280]{1,0:T(8,128)S(1)}, f32[16,1280]{1,0:T(8,128)S(1)}, u32[]{:S(2)}, u32[]{:S(2)}) collective-permute-start(f32[16,1280]{1,0:T(8,128)S(1)} %add.3.own_ref), channel_id=1, source_target_pairs={{0,128},{32,160},{64,192},{96,224},{128,0},{160,32},{192,64},{224,... | collective-permute-start | bytes 245768 | tf_op jit(solution)/shard_map/over_slides/ppermute | solution.py:522
  81.7 6.2 %collective-permute-start.10 = (f32[16,1280]{1,0:T(8,128)S(1)}, f32[16,1280]{1,0:T(8,128)S(1)}, u32[]{:S(2)}, u32[]{:S(2)}) collective-permute-start(f32[16,1280]{1,0:T(8,128)S(1)} %add.3.own_ref), channel_id=1, source_target_pairs={{0,64},{32,96},{64,128},{96,160},{128,192},{160,224},{192,0},{224,... | collective-permute-start | bytes 245768 | tf_op jit(solution)/shard_map/over_slides/ppermute | solution.py:522

commit v4 on v3

--- a/solution.py
+++ b/solution.py
@@ -166,9 +166,9 @@
             second = second + jnp.sum(value * value, axis=0, keepdims=True)
         found += [first, second]
         start += cols
-    found = jnp.concatenate(found + [jnp.zeros_like(found[0])] * 4, axis=0)
-    for tile in range(stats_ref.shape[0] // 8):
-        stats_ref[8 * tile : 8 * tile + 8, :] = found
+    found = jnp.concatenate(found + found, axis=0)
+    for pair in range(stats_ref.shape[0] // 8):
+        stats_ref[8 * pair : 8 * pair + 8, :] = found
 
 
 def same_group(channels):
@@ -179,7 +179,29 @@
 
 
 def over_tiles(all_ref, count):
-    return jnp.sum(all_ref[...].reshape(-1, count, all_ref.shape[1]), axis=0)
+    return jnp.sum(all_ref[...].astype(F32).reshape(-1, count, all_ref.shape[1]), axis=0)
+
+
+def stats_sums(stats_ref, members):
+    pairs = over_tiles(stats_ref, 8)
+    return over_group(pairs[0:4, :] + pairs[4:8, :], members)
+
+
+def lane_blocks(channels):
+    per_group = channels // GROUPS
+    row = lax.broadcasted_iota(jnp.int32, (channels, channels), 0)
+    col = lax.broadcasted_iota(jnp.int32, (channels, channels), 1)
+    block_row = lax.broadcasted_iota(jnp.int32, (per_group, channels), 0)
+    block_col = lax.broadcasted_iota(jnp.int32, (per_group, channels), 1)
+    gather = (row // per_group == lax.rem(col, GROUPS)).astype(F32)
+    back = (lax.rem(row, GROUPS) == col // per_group).astype(F32)
+    return gather, back, block_col // GROUPS == block_row
+
+
+def three_parts(values):
+    high = values.astype(BF16).astype(F32)
+    middle = (values - high).astype(BF16).astype(F32)
+    return [high, middle, values - high - middle]
 
 
 def over_group(rows, members):
@@ -212,7 +234,7 @@
     cols = fconv_ref.shape[0] // rows_fine
     half = cols // 2
     classes = class_ref.shape[0]
-    sums = over_group(over_tiles(stats_ref, 8), same_group(channels))
+    sums = stats_sums(stats_ref, same_group(channels))
     fmean, fscale = norm_terms(sums, 0, numbers[0])
     cmean, cscale = norm_terms(sums, 1, numbers[1])
     weights = class_ref[...]
@@ -270,12 +292,18 @@
         cdpre_ref[pair * half : (pair + 1) * half, :] = dpre
         rows_sum[2] = rows_sum[2] + jnp.sum(dpre * cnormed, axis=0, keepdims=True)
         rows_sum[3] = rows_sum[3] + jnp.sum(dpre, axis=0, keepdims=True)
+    gains = (fgain, fgain, cgain, cgain)
+    gather, _, own_block = lane_blocks(channels)
+    spread = jnp.concatenate([row * gain for row, gain in zip(rows_sum, gains)], axis=0)
+    packed = jnp.where(own_block, over_group(spread, gather), 0.0)
+    packed = jnp.sum(packed, axis=0, keepdims=True)
     lane = lax.broadcasted_iota(jnp.int32, (1, channels), 1)
-    loss_all = jnp.sum(loss_sum, axis=1, keepdims=True)
-    tissue_all = jnp.sum(tissue_sum, axis=1, keepdims=True)
-    counts = jnp.where(lane == 0, loss_all, jnp.where(lane == 1, tissue_all, 0.0))
-    blank = jnp.zeros((11 - classes, channels), F32)
-    head = jnp.concatenate(rows_sum + [class_sum, counts, blank], axis=0)
+    scalars = jnp.zeros((1, channels), F32)
+    totals = [jnp.sum(row, axis=1, keepdims=True) for row in (loss_sum, tissue_sum)]
+    for at, part in enumerate(three_parts(totals[0]) + three_parts(totals[1])):
+        scalars = jnp.where(lane == at, part, scalars)
+    head = rows_sum + [class_sum] + three_parts(packed) + [scalars]
+    head = jnp.concatenate(head, axis=0).astype(BF16)
     for tile in range(head_ref.shape[0] // 16):
         head_ref[16 * tile : 16 * tile + 16, :] = head
 
@@ -304,9 +332,18 @@
     fturn_ref, cturn_ref = levels(all_turn_ref, fine_size, 1)
     channels = all_conv_ref.shape[1]
     members = same_group(channels)
-    sums = over_group(over_tiles(stats_ref, 8), members)
+    sums = stats_sums(stats_ref, members)
     back = over_tiles(back_ref, 16)
-    head_ref[...] = back
+    lane = lax.broadcasted_iota(jnp.int32, (1, channels), 1)
+    loss_all, tissue_all = [
+        back[15:16, at : at + 1] + back[15:16, at + 1 : at + 2] + back[15:16, at + 2 : at + 3]
+        for at in (0, 3)
+    ]
+    counts = jnp.where(lane == 0, loss_all, jnp.where(lane == 1, tissue_all, 0.0))
+    head_ref[...] = jnp.concatenate([back[0:12, :], counts, jnp.zeros((3, channels), F32)], axis=0)
+    _, spread, own_block = lane_blocks(channels)
+    packed = back[12:13, :] + back[13:14, :] + back[14:15, :]
+    back = over_group(jnp.where(own_block, packed, 0.0), spread)
     kept = keep_ref.shape[0] // 16
     order = channel_order(off_ref.shape[1])
     above, below = [turn(order, rows) for rows in above_below(off_ref, on_ref)]
@@ -321,7 +358,7 @@
         cols = size // rows
         mean, scale = norm_terms(sums, level, numbers[level])
         gain = vectors_ref[2 * level : 2 * level + 1, :]
-        means = over_group(back[2 * level : 2 * level + 2, :] * gain, members) / numbers[level]
+        means = back[2 * level : 2 * level + 2, :] / numbers[level]
         with_normed, plain = means[0:1, :], means[1:2, :]
         for row in range(rows):
             here = slice(row * cols, (row + 1) * cols)
@@ -474,7 +511,7 @@
         )(fine, coarse, fk, ck, *vectors, class_offset)
         conv, stats = call(
             functools.partial(edges_kernel, height, height // 2),
-            (shape(pixels, channels), shape(8 * tiles, channels)),
+            (shape(pixels, channels), shape(4 * tiles, channels)),
             input_output_aliases={0: 0},
         )(part, off, on, fk, ck)
     with jax.named_scope("forward_sums"):
@@ -482,7 +519,7 @@
     with jax.named_scope("loss_and_head"):
         dpre, head = call(
             functools.partial(loss_kernel, height, numbers),
-            (shape(pixels, channels), shape(16 * tiles, channels)),
+            (shape(pixels, channels), shape(16 * tiles, channels, dtype=BF16)),
             (pltpu.VMEM((width, channels), F32), pltpu.VMEM((width, channels), F32)),
         )(conv, stats, vectors, class_kernel, labels)
     with jax.named_scope("backward_sums"):

time: 88.9 us -> 85 us (0.956)
  blocking collectives: 30.7 us -> 27.5 us
    all_to_all x1, blocking collectives: 14.2 us -> 11.6 us  [per_device(): head = lax.all_to_all(head, 'tile', 0, 0, tiled=True)]
  transfers between devices with their start and end apart: 13 -> 13, of which waited for: 9 -> 9; matrix products, arithmetic and copies ran while one was open for 0% -> 0% of each run, Pallas kernels for 3% -> 4%
where the time goes in v4:
time: 85 us; the launch traced here: 84.8 us
  blocking collectives  27.5 us (32%)
  starting transfers between devices  22.9 us (27%)
  waiting for transfers between devices  20.9 us (25%)
  Pallas kernels  9.3 us (11%)
  local copies, waits for them, and re-layouts  3.25 us (4%)
  between operations  0.86 us (1%)
    all_to_all x1, blocking collectives, per_device(): stats = lax.all_to_all(stats, 'tile', 0, 0, tiled=True)  15.9 us
    all_to_all x1, blocking collectives, per_device(): head = lax.all_to_all(head, 'tile', 0, 0, tiled=True)  11.6 us
    ppermute x3, waiting for transfers between devices, per_device(): lax.ppermute(parts[step], 'tile', x_pairs(step))  7.15 us
    ppermute x1, starting transfers between devices, per_device(): own = own + lax.ppermute(own, 'slide', [(i, i ^ 1) for i in range(slides)])  5.48 us
    ppermute x3, waiting for transfers between devices, per_device(): lax.ppermute(own, 'slide', [(i, (i + 2 * step) % slides) for i in range(s...  5.22 us
    ppermute x3, starting transfers between devices, per_device(): lax.ppermute(own, 'slide', [(i, (i + 2 * step) % slides) for i in range(s...  4.7 us
    ppermute x3, starting transfers between devices, per_device(): lax.ppermute(parts[step], 'tile', z_pairs(step))  4.17 us
    ppermute x3, starting transfers between devices, per_device(): lax.ppermute(parts[step], 'tile', x_pairs(step))  4.05 us
  transfers between devices with their start and end apart: 13, of which 9 were waited for; matrix products, arithmetic and copies ran while one was open for 0% of the time, Pallas kernels for 4%

profile of v4, /device:TPU:32, one launch (start us, length us, event | category | flops | bytes accessed | tf_op | source)
XLA Modules:
  0.0 84.8 jit_solution(8890419537442725598)
XLA Ops:
  0.7 1.0 %constant_dynamic-slice_fusion = (bf16[128,256]{1,0:T(8,128)(2,1)S(1)}, bf16[128,256]{1,0:T(8,128)(2,1)S(1)}) fusion(bf16[512,256]{1,0:T(8,128)(2,1)} %bitcast.25, u32[]{:T(128)S(6)} %mul.15, u32[]{:T(128)S(6)} %mul.13), kind=kLoop, calls=%fused_computation.2 | loop fusion | bytes 262152 | tf_op jit(solution)/shard_map/halo/dynamic_slice | solution.py:495
  1.7 1.0 %constant_dynamic-slice_fusion.1 = (bf16[256,256]{1,0:T(8,128)(2,1)S(1)}, bf16[256,256]{1,0:T(8,128)(2,1)S(1)}) fusion(bf16[2048,256]{1,0:T(8,128)(2,1)} %bitcast.21, u32[]{:T(128)S(6)} %mul.14, u32[]{:T(128)S(6)} %mul.12), kind=kLoop, calls=%fused_computation.3 | loop fusion | bytes 524296 | tf_op jit(solution)/shard_map/halo/dynamic_slice | solution.py:495
  2.7 1.9 %collective-permute-start = (bf16[384,256]{1,0:T(8,128)(2,1)S(1)}, bf16[384,256]{1,0:T(8,128)(2,1)S(1)}, u32[]{:S(2)}, u32[]{:S(2)}) collective-permute-start(bf16[384,256]{1,0:T(8,128)(2,1)S(1)} %pad_maximum_fusion), channel_id=1, source_target_pairs={{1,2},{2,1},{3,4},{4,3},{5,6},{6,5},{7,8},{8,7},{9,10},{10,9},{11,... | collective-permute-start | bytes 589832 | tf_op jit(solution)/shard_map/halo/ppermute | solution.py:499
  4.7 2.1 %collective-permute-start.1 = (bf16[384,256]{1,0:T(8,128)(2,1)S(1)}, bf16[384,256]{1,0:T(8,128)(2,1)S(1)}, u32[]{:S(2)}, u32[]{:S(2)}) collective-permute-start(bf16[384,256]{1,0:T(8,128)(2,1)S(1)} %pad_maximum_fusion.1), channel_id=1, source_target_pairs={{0,1},{1,0},{2,3},{3,2},{4,5},{5,4},{6,7},{7,6},{8,9},{9,8},{10,11... | collective-permute-start | bytes 589832 | tf_op jit(solution)/shard_map/halo/ppermute | solution.py:500
  6.9 1.2 %copy-done.2 = bf16[1,8,256,256]{3,2,1,0:T(8,128)(2,1)S(1)} copy-done((bf16[1,8,256,256]{3,2,1,0:T(8,128)(2,1)S(1)}, bf16[1,8,256,256]{3,2,1,0:T(8,128)(2,1)}, u32[]{:S(2)}) %copy-start.2) | copy-done | bytes 1048600
  8.1 3.0 %forward.2 = (f32[2560,128]{1,0:T(8,128)S(1)}, bf16[256,2560]{1,0:T(8,128)(2,1)S(1)}, f32[16,128]{1,0:T(8,128)S(1)}) custom-call(bf16[2048,256]{1,0:T(8,128)(2,1)S(1)} %bitcast.22, bf16[512,256]{1,0:T(8,128)(2,1)S(1)} %bitcast.26, bf16[9,256,128]{2,1,0:T(8,128)(2,1)S(1)} %bitcast.17, bf16[9,256,128]{2,1,0:T(8,128)(2,1)S(1)} %bitcast.19, ...), custom_call_target="tpu_custom_call" | custom-call | tf_op jit(solution)/shard_map/forward/pallas_call | solution.py:503
  11.9 15.9 %all_to_all.22 = f32[32,4,128]{2,1,0:T(4,128)S(1)} all-to-all(f32[32,4,128]{2,1,0:T(4,128)S(1)} %bitcast.29), channel_id=1, replica_groups=mesh['slide'=8,'tile'=32] {'tile'}, dimensions={0} | all-to-all | bytes 131072 | tf_op jit(solution)/shard_map/forward_sums/all_to_all | solution.py:518
  27.8 1.7 %loss_and_head.1 = (f32[2560,128]{1,0:T(8,128)S(1)}, bf16[512,128]{1,0:T(8,128)(2,1)S(1)}) custom-call(f32[2560,128]{1,0:T(8,128)S(1)} %get-tuple-element.25.conv_ref.all_conv_ref, f32[128,128]{1,0:T(8,128)S(1)} %bitcast.23, f32[16,128]{1,0:T(8,128)S(1)} %get-tuple-element.27.vectors_ref, bf16[8,128]{1,0:T(8,128)(2,1)S(1)} %copy-done.5, s32[8,256]{1,0:T(8,128)S(1)} %bitcast.30), custom_call_target="tpu_custom_call" | custom-call | tf_op jit(solution)/shard_map/loss_and_head/pallas_call | solution.py:520
  29.5 11.6 %all_to_all.23 = bf16[32,16,128]{2,1,0:T(8,128)(2,1)S(1)} all-to-all(bf16[32,16,128]{2,1,0:T(8,128)(2,1)S(1)} %bitcast.28), channel_id=1, replica_groups=mesh['slide'=8,'tile'=32] {'tile'}, dimensions={0} | all-to-all | bytes 262144 | tf_op jit(solution)/shard_map/backward_sums/all_to_all | solution.py:526
  41.1 2.8 %weight_grads.1 = (f32[256,1152]{1,0:T(8,128)S(1)}, bf16[256,1152]{1,0:T(8,128)(2,1)S(1)}, f32[16,128]{1,0:T(8,128)S(1)}) custom-call(f32[2560,128]{1,0:T(8,128)S(1)} %get-tuple-element.25.conv_ref.all_conv_ref, f32[2560,128]{1,0:T(8,128)S(1)} %get-tuple-element.28.all_dpre_ref, f32[128,128]{1,0:T(8,128)S(1)} %bitcast.24, bf16[512,128]{1,0:T(8,128)(2,1)S(1)} %bitcast.27, ...), custom_call_target="tpu_custom_call" | custom-call | tf_op jit(solution)/shard_map/weight_grads/pallas_call | solution.py:529
  44.5 1.6 %collective-permute-done.2.sent_ref = bf16[256,1152]{1,0:T(8,128)(2,1)S(1)} collective-permute-done((bf16[256,1152]{1,0:T(8,128)(2,1)S(1)}, bf16[256,1152]{1,0:T(8,128)(2,1)S(1)}, u32[]{:S(2)}, u32[]{:S(2)}) %collective-permute-start.2) | collective-permute-done | bytes 589856 | tf_op jit(solution)/shard_map/over_tiles/ppermute | solution.py:543
  46.9 2.0 %collective-permute-start.4 = (bf16[64,1152]{1,0:T(8,128)(2,1)S(1)}, bf16[64,1152]{1,0:T(8,128)(2,1)S(1)}, u32[]{:S(2)}, u32[]{:S(2)}) collective-permute-start(bf16[64,1152]{1,0:T(8,128)(2,1)S(1)} %get-tuple-element.35), channel_id=1, source_target_pairs={{0,16},{1,17},{2,18},{3,19},{4,20},{5,21},{6,22},{7,23},{8,24},{9,... | collective-permute-start | bytes 442376 | tf_op jit(solution)/shard_map/over_tiles/ppermute | solution.py:548
  48.9 1.4 %collective-permute-start.5 = (bf16[64,1152]{1,0:T(8,128)(2,1)S(1)}, bf16[64,1152]{1,0:T(8,128)(2,1)S(1)}, u32[]{:S(2)}, u32[]{:S(2)}) collective-permute-start(bf16[64,1152]{1,0:T(8,128)(2,1)S(1)} %get-tuple-element.36), channel_id=1, source_target_pairs={{0,24},{1,25},{2,26},{3,27},{4,28},{5,29},{6,30},{7,31},{8,0},{9,1... | collective-permute-start | bytes 442376 | tf_op jit(solution)/shard_map/over_tiles/ppermute | solution.py:548
  50.3 6.5 %collective-permute-done.3.one_ref = bf16[64,1152]{1,0:T(8,128)(2,1)S(1)} collective-permute-done((bf16[64,1152]{1,0:T(8,128)(2,1)S(1)}, bf16[64,1152]{1,0:T(8,128)(2,1)S(1)}, u32[]{:S(2)}, u32[]{:S(2)}) %collective-permute-start.3) | collective-permute-done | bytes 147488 | tf_op jit(solution)/shard_map/over_tiles/ppermute | solution.py:548
  57.5 0.8 collective-permute-start.6
  58.3 3.3 %collective-permute-start.7 = (bf16[16,1152]{1,0:T(8,128)(2,1)S(1)}, bf16[16,1152]{1,0:T(8,128)(2,1)S(1)}, u32[]{:S(2)}, u32[]{:S(2)}) collective-permute-start(bf16[16,1152]{1,0:T(8,128)(2,1)S(1)} %get-tuple-element.39), channel_id=1, source_target_pairs={{0,4},{1,5},{2,6},{3,7},{4,0},{5,1},{6,2},{7,3},{8,12},{9,13},{10,... | collective-permute-start | bytes 110600 | tf_op jit(solution)/shard_map/over_tiles/ppermute | solution.py:553
  61.7 2.4 %collective-permute-done.7.two_ref = bf16[16,1152]{1,0:T(8,128)(2,1)S(1)} collective-permute-done((bf16[16,1152]{1,0:T(8,128)(2,1)S(1)}, bf16[16,1152]{1,0:T(8,128)(2,1)S(1)}, u32[]{:S(2)}, u32[]{:S(2)}) %collective-permute-start.7) | collective-permute-done | bytes 36896 | tf_op jit(solution)/shard_map/over_tiles/ppermute | solution.py:553
  64.1 1.5 %collective-permute-done.8.three_ref = bf16[16,1152]{1,0:T(8,128)(2,1)S(1)} collective-permute-done((bf16[16,1152]{1,0:T(8,128)(2,1)S(1)}, bf16[16,1152]{1,0:T(8,128)(2,1)S(1)}, u32[]{:S(2)}, u32[]{:S(2)}) %collective-permute-start.8) | collective-permute-done | bytes 36896 | tf_op jit(solution)/shard_map/over_tiles/ppermute | solution.py:553
  65.7 5.5 %collective-permute-start.9 = (f32[16,1280]{1,0:T(8,128)S(1)}, f32[16,1280]{1,0:T(8,128)S(1)}, u32[]{:S(2)}, u32[]{:S(2)}) collective-permute-start(f32[16,1280]{1,0:T(8,128)S(1)} %over_tiles.5), channel_id=1, source_target_pairs={{0,32},{32,0},{64,96},{96,64},{128,160},{160,128},{192,224},{224,1... | collective-permute-start | bytes 245768 | tf_op jit(solution)/shard_map/over_slides/ppermute | solution.py:557
  71.1 3.0 %collective-permute-done.9 = f32[16,1280]{1,0:T(8,128)S(1)} collective-permute-done((f32[16,1280]{1,0:T(8,128)S(1)}, f32[16,1280]{1,0:T(8,128)S(1)}, u32[]{:S(2)}, u32[]{:S(2)}) %collective-permute-start.9) | collective-permute-done | bytes 81952 | tf_op jit(solution)/shard_map/over_slides/ppermute | solution.py:557
  74.1 3.1 %collective-permute-start.12 = (f32[16,1280]{1,0:T(8,128)S(1)}, f32[16,1280]{1,0:T(8,128)S(1)}, u32[]{:S(2)}, u32[]{:S(2)}) collective-permute-start(f32[16,1280]{1,0:T(8,128)S(1)} %add.3.own_ref), channel_id=1, source_target_pairs={{0,192},{32,224},{64,0},{96,32},{128,64},{160,96},{192,128},{224,1... | collective-permute-start | bytes 245768 | tf_op jit(solution)/shard_map/over_slides/ppermute | solution.py:559
  77.8 1.0 %collective-permute-start.10 = (f32[16,1280]{1,0:T(8,128)S(1)}, f32[16,1280]{1,0:T(8,128)S(1)}, u32[]{:S(2)}, u32[]{:S(2)}) collective-permute-start(f32[16,1280]{1,0:T(8,128)S(1)} %add.3.own_ref), channel_id=1, source_target_pairs={{0,64},{32,96},{64,128},{96,160},{128,192},{160,224},{192,0},{224,... | collective-permute-start | bytes 245768 | tf_op jit(solution)/shard_map/over_slides/ppermute | solution.py:559
  79.3 3.9 %collective-permute-done.11.two_ref = f32[16,1280]{1,0:T(8,128)S(1)} collective-permute-done((f32[16,1280]{1,0:T(8,128)S(1)}, f32[16,1280]{1,0:T(8,128)S(1)}, u32[]{:S(2)}, u32[]{:S(2)}) %collective-permute-start.11) | collective-permute-done | bytes 81952 | tf_op jit(solution)/shard_map/over_slides/ppermute | solution.py:559
  83.2 0.8 collective-permute-done.10.one_ref
  (39 shorter events, 4.8 us)
Async XLA Ops:
  0.6 6.2 %copy-start.3 = (bf16[1,4,128,256]{3,2,1,0:T(8,128)(2,1)S(1)}, bf16[1,4,128,256]{3,2,1,0:T(8,128)(2,1)}, u32[]{:S(2)}) copy-start(bf16[1,4,128,256]{3,2,1,0:T(8,128)(2,1)} %param.12) | copy-start | bytes 786436
  0.6 6.2 %copy-start.10 = (f32[8]{0:T(128)S(1)}, f32[8]{0:T(128)}, u32[]{:S(2)}) copy-start(f32[8]{0:T(128)} %bias_ref.1) | copy-start | bytes 100
  0.7 6.2 %copy-start.9 = (f32[128]{0:T(128)S(1)}, f32[128]{0:T(128)}, u32[]{:S(2)}) copy-start(f32[128]{0:T(128)} %param.18) | copy-start | bytes 1540
  0.7 6.1 %copy-start.8 = (f32[128]{0:T(128)S(1)}, f32[128]{0:T(128)}, u32[]{:S(2)}) copy-start(f32[128]{0:T(128)} %param.17) | copy-start | bytes 1540
  0.7 6.1 %copy-start.7 = (f32[128]{0:T(128)S(1)}, f32[128]{0:T(128)}, u32[]{:S(2)}) copy-start(f32[128]{0:T(128)} %param.16) | copy-start | bytes 1540
  0.7 6.1 %copy-start.6 = (f32[128]{0:T(128)S(1)}, f32[128]{0:T(128)}, u32[]{:S(2)}) copy-start(f32[128]{0:T(128)} %param.15) | copy-start | bytes 1540
  0.7 6.1 %copy-start.1 = (bf16[256,9,128]{2,0,1:T(8,128)(2,1)S(1)}, bf16[256,9,128]{2,0,1:T(8,128)(2,1)}, u32[]{:S(2)}) copy-start(bf16[256,9,128]{2,0,1:T(8,128)(2,1)} %param.14) | copy-start | bytes 1769476
  0.7 6.1 %copy-start = (bf16[256,9,128]{2,0,1:T(8,128)(2,1)S(1)}, bf16[256,9,128]{2,0,1:T(8,128)(2,1)}, u32[]{:S(2)}) copy-start(bf16[256,9,128]{2,0,1:T(8,128)(2,1)} %param.13) | copy-start | bytes 1769476
  2.7 8.3 %collective-permute-start = (bf16[384,256]{1,0:T(8,128)(2,1)S(1)}, bf16[384,256]{1,0:T(8,128)(2,1)S(1)}, u32[]{:S(2)}, u32[]{:S(2)}) collective-permute-start(bf16[384,256]{1,0:T(8,128)(2,1)S(1)} %pad_maximum_fusion), channel_id=1, source_target_pairs={{1,2},{2,1},{3,4},{4,3},{5,6},{6,5},{7,8},{8,7},{9,10},{10,9},{11,... | collective-permute-start | bytes 589832 | tf_op jit(solution)/shard_map/halo/ppermute | solution.py:499
  4.7 6.4 %collective-permute-start.1 = (bf16[384,256]{1,0:T(8,128)(2,1)S(1)}, bf16[384,256]{1,0:T(8,128)(2,1)S(1)}, u32[]{:S(2)}, u32[]{:S(2)}) collective-permute-start(bf16[384,256]{1,0:T(8,128)(2,1)S(1)} %pad_maximum_fusion.1), channel_id=1, source_target_pairs={{0,1},{1,0},{2,3},{3,2},{4,5},{5,4},{6,7},{7,6},{8,9},{9,8},{10,11... | collective-permute-start | bytes 589832 | tf_op jit(solution)/shard_map/halo/ppermute | solution.py:500
  6.9 1.2 %copy-start.2 = (bf16[1,8,256,256]{3,2,1,0:T(8,128)(2,1)S(1)}, bf16[1,8,256,256]{3,2,1,0:T(8,128)(2,1)}, u32[]{:S(2)}) copy-start(bf16[1,8,256,256]{3,2,1,0:T(8,128)(2,1)} %param.11) | copy-start | bytes 3145732
  11.1 16.7 %copy-start.4 = (s32[1,8,256]{2,1,0:T(8,128)S(1)}, s32[1,8,256]{2,1,0:T(8,128)}, u32[]{:S(2)}) copy-start(s32[1,8,256]{2,1,0:T(8,128)} %param.21) | copy-start | bytes 24580
  11.1 16.7 %copy-start.5 = (bf16[8,128]{1,0:T(8,128)(2,1)S(1)}, bf16[8,128]{1,0:T(8,128)(2,1)}, u32[]{:S(2)}) copy-start(bf16[8,128]{1,0:T(8,128)(2,1)} %class_ref.1) | copy-start | bytes 6148
  44.0 2.1 %collective-permute-start.2 = (bf16[256,1152]{1,0:T(8,128)(2,1)S(1)}, bf16[256,1152]{1,0:T(8,128)(2,1)S(1)}, u32[]{:S(2)}, u32[]{:S(2)}) collective-permute-start(bf16[256,1152]{1,0:T(8,128)(2,1)S(1)} %get-tuple-element.32), channel_id=1, source_target_pairs={{0,1},{1,0},{2,3},{3,2},{4,5},{5,4},{6,7},{7,6},{8,9},{9,8},{10,11... | collective-permute-start | bytes 1769480 | tf_op jit(solution)/shard_map/over_tiles/ppermute | solution.py:543
  46.2 10.6 %collective-permute-start.3 = (bf16[64,1152]{1,0:T(8,128)(2,1)S(1)}, bf16[64,1152]{1,0:T(8,128)(2,1)S(1)}, u32[]{:S(2)}, u32[]{:S(2)}) collective-permute-start(bf16[64,1152]{1,0:T(8,128)(2,1)S(1)} %get-tuple-element.34), channel_id=1, source_target_pairs={{0,8},{1,9},{2,10},{3,11},{4,12},{5,13},{6,14},{7,15},{8,16},{9,17... | collective-permute-start | bytes 442376 | tf_op jit(solution)/shard_map/over_tiles/ppermute | solution.py:548
  46.9 9.9 %collective-permute-start.4 = (bf16[64,1152]{1,0:T(8,128)(2,1)S(1)}, bf16[64,1152]{1,0:T(8,128)(2,1)S(1)}, u32[]{:S(2)}, u32[]{:S(2)}) collective-permute-start(bf16[64,1152]{1,0:T(8,128)(2,1)S(1)} %get-tuple-element.35), channel_id=1, source_target_pairs={{0,16},{1,17},{2,18},{3,19},{4,20},{5,21},{6,22},{7,23},{8,24},{9,... | collective-permute-start | bytes 442376 | tf_op jit(solution)/shard_map/over_tiles/ppermute | solution.py:548
  48.9 8.5 %collective-permute-start.5 = (bf16[64,1152]{1,0:T(8,128)(2,1)S(1)}, bf16[64,1152]{1,0:T(8,128)(2,1)S(1)}, u32[]{:S(2)}, u32[]{:S(2)}) collective-permute-start(bf16[64,1152]{1,0:T(8,128)(2,1)S(1)} %get-tuple-element.36), channel_id=1, source_target_pairs={{0,24},{1,25},{2,26},{3,27},{4,28},{5,29},{6,30},{7,31},{8,0},{9,1... | collective-permute-start | bytes 442376 | tf_op jit(solution)/shard_map/over_tiles/ppermute | solution.py:548
  57.5 4.2 %collective-permute-start.6 = (bf16[16,1152]{1,0:T(8,128)(2,1)S(1)}, bf16[16,1152]{1,0:T(8,128)(2,1)S(1)}, u32[]{:S(2)}, u32[]{:S(2)}) collective-permute-start(bf16[16,1152]{1,0:T(8,128)(2,1)S(1)} %get-tuple-element.38), channel_id=1, source_target_pairs={{0,2},{1,3},{2,4},{3,5},{4,6},{5,7},{6,0},{7,1},{8,10},{9,11},{10,... | collective-permute-start | bytes 110600 | tf_op jit(solution)/shard_map/over_tiles/ppermute | solution.py:553
  58.3 5.8 %collective-permute-start.7 = (bf16[16,1152]{1,0:T(8,128)(2,1)S(1)}, bf16[16,1152]{1,0:T(8,128)(2,1)S(1)}, u32[]{:S(2)}, u32[]{:S(2)}) collective-permute-start(bf16[16,1152]{1,0:T(8,128)(2,1)S(1)} %get-tuple-element.39), channel_id=1, source_target_pairs={{0,4},{1,5},{2,6},{3,7},{4,0},{5,1},{6,2},{7,3},{8,12},{9,13},{10,... | collective-permute-start | bytes 110600 | tf_op jit(solution)/shard_map/over_tiles/ppermute | solution.py:553
  61.7 4.0 %collective-permute-start.8 = (bf16[16,1152]{1,0:T(8,128)(2,1)S(1)}, bf16[16,1152]{1,0:T(8,128)(2,1)S(1)}, u32[]{:S(2)}, u32[]{:S(2)}) collective-permute-start(bf16[16,1152]{1,0:T(8,128)(2,1)S(1)} %get-tuple-element.40), channel_id=1, source_target_pairs={{0,6},{1,7},{2,0},{3,1},{4,2},{5,3},{6,4},{7,5},{8,14},{9,15},{10,... | collective-permute-start | bytes 110600 | tf_op jit(solution)/shard_map/over_tiles/ppermute | solution.py:553
  65.7 8.4 %collective-permute-start.9 = (f32[16,1280]{1,0:T(8,128)S(1)}, f32[16,1280]{1,0:T(8,128)S(1)}, u32[]{:S(2)}, u32[]{:S(2)}) collective-permute-start(f32[16,1280]{1,0:T(8,128)S(1)} %over_tiles.5), channel_id=1, source_target_pairs={{0,32},{32,0},{64,96},{96,64},{128,160},{160,128},{192,224},{224,1... | collective-permute-start | bytes 245768 | tf_op jit(solution)/shard_map/over_slides/ppermute | solution.py:557
  74.1 5.2 %collective-permute-start.12 = (f32[16,1280]{1,0:T(8,128)S(1)}, f32[16,1280]{1,0:T(8,128)S(1)}, u32[]{:S(2)}, u32[]{:S(2)}) collective-permute-start(f32[16,1280]{1,0:T(8,128)S(1)} %add.3.own_ref), channel_id=1, source_target_pairs={{0,192},{32,224},{64,0},{96,32},{128,64},{160,96},{192,128},{224,1... | collective-permute-start | bytes 245768 | tf_op jit(solution)/shard_map/over_slides/ppermute | solution.py:559
  77.2 6.0 %collective-permute-start.11 = (f32[16,1280]{1,0:T(8,128)S(1)}, f32[16,1280]{1,0:T(8,128)S(1)}, u32[]{:S(2)}, u32[]{:S(2)}) collective-permute-start(f32[16,1280]{1,0:T(8,128)S(1)} %add.3.own_ref), channel_id=1, source_target_pairs={{0,128},{32,160},{64,192},{96,224},{128,0},{160,32},{192,64},{224,... | collective-permute-start | bytes 245768 | tf_op jit(solution)/shard_map/over_slides/ppermute | solution.py:559
  77.8 6.2 %collective-permute-start.10 = (f32[16,1280]{1,0:T(8,128)S(1)}, f32[16,1280]{1,0:T(8,128)S(1)}, u32[]{:S(2)}, u32[]{:S(2)}) collective-permute-start(f32[16,1280]{1,0:T(8,128)S(1)} %add.3.own_ref), channel_id=1, source_target_pairs={{0,64},{32,96},{64,128},{96,160},{128,192},{160,224},{192,0},{224,... | collective-permute-start | bytes 245768 | tf_op jit(solution)/shard_map/over_slides/ppermute | solution.py:559

commit v5 on v4

--- a/solution.py
+++ b/solution.py
@@ -413,20 +413,40 @@
         ).astype(out_ref.dtype)
 
 
+def to_message(grads, head, out_ref):
+    wide, channels = grads.shape[1], head.shape[1]
+    out_ref[:, :wide] = grads.astype(BF16)
+    for at, part in enumerate(three_parts(head)):
+        out_ref[:, wide + at * channels : wide + (at + 1) * channels] = part.astype(BF16)
+
+
+def from_message(ref, wide):
+    values = ref[...].astype(F32)
+    channels = (values.shape[1] - wide) // 3
+    high, middle, low = [
+        values[:, wide + at * channels : wide + (at + 1) * channels] for at in range(3)
+    ]
+    return values[:, :wide], high + middle + low
+
+
 def last_tile_kernel(keep_ref, one_ref, two_ref, three_ref, head_ref, out_ref):
-    wide = keep_ref.shape[1]
-    out_ref[:, :wide] = (keep_ref[...] + one_ref[...].astype(F32)) + (
+    grads = (keep_ref[...] + one_ref[...].astype(F32)) + (
         two_ref[...].astype(F32) + three_ref[...].astype(F32)
     )
-    out_ref[:, wide:] = head_ref[...]
+    to_message(grads, head_ref[...], out_ref)
+
+
+def pair_kernel(wide, own_ref, other_ref, out_ref):
+    grads, head = from_message(own_ref, wide)
+    other_grads, other_head = from_message(other_ref, wide)
+    to_message(grads + other_grads, head + other_head, out_ref)
 
 
 def final_kernel(own_ref, one_ref, two_ref, three_ref, loss_ref, head_ref, grads_ref):
-    whole = (own_ref[...] + two_ref[...]) + (one_ref[...] + three_ref[...])
-    rows = head_ref.shape[0]
-    channels = head_ref.shape[1]
-    wide = whole.shape[1] - channels
-    head = whole[:, wide:]
+    rows, channels = head_ref.shape
+    wide = own_ref.shape[1] - 3 * channels
+    parts = [from_message(ref, wide) for ref in (own_ref, one_ref, two_ref, three_ref)]
+    whole, head = [(own + two) + (one + three) for own, one, two, three in zip(*parts)]
     total = head[rows : rows + 1, 1:2]
     loss_ref[...] = head[rows : rows + 1, 0:1] / total
     head_ref[...] = head[:rows, :] / total
@@ -551,10 +571,12 @@
             next_sum_kernel, (shape(size, wide),) + (shape(size, wide, dtype=BF16),) * 3
         )(parts[0], *got)
         got = [lax.ppermute(parts[step], "tile", z_pairs(step)) for step in (1, 2, 3)]
-        own = call(last_tile_kernel, shape(size, wide + channels))(parts[0], *got, head)
+        message = shape(size, wide + 3 * channels, dtype=BF16)
+        own = call(last_tile_kernel, message)(parts[0], *got, head)
     with jax.named_scope("over_slides"):
         slides = lax.axis_size("slide")
-        own = own + lax.ppermute(own, "slide", [(i, i ^ 1) for i in range(slides)])
+        other = lax.ppermute(own, "slide", [(i, i ^ 1) for i in range(slides)])
+        own = call(functools.partial(pair_kernel, wide), message)(own, other)
         got = [
             lax.ppermute(own, "slide", [(i, (i + 2 * step) % slides) for i in range(slides)])
             for step in (1, 2, 3)

time: 85 us -> 84 us (0.988)
  waiting for transfers between devices: 20.9 us -> 19.9 us
where the time goes in v5:
time: 84 us; the launch traced here: 83.8 us
  blocking collectives  27.5 us (33%)
  starting transfers between devices  22.9 us (27%)
  waiting for transfers between devices  19.9 us (24%)
  Pallas kernels  9.33 us (11%)
  local copies, waits for them, and re-layouts  3.25 us (4%)
  between operations  0.86 us (1%)
    all_to_all x1, blocking collectives, per_device(): stats = lax.all_to_all(stats, 'tile', 0, 0, tiled=True)  15.9 us
    all_to_all x1, blocking collectives, per_device(): head = lax.all_to_all(head, 'tile', 0, 0, tiled=True)  11.6 us
    ppermute x3, waiting for transfers between devices, per_device(): lax.ppermute(parts[step], 'tile', x_pairs(step))  7.15 us
    ppermute x1, starting transfers between devices, per_device(): other = lax.ppermute(own, 'slide', [(i, i ^ 1) for i in range(slides)])  5.48 us
    ppermute x3, starting transfers between devices, per_device(): lax.ppermute(own, 'slide', [(i, (i + 2 * step) % slides) for i in range(s...  4.7 us
    ppermute x3, waiting for transfers between devices, per_device(): lax.ppermute(own, 'slide', [(i, (i + 2 * step) % slides) for i in range(s...  4.52 us
    ppermute x3, starting transfers between devices, per_device(): lax.ppermute(parts[step], 'tile', z_pairs(step))  4.17 us
    ppermute x3, starting transfers between devices, per_device(): lax.ppermute(parts[step], 'tile', x_pairs(step))  4.05 us
  transfers between devices with their start and end apart: 13, of which 9 were waited for; matrix products, arithmetic and copies ran while one was open for 0% of the time, Pallas kernels for 4%

profile of v5, /device:TPU:32, one launch (start us, length us, event | category | flops | bytes accessed | tf_op | source)
XLA Modules:
  0.0 83.8 jit_solution(7769106951745987759)
XLA Ops:
  0.7 1.0 %constant_dynamic-slice_fusion = (bf16[128,256]{1,0:T(8,128)(2,1)S(1)}, bf16[128,256]{1,0:T(8,128)(2,1)S(1)}) fusion(bf16[512,256]{1,0:T(8,128)(2,1)} %bitcast.25, u32[]{:T(128)S(6)} %mul.15, u32[]{:T(128)S(6)} %mul.13), kind=kLoop, calls=%fused_computation.2 | loop fusion | bytes 262152 | tf_op jit(solution)/shard_map/halo/dynamic_slice | solution.py:515
  1.7 1.0 %constant_dynamic-slice_fusion.1 = (bf16[256,256]{1,0:T(8,128)(2,1)S(1)}, bf16[256,256]{1,0:T(8,128)(2,1)S(1)}) fusion(bf16[2048,256]{1,0:T(8,128)(2,1)} %bitcast.21, u32[]{:T(128)S(6)} %mul.14, u32[]{:T(128)S(6)} %mul.12), kind=kLoop, calls=%fused_computation.3 | loop fusion | bytes 524296 | tf_op jit(solution)/shard_map/halo/dynamic_slice | solution.py:515
  2.7 1.9 %collective-permute-start = (bf16[384,256]{1,0:T(8,128)(2,1)S(1)}, bf16[384,256]{1,0:T(8,128)(2,1)S(1)}, u32[]{:S(2)}, u32[]{:S(2)}) collective-permute-start(bf16[384,256]{1,0:T(8,128)(2,1)S(1)} %pad_maximum_fusion), channel_id=1, source_target_pairs={{1,2},{2,1},{3,4},{4,3},{5,6},{6,5},{7,8},{8,7},{9,10},{10,9},{11,... | collective-permute-start | bytes 589832 | tf_op jit(solution)/shard_map/halo/ppermute | solution.py:519
  4.7 2.1 %collective-permute-start.1 = (bf16[384,256]{1,0:T(8,128)(2,1)S(1)}, bf16[384,256]{1,0:T(8,128)(2,1)S(1)}, u32[]{:S(2)}, u32[]{:S(2)}) collective-permute-start(bf16[384,256]{1,0:T(8,128)(2,1)S(1)} %pad_maximum_fusion.1), channel_id=1, source_target_pairs={{0,1},{1,0},{2,3},{3,2},{4,5},{5,4},{6,7},{7,6},{8,9},{9,8},{10,11... | collective-permute-start | bytes 589832 | tf_op jit(solution)/shard_map/halo/ppermute | solution.py:520
  6.9 1.2 %copy-done.2 = bf16[1,8,256,256]{3,2,1,0:T(8,128)(2,1)S(1)} copy-done((bf16[1,8,256,256]{3,2,1,0:T(8,128)(2,1)S(1)}, bf16[1,8,256,256]{3,2,1,0:T(8,128)(2,1)}, u32[]{:S(2)}) %copy-start.2) | copy-done | bytes 1048600
  8.1 3.0 %forward.2 = (f32[2560,128]{1,0:T(8,128)S(1)}, bf16[256,2560]{1,0:T(8,128)(2,1)S(1)}, f32[16,128]{1,0:T(8,128)S(1)}) custom-call(bf16[2048,256]{1,0:T(8,128)(2,1)S(1)} %bitcast.22, bf16[512,256]{1,0:T(8,128)(2,1)S(1)} %bitcast.26, bf16[9,256,128]{2,1,0:T(8,128)(2,1)S(1)} %bitcast.17, bf16[9,256,128]{2,1,0:T(8,128)(2,1)S(1)} %bitcast.19, ...), custom_call_target="tpu_custom_call" | custom-call | tf_op jit(solution)/shard_map/forward/pallas_call | solution.py:523
  11.1 0.8 forward.3
  11.9 15.9 %all_to_all.22 = f32[32,4,128]{2,1,0:T(4,128)S(1)} all-to-all(f32[32,4,128]{2,1,0:T(4,128)S(1)} %bitcast.29), channel_id=1, replica_groups=mesh['slide'=8,'tile'=32] {'tile'}, dimensions={0} | all-to-all | bytes 131072 | tf_op jit(solution)/shard_map/forward_sums/all_to_all | solution.py:538
  27.8 1.7 %loss_and_head.1 = (f32[2560,128]{1,0:T(8,128)S(1)}, bf16[512,128]{1,0:T(8,128)(2,1)S(1)}) custom-call(f32[2560,128]{1,0:T(8,128)S(1)} %get-tuple-element.25.conv_ref.all_conv_ref, f32[128,128]{1,0:T(8,128)S(1)} %bitcast.23, f32[16,128]{1,0:T(8,128)S(1)} %get-tuple-element.27.vectors_ref, bf16[8,128]{1,0:T(8,128)(2,1)S(1)} %copy-done.5, s32[8,256]{1,0:T(8,128)S(1)} %bitcast.30), custom_call_target="tpu_custom_call" | custom-call | tf_op jit(solution)/shard_map/loss_and_head/pallas_call | solution.py:540
  29.5 11.6 %all_to_all.23 = bf16[32,16,128]{2,1,0:T(8,128)(2,1)S(1)} all-to-all(bf16[32,16,128]{2,1,0:T(8,128)(2,1)S(1)} %bitcast.28), channel_id=1, replica_groups=mesh['slide'=8,'tile'=32] {'tile'}, dimensions={0} | all-to-all | bytes 262144 | tf_op jit(solution)/shard_map/backward_sums/all_to_all | solution.py:546
  41.1 2.8 %weight_grads.1 = (f32[256,1152]{1,0:T(8,128)S(1)}, bf16[256,1152]{1,0:T(8,128)(2,1)S(1)}, f32[16,128]{1,0:T(8,128)S(1)}) custom-call(f32[2560,128]{1,0:T(8,128)S(1)} %get-tuple-element.25.conv_ref.all_conv_ref, f32[2560,128]{1,0:T(8,128)S(1)} %get-tuple-element.28.all_dpre_ref, f32[128,128]{1,0:T(8,128)S(1)} %bitcast.24, bf16[512,128]{1,0:T(8,128)(2,1)S(1)} %bitcast.27, ...), custom_call_target="tpu_custom_call" | custom-call | tf_op jit(solution)/shard_map/weight_grads/pallas_call | solution.py:549
  44.5 1.6 %collective-permute-done.2.sent_ref = bf16[256,1152]{1,0:T(8,128)(2,1)S(1)} collective-permute-done((bf16[256,1152]{1,0:T(8,128)(2,1)S(1)}, bf16[256,1152]{1,0:T(8,128)(2,1)S(1)}, u32[]{:S(2)}, u32[]{:S(2)}) %collective-permute-start.2) | collective-permute-done | bytes 589856 | tf_op jit(solution)/shard_map/over_tiles/ppermute | solution.py:563
  46.9 2.0 %collective-permute-start.4 = (bf16[64,1152]{1,0:T(8,128)(2,1)S(1)}, bf16[64,1152]{1,0:T(8,128)(2,1)S(1)}, u32[]{:S(2)}, u32[]{:S(2)}) collective-permute-start(bf16[64,1152]{1,0:T(8,128)(2,1)S(1)} %get-tuple-element.35), channel_id=1, source_target_pairs={{0,16},{1,17},{2,18},{3,19},{4,20},{5,21},{6,22},{7,23},{8,24},{9,... | collective-permute-start | bytes 442376 | tf_op jit(solution)/shard_map/over_tiles/ppermute | solution.py:568
  48.9 1.4 %collective-permute-start.5 = (bf16[64,1152]{1,0:T(8,128)(2,1)S(1)}, bf16[64,1152]{1,0:T(8,128)(2,1)S(1)}, u32[]{:S(2)}, u32[]{:S(2)}) collective-permute-start(bf16[64,1152]{1,0:T(8,128)(2,1)S(1)} %get-tuple-element.36), channel_id=1, source_target_pairs={{0,24},{1,25},{2,26},{3,27},{4,28},{5,29},{6,30},{7,31},{8,0},{9,1... | collective-permute-start | bytes 442376 | tf_op jit(solution)/shard_map/over_tiles/ppermute | solution.py:568
  50.3 6.5 %collective-permute-done.3.one_ref = bf16[64,1152]{1,0:T(8,128)(2,1)S(1)} collective-permute-done((bf16[64,1152]{1,0:T(8,128)(2,1)S(1)}, bf16[64,1152]{1,0:T(8,128)(2,1)S(1)}, u32[]{:S(2)}, u32[]{:S(2)}) %collective-permute-start.3) | collective-permute-done | bytes 147488 | tf_op jit(solution)/shard_map/over_tiles/ppermute | solution.py:568
  57.5 0.8 %collective-permute-start.6 = (bf16[16,1152]{1,0:T(8,128)(2,1)S(1)}, bf16[16,1152]{1,0:T(8,128)(2,1)S(1)}, u32[]{:S(2)}, u32[]{:S(2)}) collective-permute-start(bf16[16,1152]{1,0:T(8,128)(2,1)S(1)} %get-tuple-element.38), channel_id=1, source_target_pairs={{0,2},{1,3},{2,4},{3,5},{4,6},{5,7},{6,0},{7,1},{8,10},{9,11},{10,... | collective-permute-start | bytes 110600 | tf_op jit(solution)/shard_map/over_tiles/ppermute | solution.py:573
  58.3 3.3 %collective-permute-start.7 = (bf16[16,1152]{1,0:T(8,128)(2,1)S(1)}, bf16[16,1152]{1,0:T(8,128)(2,1)S(1)}, u32[]{:S(2)}, u32[]{:S(2)}) collective-permute-start(bf16[16,1152]{1,0:T(8,128)(2,1)S(1)} %get-tuple-element.39), channel_id=1, source_target_pairs={{0,4},{1,5},{2,6},{3,7},{4,0},{5,1},{6,2},{7,3},{8,12},{9,13},{10,... | collective-permute-start | bytes 110600 | tf_op jit(solution)/shard_map/over_tiles/ppermute | solution.py:573
  61.7 2.4 %collective-permute-done.7.two_ref = bf16[16,1152]{1,0:T(8,128)(2,1)S(1)} collective-permute-done((bf16[16,1152]{1,0:T(8,128)(2,1)S(1)}, bf16[16,1152]{1,0:T(8,128)(2,1)S(1)}, u32[]{:S(2)}, u32[]{:S(2)}) %collective-permute-start.7) | collective-permute-done | bytes 36896 | tf_op jit(solution)/shard_map/over_tiles/ppermute | solution.py:573
  64.1 1.5 %collective-permute-done.8.three_ref = bf16[16,1152]{1,0:T(8,128)(2,1)S(1)} collective-permute-done((bf16[16,1152]{1,0:T(8,128)(2,1)S(1)}, bf16[16,1152]{1,0:T(8,128)(2,1)S(1)}, u32[]{:S(2)}, u32[]{:S(2)}) %collective-permute-start.8) | collective-permute-done | bytes 36896 | tf_op jit(solution)/shard_map/over_tiles/ppermute | solution.py:573
  65.7 5.5 %collective-permute-start.9 = (bf16[16,1536]{1,0:T(8,128)(2,1)S(1)}, bf16[16,1536]{1,0:T(8,128)(2,1)S(1)}, u32[]{:S(2)}, u32[]{:S(2)}) collective-permute-start(bf16[16,1536]{1,0:T(8,128)(2,1)S(1)} %over_tiles.5.own_ref), channel_id=1, source_target_pairs={{0,32},{32,0},{64,96},{96,64},{128,160},{160,128},{192,224},{224,1... | collective-permute-start | bytes 147464 | tf_op jit(solution)/shard_map/over_slides/ppermute | solution.py:578
  71.1 2.6 %collective-permute-done.9.other_ref = bf16[16,1536]{1,0:T(8,128)(2,1)S(1)} collective-permute-done((bf16[16,1536]{1,0:T(8,128)(2,1)S(1)}, bf16[16,1536]{1,0:T(8,128)(2,1)S(1)}, u32[]{:S(2)}, u32[]{:S(2)}) %collective-permute-start.9) | collective-permute-done | bytes 49184 | tf_op jit(solution)/shard_map/over_slides/ppermute | solution.py:578
  73.8 3.1 %collective-permute-start.12 = (bf16[16,1536]{1,0:T(8,128)(2,1)S(1)}, bf16[16,1536]{1,0:T(8,128)(2,1)S(1)}, u32[]{:S(2)}, u32[]{:S(2)}) collective-permute-start(bf16[16,1536]{1,0:T(8,128)(2,1)S(1)} %over_slides.2.own_ref), channel_id=1, source_target_pairs={{0,192},{32,224},{64,0},{96,32},{128,64},{160,96},{192,128},{224,1... | collective-permute-start | bytes 147464 | tf_op jit(solution)/shard_map/over_slides/ppermute | solution.py:581
  77.5 1.0 %collective-permute-start.10 = (bf16[16,1536]{1,0:T(8,128)(2,1)S(1)}, bf16[16,1536]{1,0:T(8,128)(2,1)S(1)}, u32[]{:S(2)}, u32[]{:S(2)}) collective-permute-start(bf16[16,1536]{1,0:T(8,128)(2,1)S(1)} %over_slides.2.own_ref), channel_id=1, source_target_pairs={{0,64},{32,96},{64,128},{96,160},{128,192},{160,224},{192,0},{224,... | collective-permute-start | bytes 147464 | tf_op jit(solution)/shard_map/over_slides/ppermute | solution.py:581
  78.6 3.9 %collective-permute-done.11.two_ref = bf16[16,1536]{1,0:T(8,128)(2,1)S(1)} collective-permute-done((bf16[16,1536]{1,0:T(8,128)(2,1)S(1)}, bf16[16,1536]{1,0:T(8,128)(2,1)S(1)}, u32[]{:S(2)}, u32[]{:S(2)}) %collective-permute-start.11) | collective-permute-done | bytes 49184 | tf_op jit(solution)/shard_map/over_slides/ppermute | solution.py:581
  (39 shorter events, 4.3 us)
Async XLA Ops:
  0.6 6.2 %copy-start.3 = (bf16[1,4,128,256]{3,2,1,0:T(8,128)(2,1)S(1)}, bf16[1,4,128,256]{3,2,1,0:T(8,128)(2,1)}, u32[]{:S(2)}) copy-start(bf16[1,4,128,256]{3,2,1,0:T(8,128)(2,1)} %param.12) | copy-start | bytes 786436
  0.6 6.2 %copy-start.10 = (f32[8]{0:T(128)S(1)}, f32[8]{0:T(128)}, u32[]{:S(2)}) copy-start(f32[8]{0:T(128)} %bias_ref.1) | copy-start | bytes 100
  0.7 6.2 %copy-start.9 = (f32[128]{0:T(128)S(1)}, f32[128]{0:T(128)}, u32[]{:S(2)}) copy-start(f32[128]{0:T(128)} %param.18) | copy-start | bytes 1540
  0.7 6.1 %copy-start.8 = (f32[128]{0:T(128)S(1)}, f32[128]{0:T(128)}, u32[]{:S(2)}) copy-start(f32[128]{0:T(128)} %param.17) | copy-start | bytes 1540
  0.7 6.1 %copy-start.7 = (f32[128]{0:T(128)S(1)}, f32[128]{0:T(128)}, u32[]{:S(2)}) copy-start(f32[128]{0:T(128)} %param.16) | copy-start | bytes 1540
  0.7 6.1 %copy-start.6 = (f32[128]{0:T(128)S(1)}, f32[128]{0:T(128)}, u32[]{:S(2)}) copy-start(f32[128]{0:T(128)} %param.15) | copy-start | bytes 1540
  0.7 6.1 %copy-start.1 = (bf16[256,9,128]{2,0,1:T(8,128)(2,1)S(1)}, bf16[256,9,128]{2,0,1:T(8,128)(2,1)}, u32[]{:S(2)}) copy-start(bf16[256,9,128]{2,0,1:T(8,128)(2,1)} %param.14) | copy-start | bytes 1769476
  0.7 6.1 %copy-start = (bf16[256,9,128]{2,0,1:T(8,128)(2,1)S(1)}, bf16[256,9,128]{2,0,1:T(8,128)(2,1)}, u32[]{:S(2)}) copy-start(bf16[256,9,128]{2,0,1:T(8,128)(2,1)} %param.13) | copy-start | bytes 1769476
  2.7 8.3 %collective-permute-start = (bf16[384,256]{1,0:T(8,128)(2,1)S(1)}, bf16[384,256]{1,0:T(8,128)(2,1)S(1)}, u32[]{:S(2)}, u32[]{:S(2)}) collective-permute-start(bf16[384,256]{1,0:T(8,128)(2,1)S(1)} %pad_maximum_fusion), channel_id=1, source_target_pairs={{1,2},{2,1},{3,4},{4,3},{5,6},{6,5},{7,8},{8,7},{9,10},{10,9},{11,... | collective-permute-start | bytes 589832 | tf_op jit(solution)/shard_map/halo/ppermute | solution.py:519
  4.7 6.4 %collective-permute-start.1 = (bf16[384,256]{1,0:T(8,128)(2,1)S(1)}, bf16[384,256]{1,0:T(8,128)(2,1)S(1)}, u32[]{:S(2)}, u32[]{:S(2)}) collective-permute-start(bf16[384,256]{1,0:T(8,128)(2,1)S(1)} %pad_maximum_fusion.1), channel_id=1, source_target_pairs={{0,1},{1,0},{2,3},{3,2},{4,5},{5,4},{6,7},{7,6},{8,9},{9,8},{10,11... | collective-permute-start | bytes 589832 | tf_op jit(solution)/shard_map/halo/ppermute | solution.py:520
  6.9 1.2 %copy-start.2 = (bf16[1,8,256,256]{3,2,1,0:T(8,128)(2,1)S(1)}, bf16[1,8,256,256]{3,2,1,0:T(8,128)(2,1)}, u32[]{:S(2)}) copy-start(bf16[1,8,256,256]{3,2,1,0:T(8,128)(2,1)} %param.11) | copy-start | bytes 3145732
  11.1 16.7 %copy-start.4 = (s32[1,8,256]{2,1,0:T(8,128)S(1)}, s32[1,8,256]{2,1,0:T(8,128)}, u32[]{:S(2)}) copy-start(s32[1,8,256]{2,1,0:T(8,128)} %param.21) | copy-start | bytes 24580
  11.1 16.7 %copy-start.5 = (bf16[8,128]{1,0:T(8,128)(2,1)S(1)}, bf16[8,128]{1,0:T(8,128)(2,1)}, u32[]{:S(2)}) copy-start(bf16[8,128]{1,0:T(8,128)(2,1)} %class_ref.1) | copy-start | bytes 6148
  44.0 2.1 %collective-permute-start.2 = (bf16[256,1152]{1,0:T(8,128)(2,1)S(1)}, bf16[256,1152]{1,0:T(8,128)(2,1)S(1)}, u32[]{:S(2)}, u32[]{:S(2)}) collective-permute-start(bf16[256,1152]{1,0:T(8,128)(2,1)S(1)} %get-tuple-element.32), channel_id=1, source_target_pairs={{0,1},{1,0},{2,3},{3,2},{4,5},{5,4},{6,7},{7,6},{8,9},{9,8},{10,11... | collective-permute-start | bytes 1769480 | tf_op jit(solution)/shard_map/over_tiles/ppermute | solution.py:563
  46.2 10.6 %collective-permute-start.3 = (bf16[64,1152]{1,0:T(8,128)(2,1)S(1)}, bf16[64,1152]{1,0:T(8,128)(2,1)S(1)}, u32[]{:S(2)}, u32[]{:S(2)}) collective-permute-start(bf16[64,1152]{1,0:T(8,128)(2,1)S(1)} %get-tuple-element.34), channel_id=1, source_target_pairs={{0,8},{1,9},{2,10},{3,11},{4,12},{5,13},{6,14},{7,15},{8,16},{9,17... | collective-permute-start | bytes 442376 | tf_op jit(solution)/shard_map/over_tiles/ppermute | solution.py:568
  46.9 9.9 %collective-permute-start.4 = (bf16[64,1152]{1,0:T(8,128)(2,1)S(1)}, bf16[64,1152]{1,0:T(8,128)(2,1)S(1)}, u32[]{:S(2)}, u32[]{:S(2)}) collective-permute-start(bf16[64,1152]{1,0:T(8,128)(2,1)S(1)} %get-tuple-element.35), channel_id=1, source_target_pairs={{0,16},{1,17},{2,18},{3,19},{4,20},{5,21},{6,22},{7,23},{8,24},{9,... | collective-permute-start | bytes 442376 | tf_op jit(solution)/shard_map/over_tiles/ppermute | solution.py:568
  48.9 8.5 %collective-permute-start.5 = (bf16[64,1152]{1,0:T(8,128)(2,1)S(1)}, bf16[64,1152]{1,0:T(8,128)(2,1)S(1)}, u32[]{:S(2)}, u32[]{:S(2)}) collective-permute-start(bf16[64,1152]{1,0:T(8,128)(2,1)S(1)} %get-tuple-element.36), channel_id=1, source_target_pairs={{0,24},{1,25},{2,26},{3,27},{4,28},{5,29},{6,30},{7,31},{8,0},{9,1... | collective-permute-start | bytes 442376 | tf_op jit(solution)/shard_map/over_tiles/ppermute | solution.py:568
  57.5 4.2 %collective-permute-start.6 = (bf16[16,1152]{1,0:T(8,128)(2,1)S(1)}, bf16[16,1152]{1,0:T(8,128)(2,1)S(1)}, u32[]{:S(2)}, u32[]{:S(2)}) collective-permute-start(bf16[16,1152]{1,0:T(8,128)(2,1)S(1)} %get-tuple-element.38), channel_id=1, source_target_pairs={{0,2},{1,3},{2,4},{3,5},{4,6},{5,7},{6,0},{7,1},{8,10},{9,11},{10,... | collective-permute-start | bytes 110600 | tf_op jit(solution)/shard_map/over_tiles/ppermute | solution.py:573
  58.3 5.8 %collective-permute-start.7 = (bf16[16,1152]{1,0:T(8,128)(2,1)S(1)}, bf16[16,1152]{1,0:T(8,128)(2,1)S(1)}, u32[]{:S(2)}, u32[]{:S(2)}) collective-permute-start(bf16[16,1152]{1,0:T(8,128)(2,1)S(1)} %get-tuple-element.39), channel_id=1, source_target_pairs={{0,4},{1,5},{2,6},{3,7},{4,0},{5,1},{6,2},{7,3},{8,12},{9,13},{10,... | collective-permute-start | bytes 110600 | tf_op jit(solution)/shard_map/over_tiles/ppermute | solution.py:573
  61.7 4.0 %collective-permute-start.8 = (bf16[16,1152]{1,0:T(8,128)(2,1)S(1)}, bf16[16,1152]{1,0:T(8,128)(2,1)S(1)}, u32[]{:S(2)}, u32[]{:S(2)}) collective-permute-start(bf16[16,1152]{1,0:T(8,128)(2,1)S(1)} %get-tuple-element.40), channel_id=1, source_target_pairs={{0,6},{1,7},{2,0},{3,1},{4,2},{5,3},{6,4},{7,5},{8,14},{9,15},{10,... | collective-permute-start | bytes 110600 | tf_op jit(solution)/shard_map/over_tiles/ppermute | solution.py:573
  65.7 8.1 %collective-permute-start.9 = (bf16[16,1536]{1,0:T(8,128)(2,1)S(1)}, bf16[16,1536]{1,0:T(8,128)(2,1)S(1)}, u32[]{:S(2)}, u32[]{:S(2)}) collective-permute-start(bf16[16,1536]{1,0:T(8,128)(2,1)S(1)} %over_tiles.5.own_ref), channel_id=1, source_target_pairs={{0,32},{32,0},{64,96},{96,64},{128,160},{160,128},{192,224},{224,1... | collective-permute-start | bytes 147464 | tf_op jit(solution)/shard_map/over_slides/ppermute | solution.py:578
  73.8 4.9 %collective-permute-start.12 = (bf16[16,1536]{1,0:T(8,128)(2,1)S(1)}, bf16[16,1536]{1,0:T(8,128)(2,1)S(1)}, u32[]{:S(2)}, u32[]{:S(2)}) collective-permute-start(bf16[16,1536]{1,0:T(8,128)(2,1)S(1)} %over_slides.2.own_ref), channel_id=1, source_target_pairs={{0,192},{32,224},{64,0},{96,32},{128,64},{160,96},{192,128},{224,1... | collective-permute-start | bytes 147464 | tf_op jit(solution)/shard_map/over_slides/ppermute | solution.py:581
  76.9 5.6 %collective-permute-start.11 = (bf16[16,1536]{1,0:T(8,128)(2,1)S(1)}, bf16[16,1536]{1,0:T(8,128)(2,1)S(1)}, u32[]{:S(2)}, u32[]{:S(2)}) collective-permute-start(bf16[16,1536]{1,0:T(8,128)(2,1)S(1)} %over_slides.2.own_ref), channel_id=1, source_target_pairs={{0,128},{32,160},{64,192},{96,224},{128,0},{160,32},{192,64},{224,... | collective-permute-start | bytes 147464 | tf_op jit(solution)/shard_map/over_slides/ppermute | solution.py:581
  77.5 5.5 %collective-permute-start.10 = (bf16[16,1536]{1,0:T(8,128)(2,1)S(1)}, bf16[16,1536]{1,0:T(8,128)(2,1)S(1)}, u32[]{:S(2)}, u32[]{:S(2)}) collective-permute-start(bf16[16,1536]{1,0:T(8,128)(2,1)S(1)} %over_slides.2.own_ref), channel_id=1, source_target_pairs={{0,64},{32,96},{64,128},{96,160},{128,192},{160,224},{192,0},{224,... | collective-permute-start | bytes 147464 | tf_op jit(solution)/shard_map/over_slides/ppermute | solution.py:581

commit v6 on v5

--- a/solution.py
+++ b/solution.py
@@ -91,6 +91,7 @@
     conv_ref,
     turn_ref,
     vectors_ref,
+    inner_ref,
 ):
     for at, ref in enumerate((fgain_ref, foffset_ref, cgain_ref, coffset_ref)):
         vectors_ref[at : at + 1, :] = ref[...]
@@ -100,8 +101,9 @@
     fine_size = fine_ref.shape[0]
     fconv_ref, cconv_ref = levels(conv_ref, fine_size)
     fturn_ref, cturn_ref = levels(turn_ref, fine_size, 1)
-    level_products(coarse_ref, ck_ref, cconv_ref, rows_coarse)
-    level_products(fine_ref, fk_ref, fconv_ref, rows_fine)
+    coarse_sums = level_products(coarse_ref, ck_ref, cconv_ref, rows_coarse)
+    fine_sums = level_products(fine_ref, fk_ref, fconv_ref, rows_fine)
+    inner_ref[...] = jnp.concatenate((fine_sums + coarse_sums) * 2, axis=0)
     order = channel_order(fine_ref.shape[1])
     cturn_ref[...] = turn(order, coarse_ref[...])
     fturn_ref[...] = turn(order, fine_ref[...])
@@ -110,6 +112,7 @@
 def level_products(x_ref, k_ref, out_ref, rows):
     cols = x_ref.shape[0] // rows
     channels = k_ref.shape[2]
+    sums = [jnp.zeros((1, channels), F32)] * 2
     for row in range(rows):
         total = None
         for a in range(3):
@@ -121,70 +124,76 @@
                     preferred_element_type=F32,
                 )
                 total = part if total is None else total + part
-        out_ref[row * cols : (row + 1) * cols, :] = joined(total, channels)
+        value = joined(total, channels)
+        out_ref[row * cols : (row + 1) * cols, :] = value
+        if 0 < row < rows - 1:
+            sums = with_sums(sums, value)
+    return sums
+
+
+def with_sums(sums, value):
+    added = [jnp.sum(v, axis=0, keepdims=True) for v in (value, value * value)]
+    return [total + part for total, part in zip(sums, added)]
 
 
 def edges_kernel(
     rows_fine,
     rows_coarse,
     part_ref,
+    inner_ref,
     off_ref,
     on_ref,
     fk_ref,
     ck_ref,
-    conv_ref,
+    edges_ref,
     stats_ref,
 ):
     fine_size = part_ref.shape[0] * 4 // 5
-    fpart_ref, cpart_ref = levels(part_ref, fine_size)
-    fconv_ref, cconv_ref = levels(conv_ref, fine_size)
     above, below = above_below(off_ref, on_ref)
     start = 0
     found = []
-    for part_ref, k_ref, out_ref, rows in (
-        (fpart_ref, fk_ref, fconv_ref, rows_fine),
-        (cpart_ref, ck_ref, cconv_ref, rows_coarse),
+    for level, (level_ref, k_ref, rows) in enumerate(
+        zip(levels(part_ref, fine_size), (fk_ref, ck_ref), (rows_fine, rows_coarse))
     ):
-        cols = part_ref.shape[0] // rows
+        cols = level_ref.shape[0] // rows
         channels = k_ref.shape[2]
-        first = jnp.zeros((1, channels), F32)
-        second = jnp.zeros((1, channels), F32)
-        for row in range(rows):
-            value = part_ref[row * cols : (row + 1) * cols, :]
-            for edge, halo, a in ((0, above, 0), (rows - 1, below, 2)):
-                if row == edge:
-                    value = value + joined(
-                        jnp.dot(
-                            halo[start : start + cols, :],
-                            taps_of(k_ref, a),
-                            preferred_element_type=F32,
-                        ),
-                        channels,
-                    )
-            out_ref[row * cols : (row + 1) * cols, :] = value
-            first = first + jnp.sum(value, axis=0, keepdims=True)
-            second = second + jnp.sum(value * value, axis=0, keepdims=True)
-        found += [first, second]
+        sums = [inner_ref[2 * level + at : 2 * level + at + 1, :] for at in range(2)]
+        for edge, (row, halo, a) in enumerate(((0, above, 0), (rows - 1, below, 2))):
+            product = jnp.dot(
+                halo[start : start + cols, :], taps_of(k_ref, a), preferred_element_type=F32
+            )
+            value = level_ref[row * cols : (row + 1) * cols, :] + joined(product, channels)
+            to = 2 * start + edge * cols
+            edges_ref[to : to + cols, :] = value
+            sums = with_sums(sums, value)
+        found += sums
         start += cols
-    found = jnp.concatenate(found + found, axis=0)
-    for pair in range(stats_ref.shape[0] // 8):
-        stats_ref[8 * pair : 8 * pair + 8, :] = found
-
-
-def same_group(channels):
-    per_group = channels // GROUPS
-    row = lax.broadcasted_iota(jnp.int32, (channels, channels), 0)
-    col = lax.broadcasted_iota(jnp.int32, (channels, channels), 1)
-    return (row // per_group == col // per_group).astype(F32)
+    gather, _, own_block = lane_blocks(channels)
+    stats_ref[...] = jnp.broadcast_to(packed_sums(found, gather, own_block), stats_ref.shape)
+
+
+def conv_rows(part_ref, edges_ref, level, row, rows):
+    wide = edges_ref.shape[0] // 3
+    cols = wide // (level + 1)
+    if 0 < row < rows - 1:
+        return part_ref[row * cols : (row + 1) * cols, :]
+    at = 2 * level * wide + (cols if row else 0)
+    return edges_ref[at : at + cols, :]
 
 
 def over_tiles(all_ref, count):
     return jnp.sum(all_ref[...].astype(F32).reshape(-1, count, all_ref.shape[1]), axis=0)
 
 
-def stats_sums(stats_ref, members):
-    pairs = over_tiles(stats_ref, 8)
-    return over_group(pairs[0:4, :] + pairs[4:8, :], members)
+def stats_sums(stats_ref, channels):
+    _, spread, own_block = lane_blocks(channels)
+    total = jnp.sum(stats_ref[...], axis=0, keepdims=True)
+    return over_group(jnp.where(own_block, total, 0.0), spread)
+
+
+def packed_sums(rows, gather, own_block):
+    groups = over_group(jnp.concatenate(rows, axis=0), gather)
+    return jnp.sum(jnp.where(own_block, groups, 0.0), axis=0, keepdims=True)
 
 
 def lane_blocks(channels):
@@ -218,6 +227,7 @@
     rows_fine,
     numbers,
     conv_ref,
+    edges_ref,
     stats_ref,
     vectors_ref,
     class_ref,
@@ -234,7 +244,7 @@
     cols = fconv_ref.shape[0] // rows_fine
     half = cols // 2
     classes = class_ref.shape[0]
-    sums = stats_sums(stats_ref, same_group(channels))
+    sums = stats_sums(stats_ref, channels)
     fmean, fscale = norm_terms(sums, 0, numbers[0])
     cmean, cscale = norm_terms(sums, 1, numbers[1])
     weights = class_ref[...]
@@ -248,7 +258,8 @@
     tissue_sum = jnp.zeros((1, 2 * cols), F32)
     class_id = lax.broadcasted_iota(jnp.int32, (classes, 2 * cols), 0)
     for pair in range(rows_fine // 2):
-        cnormed = (cconv_ref[pair * half : (pair + 1) * half, :] - cmean) * cscale
+        cconv = conv_rows(cconv_ref, edges_ref, 1, pair, rows_fine // 2)
+        cnormed = (cconv - cmean) * cscale
         cpre = cnormed * cgain + coffset
         cact = jnp.maximum(cpre, 0.0)
         wide_ref[pl.ds(0, half, stride=2), :] = cact
@@ -256,7 +267,8 @@
         up = wide_ref[...]
         up = jnp.concatenate([up, up], axis=0)
         here = slice(2 * pair * cols, 2 * (pair + 1) * cols)
-        normed = (fconv_ref[here, :] - fmean) * fscale
+        fconv = [conv_rows(fconv_ref, edges_ref, 0, 2 * pair + at, rows_fine) for at in range(2)]
+        normed = (jnp.concatenate(fconv, axis=0) - fmean) * fscale
         pre = normed * fgain + foffset
         merged = (jnp.maximum(pre, 0.0) + up).astype(BF16)
         logits = (
@@ -294,9 +306,7 @@
         rows_sum[3] = rows_sum[3] + jnp.sum(dpre, axis=0, keepdims=True)
     gains = (fgain, fgain, cgain, cgain)
     gather, _, own_block = lane_blocks(channels)
-    spread = jnp.concatenate([row * gain for row, gain in zip(rows_sum, gains)], axis=0)
-    packed = jnp.where(own_block, over_group(spread, gather), 0.0)
-    packed = jnp.sum(packed, axis=0, keepdims=True)
+    packed = packed_sums([row * gain for row, gain in zip(rows_sum, gains)], gather, own_block)
     lane = lax.broadcasted_iota(jnp.int32, (1, channels), 1)
     scalars = jnp.zeros((1, channels), F32)
     totals = [jnp.sum(row, axis=1, keepdims=True) for row in (loss_sum, tissue_sum)]
@@ -312,6 +322,7 @@
     rows_fine,
     numbers,
     all_conv_ref,
+    edges_ref,
     all_dpre_ref,
     stats_ref,
     back_ref,
@@ -331,8 +342,7 @@
     fdpre_ref, cdpre_ref = levels(all_dpre_ref, fine_size)
     fturn_ref, cturn_ref = levels(all_turn_ref, fine_size, 1)
     channels = all_conv_ref.shape[1]
-    members = same_group(channels)
-    sums = stats_sums(stats_ref, members)
+    sums = stats_sums(stats_ref, channels)
     back = over_tiles(back_ref, 16)
     lane = lax.broadcasted_iota(jnp.int32, (1, channels), 1)
     loss_all, tissue_all = [
@@ -362,7 +372,7 @@
         with_normed, plain = means[0:1, :], means[1:2, :]
         for row in range(rows):
             here = slice(row * cols, (row + 1) * cols)
-            normed = (conv_ref[here, :] - mean) * scale
+            normed = (conv_rows(conv_ref, edges_ref, level, row, rows) - mean) * scale
             dconv = (dpre_ref[here, :] * gain - plain - normed * with_normed) * scale
             d_ref[here, :channels] = moved(dconv, -1).astype(BF16)
             d_ref[here, channels : 2 * channels] = dconv.astype(BF16)
@@ -520,20 +530,20 @@
         on = lax.ppermute(on, "tile", swaps(range(0, tiles, 2)))
     with jax.named_scope("forward"):
         whole = pl.BlockSpec(memory_space=pltpu.VMEM)
-        part, turned, vectors = call(
+        conv, turned, vectors, inner = call(
             functools.partial(interior_kernel, height, height // 2),
             (
                 shape(pixels, channels),
                 shape(in_channels, pixels, dtype=BF16),
                 shape(8 + classes, channels),
+                shape(8, channels),
             ),
             in_specs=[whole] * 8 + [pl.BlockSpec(memory_space=pltpu.SMEM)],
         )(fine, coarse, fk, ck, *vectors, class_offset)
-        conv, stats = call(
+        edges, stats = call(
             functools.partial(edges_kernel, height, height // 2),
-            (shape(pixels, channels), shape(4 * tiles, channels)),
-            input_output_aliases={0: 0},
-        )(part, off, on, fk, ck)
+            (shape(3 * width, channels), shape(tiles, channels)),
+        )(conv, inner, off, on, fk, ck)
     with jax.named_scope("forward_sums"):
         stats = lax.all_to_all(stats, "tile", 0, 0, tiled=True)
     with jax.named_scope("loss_and_head"):
@@ -541,7 +551,7 @@
             functools.partial(loss_kernel, height, numbers),
             (shape(pixels, channels), shape(16 * tiles, channels, dtype=BF16)),
             (pltpu.VMEM((width, channels), F32), pltpu.VMEM((width, channels), F32)),
-        )(conv, stats, vectors, class_kernel, labels)
+        )(conv, edges, stats, vectors, class_kernel, labels)
     with jax.named_scope("backward_sums"):
         head = lax.all_to_all(head, "tile", 0, 0, tiled=True)
     with jax.named_scope("weight_grads"):
@@ -558,7 +568,7 @@
                 pltpu.VMEM((coarse_size, 3 * channels), BF16),
                 pltpu.VMEM((in_channels, wide), F32),
             ),
-        )(conv, dpre, stats, head, vectors, turned, off, on)
+        )(conv, edges, dpre, stats, head, vectors, turned, off, on)
     with jax.named_scope("over_tiles"):
         sent = lax.ppermute(send, "tile", core_pairs())
         size = in_channels // 4

time: 84 us -> 83.5 us (level)
  no operation moved by 1% of the time
where the time goes in v6:
time: 83.5 us; the launch traced here: 83.3 us
  blocking collectives  27.2 us (33%)
  starting transfers between devices  22.9 us (27%)
  waiting for transfers between devices  19.9 us (24%)
  Pallas kernels  9.2 us (11%)
  local copies, waits for them, and re-layouts  3.25 us (4%)
  between operations  0.85 us (1%)
    all_to_all x1, blocking collectives, per_device(): stats = lax.all_to_all(stats, 'tile', 0, 0, tiled=True)  15.7 us
    all_to_all x1, blocking collectives, per_device(): head = lax.all_to_all(head, 'tile', 0, 0, tiled=True)  11.5 us
    ppermute x3, waiting for transfers between devices, per_device(): lax.ppermute(parts[step], 'tile', x_pairs(step))  7.14 us
    ppermute x1, starting transfers between devices, per_device(): other = lax.ppermute(own, 'slide', [(i, i ^ 1) for i in range(slides)])  5.47 us
    ppermute x3, starting transfers between devices, per_device(): lax.ppermute(own, 'slide', [(i, (i + 2 * step) % slides) for i in range(s...  4.69 us
    ppermute x3, waiting for transfers between devices, per_device(): lax.ppermute(own, 'slide', [(i, (i + 2 * step) % slides) for i in range(s...  4.52 us
    ppermute x3, starting transfers between devices, per_device(): lax.ppermute(parts[step], 'tile', z_pairs(step))  4.17 us
    ppermute x3, starting transfers between devices, per_device(): lax.ppermute(parts[step], 'tile', x_pairs(step))  4.05 us
  transfers between devices with their start and end apart: 13, of which 9 were waited for; matrix products, arithmetic and copies ran while one was open for 0% of the time, Pallas kernels for 4%

profile of v6, /device:TPU:32, one launch (start us, length us, event | category | flops | bytes accessed | tf_op | source)
XLA Modules:
  0.0 83.3 jit_solution(11476160986559709084)
XLA Ops:
  0.7 1.0 %constant_dynamic-slice_fusion = (bf16[128,256]{1,0:T(8,128)(2,1)S(1)}, bf16[128,256]{1,0:T(8,128)(2,1)S(1)}) fusion(bf16[512,256]{1,0:T(8,128)(2,1)} %bitcast.25, u32[]{:T(128)S(6)} %mul.15, u32[]{:T(128)S(6)} %mul.13), kind=kLoop, calls=%fused_computation.2 | loop fusion | bytes 262152 | tf_op jit(solution)/shard_map/halo/dynamic_slice | solution.py:525
  1.7 1.0 %constant_dynamic-slice_fusion.1 = (bf16[256,256]{1,0:T(8,128)(2,1)S(1)}, bf16[256,256]{1,0:T(8,128)(2,1)S(1)}) fusion(bf16[2048,256]{1,0:T(8,128)(2,1)} %bitcast.23, u32[]{:T(128)S(6)} %mul.14, u32[]{:T(128)S(6)} %mul.12), kind=kLoop, calls=%fused_computation.3 | loop fusion | bytes 524296 | tf_op jit(solution)/shard_map/halo/dynamic_slice | solution.py:525
  2.7 1.9 %collective-permute-start = (bf16[384,256]{1,0:T(8,128)(2,1)S(1)}, bf16[384,256]{1,0:T(8,128)(2,1)S(1)}, u32[]{:S(2)}, u32[]{:S(2)}) collective-permute-start(bf16[384,256]{1,0:T(8,128)(2,1)S(1)} %pad_maximum_fusion), channel_id=1, source_target_pairs={{1,2},{2,1},{3,4},{4,3},{5,6},{6,5},{7,8},{8,7},{9,10},{10,9},{11,... | collective-permute-start | bytes 589832 | tf_op jit(solution)/shard_map/halo/ppermute | solution.py:529
  4.7 2.1 %collective-permute-start.1 = (bf16[384,256]{1,0:T(8,128)(2,1)S(1)}, bf16[384,256]{1,0:T(8,128)(2,1)S(1)}, u32[]{:S(2)}, u32[]{:S(2)}) collective-permute-start(bf16[384,256]{1,0:T(8,128)(2,1)S(1)} %pad_maximum_fusion.1), channel_id=1, source_target_pairs={{0,1},{1,0},{2,3},{3,2},{4,5},{5,4},{6,7},{7,6},{8,9},{9,8},{10,11... | collective-permute-start | bytes 589832 | tf_op jit(solution)/shard_map/halo/ppermute | solution.py:530
  6.9 1.2 %copy-done.2 = bf16[1,8,256,256]{3,2,1,0:T(8,128)(2,1)S(1)} copy-done((bf16[1,8,256,256]{3,2,1,0:T(8,128)(2,1)S(1)}, bf16[1,8,256,256]{3,2,1,0:T(8,128)(2,1)}, u32[]{:S(2)}) %copy-start.2) | copy-done | bytes 1048600
  8.1 3.0 %forward.2 = (f32[2560,128]{1,0:T(8,128)S(1)}, bf16[256,2560]{1,0:T(8,128)(2,1)S(1)}, f32[16,128]{1,0:T(8,128)S(1)}, f32[8,128]{1,0:T(8,128)S(1)}) custom-call(bf16[2048,256]{1,0:T(8,128)(2,1)S(1)} %bitcast.24, bf16[512,256]{1,0:T(8,128)(2,1)S(1)} %bitcast.26, bf16[9,256,128]{2,1,0:T(8,128)(2,1)S(1)} %bitcast.19, bf16[9,256,128]{2,1,0:T(8,128)(2,1)S(1)} %bitcast.21, ...), custom_call_target="tpu_custom_call" | custom-call | tf_op jit(solution)/shard_map/forward/pallas_call | solution.py:533
  11.7 15.7 %all_to_all.22 = f32[32,1,128]{2,1,0:T(1,128)S(1)} all-to-all(f32[32,1,128]{2,1,0:T(1,128)S(1)} %bitcast.31), channel_id=1, replica_groups=mesh['slide'=8,'tile'=32] {'tile'}, dimensions={0} | all-to-all | bytes 32768 | tf_op jit(solution)/shard_map/forward_sums/all_to_all | solution.py:548
  27.4 1.7 %loss_and_head.1 = (f32[2560,128]{1,0:T(8,128)S(1)}, bf16[512,128]{1,0:T(8,128)(2,1)S(1)}) custom-call(f32[2560,128]{1,0:T(8,128)S(1)} %get-tuple-element.25.part_ref.conv_ref.all_conv_ref, f32[768,128]{1,0:T(8,128)S(1)} %get-tuple-element.27.edges_ref, f32[32,128]{1,0:T(8,128)S(1)} %bitcast.28, f32[16,128]{1,0:T(8,128)S(1)} %get-tuple-element.29.vectors_ref, ...), custom_call_target="tpu_custom_call" | custom-call | tf_op jit(solution)/shard_map/loss_and_head/pallas_call | solution.py:550
  29.1 11.5 %all_to_all.23 = bf16[32,16,128]{2,1,0:T(8,128)(2,1)S(1)} all-to-all(bf16[32,16,128]{2,1,0:T(8,128)(2,1)S(1)} %bitcast.30), channel_id=1, replica_groups=mesh['slide'=8,'tile'=32] {'tile'}, dimensions={0} | all-to-all | bytes 262144 | tf_op jit(solution)/shard_map/backward_sums/all_to_all | solution.py:556
  40.6 2.9 %weight_grads.1 = (f32[256,1152]{1,0:T(8,128)S(1)}, bf16[256,1152]{1,0:T(8,128)(2,1)S(1)}, f32[16,128]{1,0:T(8,128)S(1)}) custom-call(f32[2560,128]{1,0:T(8,128)S(1)} %get-tuple-element.25.part_ref.conv_ref.all_conv_ref, f32[768,128]{1,0:T(8,128)S(1)} %get-tuple-element.27.edges_ref, f32[2560,128]{1,0:T(8,128)S(1)} %get-tuple-element.30.all_dpre_ref, ...), custom_call_target="tpu_custom_call" | custom-call | tf_op jit(solution)/shard_map/weight_grads/pallas_call | solution.py:559
  44.0 1.6 %collective-permute-done.2.sent_ref = bf16[256,1152]{1,0:T(8,128)(2,1)S(1)} collective-permute-done((bf16[256,1152]{1,0:T(8,128)(2,1)S(1)}, bf16[256,1152]{1,0:T(8,128)(2,1)S(1)}, u32[]{:S(2)}, u32[]{:S(2)}) %collective-permute-start.2) | collective-permute-done | bytes 589856 | tf_op jit(solution)/shard_map/over_tiles/ppermute | solution.py:573
  46.5 2.0 %collective-permute-start.4 = (bf16[64,1152]{1,0:T(8,128)(2,1)S(1)}, bf16[64,1152]{1,0:T(8,128)(2,1)S(1)}, u32[]{:S(2)}, u32[]{:S(2)}) collective-permute-start(bf16[64,1152]{1,0:T(8,128)(2,1)S(1)} %get-tuple-element.37), channel_id=1, source_target_pairs={{0,16},{1,17},{2,18},{3,19},{4,20},{5,21},{6,22},{7,23},{8,24},{9,... | collective-permute-start | bytes 442376 | tf_op jit(solution)/shard_map/over_tiles/ppermute | solution.py:578
  48.4 1.4 %collective-permute-start.5 = (bf16[64,1152]{1,0:T(8,128)(2,1)S(1)}, bf16[64,1152]{1,0:T(8,128)(2,1)S(1)}, u32[]{:S(2)}, u32[]{:S(2)}) collective-permute-start(bf16[64,1152]{1,0:T(8,128)(2,1)S(1)} %get-tuple-element.38), channel_id=1, source_target_pairs={{0,24},{1,25},{2,26},{3,27},{4,28},{5,29},{6,30},{7,31},{8,0},{9,1... | collective-permute-start | bytes 442376 | tf_op jit(solution)/shard_map/over_tiles/ppermute | solution.py:578
  49.8 6.5 %collective-permute-done.3.one_ref = bf16[64,1152]{1,0:T(8,128)(2,1)S(1)} collective-permute-done((bf16[64,1152]{1,0:T(8,128)(2,1)S(1)}, bf16[64,1152]{1,0:T(8,128)(2,1)S(1)}, u32[]{:S(2)}, u32[]{:S(2)}) %collective-permute-start.3) | collective-permute-done | bytes 147488 | tf_op jit(solution)/shard_map/over_tiles/ppermute | solution.py:578
  57.0 0.8 collective-permute-start.6
  57.8 3.4 %collective-permute-start.7 = (bf16[16,1152]{1,0:T(8,128)(2,1)S(1)}, bf16[16,1152]{1,0:T(8,128)(2,1)S(1)}, u32[]{:S(2)}, u32[]{:S(2)}) collective-permute-start(bf16[16,1152]{1,0:T(8,128)(2,1)S(1)} %get-tuple-element.41), channel_id=1, source_target_pairs={{0,4},{1,5},{2,6},{3,7},{4,0},{5,1},{6,2},{7,3},{8,12},{9,13},{10,... | collective-permute-start | bytes 110600 | tf_op jit(solution)/shard_map/over_tiles/ppermute | solution.py:583
  61.3 2.4 %collective-permute-done.7.two_ref = bf16[16,1152]{1,0:T(8,128)(2,1)S(1)} collective-permute-done((bf16[16,1152]{1,0:T(8,128)(2,1)S(1)}, bf16[16,1152]{1,0:T(8,128)(2,1)S(1)}, u32[]{:S(2)}, u32[]{:S(2)}) %collective-permute-start.7) | collective-permute-done | bytes 36896 | tf_op jit(solution)/shard_map/over_tiles/ppermute | solution.py:583
  63.6 1.5 %collective-permute-done.8.three_ref = bf16[16,1152]{1,0:T(8,128)(2,1)S(1)} collective-permute-done((bf16[16,1152]{1,0:T(8,128)(2,1)S(1)}, bf16[16,1152]{1,0:T(8,128)(2,1)S(1)}, u32[]{:S(2)}, u32[]{:S(2)}) %collective-permute-start.8) | collective-permute-done | bytes 36896 | tf_op jit(solution)/shard_map/over_tiles/ppermute | solution.py:583
  65.2 5.5 %collective-permute-start.9 = (bf16[16,1536]{1,0:T(8,128)(2,1)S(1)}, bf16[16,1536]{1,0:T(8,128)(2,1)S(1)}, u32[]{:S(2)}, u32[]{:S(2)}) collective-permute-start(bf16[16,1536]{1,0:T(8,128)(2,1)S(1)} %over_tiles.5.own_ref), channel_id=1, source_target_pairs={{0,32},{32,0},{64,96},{96,64},{128,160},{160,128},{192,224},{224,1... | collective-permute-start | bytes 147464 | tf_op jit(solution)/shard_map/over_slides/ppermute | solution.py:588
  70.7 2.6 %collective-permute-done.9.other_ref = bf16[16,1536]{1,0:T(8,128)(2,1)S(1)} collective-permute-done((bf16[16,1536]{1,0:T(8,128)(2,1)S(1)}, bf16[16,1536]{1,0:T(8,128)(2,1)S(1)}, u32[]{:S(2)}, u32[]{:S(2)}) %collective-permute-start.9) | collective-permute-done | bytes 49184 | tf_op jit(solution)/shard_map/over_slides/ppermute | solution.py:588
  73.3 3.1 %collective-permute-start.12 = (bf16[16,1536]{1,0:T(8,128)(2,1)S(1)}, bf16[16,1536]{1,0:T(8,128)(2,1)S(1)}, u32[]{:S(2)}, u32[]{:S(2)}) collective-permute-start(bf16[16,1536]{1,0:T(8,128)(2,1)S(1)} %over_slides.2.own_ref), channel_id=1, source_target_pairs={{0,192},{32,224},{64,0},{96,32},{128,64},{160,96},{192,128},{224,1... | collective-permute-start | bytes 147464 | tf_op jit(solution)/shard_map/over_slides/ppermute | solution.py:591
  77.0 1.0 %collective-permute-start.10 = (bf16[16,1536]{1,0:T(8,128)(2,1)S(1)}, bf16[16,1536]{1,0:T(8,128)(2,1)S(1)}, u32[]{:S(2)}, u32[]{:S(2)}) collective-permute-start(bf16[16,1536]{1,0:T(8,128)(2,1)S(1)} %over_slides.2.own_ref), channel_id=1, source_target_pairs={{0,64},{32,96},{64,128},{96,160},{128,192},{160,224},{192,0},{224,... | collective-permute-start | bytes 147464 | tf_op jit(solution)/shard_map/over_slides/ppermute | solution.py:591
  78.1 3.9 %collective-permute-done.11.two_ref = bf16[16,1536]{1,0:T(8,128)(2,1)S(1)} collective-permute-done((bf16[16,1536]{1,0:T(8,128)(2,1)S(1)}, bf16[16,1536]{1,0:T(8,128)(2,1)S(1)}, u32[]{:S(2)}, u32[]{:S(2)}) %collective-permute-start.11) | collective-permute-done | bytes 49184 | tf_op jit(solution)/shard_map/over_slides/ppermute | solution.py:591
  82.5 0.8 over_slides.3
  (39 shorter events, 4.1 us)
Async XLA Ops:
  0.6 6.2 %copy-start.3 = (bf16[1,4,128,256]{3,2,1,0:T(8,128)(2,1)S(1)}, bf16[1,4,128,256]{3,2,1,0:T(8,128)(2,1)}, u32[]{:S(2)}) copy-start(bf16[1,4,128,256]{3,2,1,0:T(8,128)(2,1)} %param.12) | copy-start | bytes 786436
  0.6 6.2 %copy-start.10 = (f32[8]{0:T(128)S(1)}, f32[8]{0:T(128)}, u32[]{:S(2)}) copy-start(f32[8]{0:T(128)} %bias_ref.1) | copy-start | bytes 100
  0.7 6.2 %copy-start.9 = (f32[128]{0:T(128)S(1)}, f32[128]{0:T(128)}, u32[]{:S(2)}) copy-start(f32[128]{0:T(128)} %param.18) | copy-start | bytes 1540
  0.7 6.1 %copy-start.8 = (f32[128]{0:T(128)S(1)}, f32[128]{0:T(128)}, u32[]{:S(2)}) copy-start(f32[128]{0:T(128)} %param.17) | copy-start | bytes 1540
  0.7 6.1 %copy-start.7 = (f32[128]{0:T(128)S(1)}, f32[128]{0:T(128)}, u32[]{:S(2)}) copy-start(f32[128]{0:T(128)} %param.16) | copy-start | bytes 1540
  0.7 6.1 %copy-start.6 = (f32[128]{0:T(128)S(1)}, f32[128]{0:T(128)}, u32[]{:S(2)}) copy-start(f32[128]{0:T(128)} %param.15) | copy-start | bytes 1540
  0.7 6.1 %copy-start.1 = (bf16[256,9,128]{2,0,1:T(8,128)(2,1)S(1)}, bf16[256,9,128]{2,0,1:T(8,128)(2,1)}, u32[]{:S(2)}) copy-start(bf16[256,9,128]{2,0,1:T(8,128)(2,1)} %param.14) | copy-start | bytes 1769476
  0.7 6.1 %copy-start = (bf16[256,9,128]{2,0,1:T(8,128)(2,1)S(1)}, bf16[256,9,128]{2,0,1:T(8,128)(2,1)}, u32[]{:S(2)}) copy-start(bf16[256,9,128]{2,0,1:T(8,128)(2,1)} %param.13) | copy-start | bytes 1769476
  2.7 8.3 %collective-permute-start = (bf16[384,256]{1,0:T(8,128)(2,1)S(1)}, bf16[384,256]{1,0:T(8,128)(2,1)S(1)}, u32[]{:S(2)}, u32[]{:S(2)}) collective-permute-start(bf16[384,256]{1,0:T(8,128)(2,1)S(1)} %pad_maximum_fusion), channel_id=1, source_target_pairs={{1,2},{2,1},{3,4},{4,3},{5,6},{6,5},{7,8},{8,7},{9,10},{10,9},{11,... | collective-permute-start | bytes 589832 | tf_op jit(solution)/shard_map/halo/ppermute | solution.py:529
  4.7 6.4 %collective-permute-start.1 = (bf16[384,256]{1,0:T(8,128)(2,1)S(1)}, bf16[384,256]{1,0:T(8,128)(2,1)S(1)}, u32[]{:S(2)}, u32[]{:S(2)}) collective-permute-start(bf16[384,256]{1,0:T(8,128)(2,1)S(1)} %pad_maximum_fusion.1), channel_id=1, source_target_pairs={{0,1},{1,0},{2,3},{3,2},{4,5},{5,4},{6,7},{7,6},{8,9},{9,8},{10,11... | collective-permute-start | bytes 589832 | tf_op jit(solution)/shard_map/halo/ppermute | solution.py:530
  6.9 1.2 %copy-start.2 = (bf16[1,8,256,256]{3,2,1,0:T(8,128)(2,1)S(1)}, bf16[1,8,256,256]{3,2,1,0:T(8,128)(2,1)}, u32[]{:S(2)}) copy-start(bf16[1,8,256,256]{3,2,1,0:T(8,128)(2,1)} %param.11) | copy-start | bytes 3145732
  11.1 16.3 %copy-start.4 = (s32[1,8,256]{2,1,0:T(8,128)S(1)}, s32[1,8,256]{2,1,0:T(8,128)}, u32[]{:S(2)}) copy-start(s32[1,8,256]{2,1,0:T(8,128)} %param.21) | copy-start | bytes 24580
  11.1 16.3 %copy-start.5 = (bf16[8,128]{1,0:T(8,128)(2,1)S(1)}, bf16[8,128]{1,0:T(8,128)(2,1)}, u32[]{:S(2)}) copy-start(bf16[8,128]{1,0:T(8,128)(2,1)} %class_ref.1) | copy-start | bytes 6148
  43.5 2.1 %collective-permute-start.2 = (bf16[256,1152]{1,0:T(8,128)(2,1)S(1)}, bf16[256,1152]{1,0:T(8,128)(2,1)S(1)}, u32[]{:S(2)}, u32[]{:S(2)}) collective-permute-start(bf16[256,1152]{1,0:T(8,128)(2,1)S(1)} %get-tuple-element.34), channel_id=1, source_target_pairs={{0,1},{1,0},{2,3},{3,2},{4,5},{5,4},{6,7},{7,6},{8,9},{9,8},{10,11... | collective-permute-start | bytes 1769480 | tf_op jit(solution)/shard_map/over_tiles/ppermute | solution.py:573
  45.8 10.6 %collective-permute-start.3 = (bf16[64,1152]{1,0:T(8,128)(2,1)S(1)}, bf16[64,1152]{1,0:T(8,128)(2,1)S(1)}, u32[]{:S(2)}, u32[]{:S(2)}) collective-permute-start(bf16[64,1152]{1,0:T(8,128)(2,1)S(1)} %get-tuple-element.36), channel_id=1, source_target_pairs={{0,8},{1,9},{2,10},{3,11},{4,12},{5,13},{6,14},{7,15},{8,16},{9,17... | collective-permute-start | bytes 442376 | tf_op jit(solution)/shard_map/over_tiles/ppermute | solution.py:578
  46.5 9.9 %collective-permute-start.4 = (bf16[64,1152]{1,0:T(8,128)(2,1)S(1)}, bf16[64,1152]{1,0:T(8,128)(2,1)S(1)}, u32[]{:S(2)}, u32[]{:S(2)}) collective-permute-start(bf16[64,1152]{1,0:T(8,128)(2,1)S(1)} %get-tuple-element.37), channel_id=1, source_target_pairs={{0,16},{1,17},{2,18},{3,19},{4,20},{5,21},{6,22},{7,23},{8,24},{9,... | collective-permute-start | bytes 442376 | tf_op jit(solution)/shard_map/over_tiles/ppermute | solution.py:578
  48.4 8.5 %collective-permute-start.5 = (bf16[64,1152]{1,0:T(8,128)(2,1)S(1)}, bf16[64,1152]{1,0:T(8,128)(2,1)S(1)}, u32[]{:S(2)}, u32[]{:S(2)}) collective-permute-start(bf16[64,1152]{1,0:T(8,128)(2,1)S(1)} %get-tuple-element.38), channel_id=1, source_target_pairs={{0,24},{1,25},{2,26},{3,27},{4,28},{5,29},{6,30},{7,31},{8,0},{9,1... | collective-permute-start | bytes 442376 | tf_op jit(solution)/shard_map/over_tiles/ppermute | solution.py:578
  57.0 4.2 %collective-permute-start.6 = (bf16[16,1152]{1,0:T(8,128)(2,1)S(1)}, bf16[16,1152]{1,0:T(8,128)(2,1)S(1)}, u32[]{:S(2)}, u32[]{:S(2)}) collective-permute-start(bf16[16,1152]{1,0:T(8,128)(2,1)S(1)} %get-tuple-element.40), channel_id=1, source_target_pairs={{0,2},{1,3},{2,4},{3,5},{4,6},{5,7},{6,0},{7,1},{8,10},{9,11},{10,... | collective-permute-start | bytes 110600 | tf_op jit(solution)/shard_map/over_tiles/ppermute | solution.py:583
  57.8 5.8 %collective-permute-start.7 = (bf16[16,1152]{1,0:T(8,128)(2,1)S(1)}, bf16[16,1152]{1,0:T(8,128)(2,1)S(1)}, u32[]{:S(2)}, u32[]{:S(2)}) collective-permute-start(bf16[16,1152]{1,0:T(8,128)(2,1)S(1)} %get-tuple-element.41), channel_id=1, source_target_pairs={{0,4},{1,5},{2,6},{3,7},{4,0},{5,1},{6,2},{7,3},{8,12},{9,13},{10,... | collective-permute-start | bytes 110600 | tf_op jit(solution)/shard_map/over_tiles/ppermute | solution.py:583
  61.2 4.0 %collective-permute-start.8 = (bf16[16,1152]{1,0:T(8,128)(2,1)S(1)}, bf16[16,1152]{1,0:T(8,128)(2,1)S(1)}, u32[]{:S(2)}, u32[]{:S(2)}) collective-permute-start(bf16[16,1152]{1,0:T(8,128)(2,1)S(1)} %get-tuple-element.42), channel_id=1, source_target_pairs={{0,6},{1,7},{2,0},{3,1},{4,2},{5,3},{6,4},{7,5},{8,14},{9,15},{10,... | collective-permute-start | bytes 110600 | tf_op jit(solution)/shard_map/over_tiles/ppermute | solution.py:583
  65.2 8.1 %collective-permute-start.9 = (bf16[16,1536]{1,0:T(8,128)(2,1)S(1)}, bf16[16,1536]{1,0:T(8,128)(2,1)S(1)}, u32[]{:S(2)}, u32[]{:S(2)}) collective-permute-start(bf16[16,1536]{1,0:T(8,128)(2,1)S(1)} %over_tiles.5.own_ref), channel_id=1, source_target_pairs={{0,32},{32,0},{64,96},{96,64},{128,160},{160,128},{192,224},{224,1... | collective-permute-start | bytes 147464 | tf_op jit(solution)/shard_map/over_slides/ppermute | solution.py:588
  73.3 4.8 %collective-permute-start.12 = (bf16[16,1536]{1,0:T(8,128)(2,1)S(1)}, bf16[16,1536]{1,0:T(8,128)(2,1)S(1)}, u32[]{:S(2)}, u32[]{:S(2)}) collective-permute-start(bf16[16,1536]{1,0:T(8,128)(2,1)S(1)} %over_slides.2.own_ref), channel_id=1, source_target_pairs={{0,192},{32,224},{64,0},{96,32},{128,64},{160,96},{192,128},{224,1... | collective-permute-start | bytes 147464 | tf_op jit(solution)/shard_map/over_slides/ppermute | solution.py:591
  76.4 5.6 %collective-permute-start.11 = (bf16[16,1536]{1,0:T(8,128)(2,1)S(1)}, bf16[16,1536]{1,0:T(8,128)(2,1)S(1)}, u32[]{:S(2)}, u32[]{:S(2)}) collective-permute-start(bf16[16,1536]{1,0:T(8,128)(2,1)S(1)} %over_slides.2.own_ref), channel_id=1, source_target_pairs={{0,128},{32,160},{64,192},{96,224},{128,0},{160,32},{192,64},{224,... | collective-permute-start | bytes 147464 | tf_op jit(solution)/shard_map/over_slides/ppermute | solution.py:591
  77.0 5.5 %collective-permute-start.10 = (bf16[16,1536]{1,0:T(8,128)(2,1)S(1)}, bf16[16,1536]{1,0:T(8,128)(2,1)S(1)}, u32[]{:S(2)}, u32[]{:S(2)}) collective-permute-start(bf16[16,1536]{1,0:T(8,128)(2,1)S(1)} %over_slides.2.own_ref), channel_id=1, source_target_pairs={{0,64},{32,96},{64,128},{96,160},{128,192},{160,224},{192,0},{224,... | collective-permute-start | bytes 147464 | tf_op jit(solution)/shard_map/over_slides/ppermute | solution.py:591

commit v7 on v6

--- a/solution.py
+++ b/solution.py
@@ -575,7 +575,7 @@
         parts = call(
             first_sum_kernel, (shape(size, wide),) + (shape(size, wide, dtype=BF16),) * 3
         )(keep, sent)
-        got = [lax.ppermute(parts[step], "tile", x_pairs(step)) for step in (1, 2, 3)]
+        got = [lax.ppermute(parts[step], "tile", x_pairs(step)) for step in (2, 1, 3)]
         size = size // 4
         parts = call(
             next_sum_kernel, (shape(size, wide),) + (shape(size, wide, dtype=BF16),) * 3

time: 83.5 us -> 83.2 us (level)
  waiting for transfers between devices: 19.9 us -> 18.9 us
    ppermute x3, waiting for transfers between devices: 7.14 us -> 6.22 us  [per_device(): lax.ppermute(parts[step], 'tile', x_pairs(step))]
  transfers between devices with their start and end apart: 13 -> 13, of which waited for: 9 -> 10; matrix products, arithmetic and copies ran while one was open for 0% -> 0% of each run, Pallas kernels for 4% -> 4%
where the time goes in v7:
time: 83.2 us; the launch traced here: 83 us
  blocking collectives  27.2 us (33%)
  starting transfers between devices  23.5 us (28%)
  waiting for transfers between devices  18.9 us (23%)
  Pallas kernels  9.2 us (11%)
  local copies, waits for them, and re-layouts  3.25 us (4%)
  between operations  0.85 us (1%)
    all_to_all x1, blocking collectives, per_device(): stats = lax.all_to_all(stats, 'tile', 0, 0, tiled=True)  15.7 us
    all_to_all x1, blocking collectives, per_device(): head = lax.all_to_all(head, 'tile', 0, 0, tiled=True)  11.5 us
    ppermute x3, waiting for transfers between devices, per_device(): lax.ppermute(parts[step], 'tile', x_pairs(step))  6.22 us
    ppermute x1, starting transfers between devices, per_device(): other = lax.ppermute(own, 'slide', [(i, i ^ 1) for i in range(slides)])  5.47 us
    ppermute x3, starting transfers between devices, per_device(): lax.ppermute(own, 'slide', [(i, (i + 2 * step) % slides) for i in range(s...  4.69 us
    ppermute x3, starting transfers between devices, per_device(): lax.ppermute(parts[step], 'tile', x_pairs(step))  4.66 us
    ppermute x3, waiting for transfers between devices, per_device(): lax.ppermute(own, 'slide', [(i, (i + 2 * step) % slides) for i in range(s...  4.52 us
    ppermute x3, starting transfers between devices, per_device(): lax.ppermute(parts[step], 'tile', z_pairs(step))  4.18 us
  transfers between devices with their start and end apart: 13, of which 10 were waited for; matrix products, arithmetic and copies ran while one was open for 0% of the time, Pallas kernels for 4%

profile of v7, /device:TPU:32, one launch (start us, length us, event | category | flops | bytes accessed | tf_op | source)
XLA Modules:
  0.0 83.0 jit_solution(16222234282485807928)
XLA Ops:
  0.7 1.0 %constant_dynamic-slice_fusion = (bf16[128,256]{1,0:T(8,128)(2,1)S(1)}, bf16[128,256]{1,0:T(8,128)(2,1)S(1)}) fusion(bf16[512,256]{1,0:T(8,128)(2,1)} %bitcast.25, u32[]{:T(128)S(6)} %mul.15, u32[]{:T(128)S(6)} %mul.13), kind=kLoop, calls=%fused_computation.2 | loop fusion | bytes 262152 | tf_op jit(solution)/shard_map/halo/dynamic_slice | solution.py:525
  1.7 1.0 %constant_dynamic-slice_fusion.1 = (bf16[256,256]{1,0:T(8,128)(2,1)S(1)}, bf16[256,256]{1,0:T(8,128)(2,1)S(1)}) fusion(bf16[2048,256]{1,0:T(8,128)(2,1)} %bitcast.23, u32[]{:T(128)S(6)} %mul.14, u32[]{:T(128)S(6)} %mul.12), kind=kLoop, calls=%fused_computation.3 | loop fusion | bytes 524296 | tf_op jit(solution)/shard_map/halo/dynamic_slice | solution.py:525
  2.7 1.9 %collective-permute-start = (bf16[384,256]{1,0:T(8,128)(2,1)S(1)}, bf16[384,256]{1,0:T(8,128)(2,1)S(1)}, u32[]{:S(2)}, u32[]{:S(2)}) collective-permute-start(bf16[384,256]{1,0:T(8,128)(2,1)S(1)} %pad_maximum_fusion), channel_id=1, source_target_pairs={{1,2},{2,1},{3,4},{4,3},{5,6},{6,5},{7,8},{8,7},{9,10},{10,9},{11,... | collective-permute-start | bytes 589832 | tf_op jit(solution)/shard_map/halo/ppermute | solution.py:529
  4.7 2.1 %collective-permute-start.1 = (bf16[384,256]{1,0:T(8,128)(2,1)S(1)}, bf16[384,256]{1,0:T(8,128)(2,1)S(1)}, u32[]{:S(2)}, u32[]{:S(2)}) collective-permute-start(bf16[384,256]{1,0:T(8,128)(2,1)S(1)} %pad_maximum_fusion.1), channel_id=1, source_target_pairs={{0,1},{1,0},{2,3},{3,2},{4,5},{5,4},{6,7},{7,6},{8,9},{9,8},{10,11... | collective-permute-start | bytes 589832 | tf_op jit(solution)/shard_map/halo/ppermute | solution.py:530
  6.9 1.2 %copy-done.2 = bf16[1,8,256,256]{3,2,1,0:T(8,128)(2,1)S(1)} copy-done((bf16[1,8,256,256]{3,2,1,0:T(8,128)(2,1)S(1)}, bf16[1,8,256,256]{3,2,1,0:T(8,128)(2,1)}, u32[]{:S(2)}) %copy-start.2) | copy-done | bytes 1048600
  8.1 3.0 %forward.2 = (f32[2560,128]{1,0:T(8,128)S(1)}, bf16[256,2560]{1,0:T(8,128)(2,1)S(1)}, f32[16,128]{1,0:T(8,128)S(1)}, f32[8,128]{1,0:T(8,128)S(1)}) custom-call(bf16[2048,256]{1,0:T(8,128)(2,1)S(1)} %bitcast.24, bf16[512,256]{1,0:T(8,128)(2,1)S(1)} %bitcast.26, bf16[9,256,128]{2,1,0:T(8,128)(2,1)S(1)} %bitcast.19, bf16[9,256,128]{2,1,0:T(8,128)(2,1)S(1)} %bitcast.21, ...), custom_call_target="tpu_custom_call" | custom-call | tf_op jit(solution)/shard_map/forward/pallas_call | solution.py:533
  11.7 15.7 %all_to_all.22 = f32[32,1,128]{2,1,0:T(1,128)S(1)} all-to-all(f32[32,1,128]{2,1,0:T(1,128)S(1)} %bitcast.31), channel_id=1, replica_groups=mesh['slide'=8,'tile'=32] {'tile'}, dimensions={0} | all-to-all | bytes 32768 | tf_op jit(solution)/shard_map/forward_sums/all_to_all | solution.py:548
  27.4 1.7 %loss_and_head.1 = (f32[2560,128]{1,0:T(8,128)S(1)}, bf16[512,128]{1,0:T(8,128)(2,1)S(1)}) custom-call(f32[2560,128]{1,0:T(8,128)S(1)} %get-tuple-element.25.part_ref.conv_ref.all_conv_ref, f32[768,128]{1,0:T(8,128)S(1)} %get-tuple-element.27.edges_ref, f32[32,128]{1,0:T(8,128)S(1)} %bitcast.28, f32[16,128]{1,0:T(8,128)S(1)} %get-tuple-element.29.vectors_ref, ...), custom_call_target="tpu_custom_call" | custom-call | tf_op jit(solution)/shard_map/loss_and_head/pallas_call | solution.py:550
  29.1 11.5 %all_to_all.23 = bf16[32,16,128]{2,1,0:T(8,128)(2,1)S(1)} all-to-all(bf16[32,16,128]{2,1,0:T(8,128)(2,1)S(1)} %bitcast.30), channel_id=1, replica_groups=mesh['slide'=8,'tile'=32] {'tile'}, dimensions={0} | all-to-all | bytes 262144 | tf_op jit(solution)/shard_map/backward_sums/all_to_all | solution.py:556
  40.6 2.9 %weight_grads.1 = (f32[256,1152]{1,0:T(8,128)S(1)}, bf16[256,1152]{1,0:T(8,128)(2,1)S(1)}, f32[16,128]{1,0:T(8,128)S(1)}) custom-call(f32[2560,128]{1,0:T(8,128)S(1)} %get-tuple-element.25.part_ref.conv_ref.all_conv_ref, f32[768,128]{1,0:T(8,128)S(1)} %get-tuple-element.27.edges_ref, f32[2560,128]{1,0:T(8,128)S(1)} %get-tuple-element.30.all_dpre_ref, ...), custom_call_target="tpu_custom_call" | custom-call | tf_op jit(solution)/shard_map/weight_grads/pallas_call | solution.py:559
  44.0 1.6 %collective-permute-done.2.sent_ref = bf16[256,1152]{1,0:T(8,128)(2,1)S(1)} collective-permute-done((bf16[256,1152]{1,0:T(8,128)(2,1)S(1)}, bf16[256,1152]{1,0:T(8,128)(2,1)S(1)}, u32[]{:S(2)}, u32[]{:S(2)}) %collective-permute-start.2) | collective-permute-done | bytes 589856 | tf_op jit(solution)/shard_map/over_tiles/ppermute | solution.py:573
  45.8 1.4 %collective-permute-start.3 = (bf16[64,1152]{1,0:T(8,128)(2,1)S(1)}, bf16[64,1152]{1,0:T(8,128)(2,1)S(1)}, u32[]{:S(2)}, u32[]{:S(2)}) collective-permute-start(bf16[64,1152]{1,0:T(8,128)(2,1)S(1)} %get-tuple-element.36), channel_id=1, source_target_pairs={{0,16},{1,17},{2,18},{3,19},{4,20},{5,21},{6,22},{7,23},{8,24},{9,... | collective-permute-start | bytes 442376 | tf_op jit(solution)/shard_map/over_tiles/ppermute | solution.py:578
  47.8 2.6 %collective-permute-start.5 = (bf16[64,1152]{1,0:T(8,128)(2,1)S(1)}, bf16[64,1152]{1,0:T(8,128)(2,1)S(1)}, u32[]{:S(2)}, u32[]{:S(2)}) collective-permute-start(bf16[64,1152]{1,0:T(8,128)(2,1)S(1)} %get-tuple-element.38), channel_id=1, source_target_pairs={{0,24},{1,25},{2,26},{3,27},{4,28},{5,29},{6,30},{7,31},{8,0},{9,1... | collective-permute-start | bytes 442376 | tf_op jit(solution)/shard_map/over_tiles/ppermute | solution.py:578
  50.4 3.7 %collective-permute-done.3.one_ref = bf16[64,1152]{1,0:T(8,128)(2,1)S(1)} collective-permute-done((bf16[64,1152]{1,0:T(8,128)(2,1)S(1)}, bf16[64,1152]{1,0:T(8,128)(2,1)S(1)}, u32[]{:S(2)}, u32[]{:S(2)}) %collective-permute-start.3) | collective-permute-done | bytes 147488 | tf_op jit(solution)/shard_map/over_tiles/ppermute | solution.py:578
  54.1 2.6 %collective-permute-done.4.two_ref = bf16[64,1152]{1,0:T(8,128)(2,1)S(1)} collective-permute-done((bf16[64,1152]{1,0:T(8,128)(2,1)S(1)}, bf16[64,1152]{1,0:T(8,128)(2,1)S(1)}, u32[]{:S(2)}, u32[]{:S(2)}) %collective-permute-start.4) | collective-permute-done | bytes 147488 | tf_op jit(solution)/shard_map/over_tiles/ppermute | solution.py:578
  56.7 0.8 collective-permute-start.6
  57.5 3.4 %collective-permute-start.7 = (bf16[16,1152]{1,0:T(8,128)(2,1)S(1)}, bf16[16,1152]{1,0:T(8,128)(2,1)S(1)}, u32[]{:S(2)}, u32[]{:S(2)}) collective-permute-start(bf16[16,1152]{1,0:T(8,128)(2,1)S(1)} %get-tuple-element.41), channel_id=1, source_target_pairs={{0,4},{1,5},{2,6},{3,7},{4,0},{5,1},{6,2},{7,3},{8,12},{9,13},{10,... | collective-permute-start | bytes 110600 | tf_op jit(solution)/shard_map/over_tiles/ppermute | solution.py:583
  61.3 2.3 %collective-permute-done.7.two_ref = bf16[16,1152]{1,0:T(8,128)(2,1)S(1)} collective-permute-done((bf16[16,1152]{1,0:T(8,128)(2,1)S(1)}, bf16[16,1152]{1,0:T(8,128)(2,1)S(1)}, u32[]{:S(2)}, u32[]{:S(2)}) %collective-permute-start.7) | collective-permute-done | bytes 36896 | tf_op jit(solution)/shard_map/over_tiles/ppermute | solution.py:583
  63.5 1.3 %collective-permute-done.8.three_ref = bf16[16,1152]{1,0:T(8,128)(2,1)S(1)} collective-permute-done((bf16[16,1152]{1,0:T(8,128)(2,1)S(1)}, bf16[16,1152]{1,0:T(8,128)(2,1)S(1)}, u32[]{:S(2)}, u32[]{:S(2)}) %collective-permute-start.8) | collective-permute-done | bytes 36896 | tf_op jit(solution)/shard_map/over_tiles/ppermute | solution.py:583
  64.9 5.5 %collective-permute-start.9 = (bf16[16,1536]{1,0:T(8,128)(2,1)S(1)}, bf16[16,1536]{1,0:T(8,128)(2,1)S(1)}, u32[]{:S(2)}, u32[]{:S(2)}) collective-permute-start(bf16[16,1536]{1,0:T(8,128)(2,1)S(1)} %over_tiles.5.own_ref), channel_id=1, source_target_pairs={{0,32},{32,0},{64,96},{96,64},{128,160},{160,128},{192,224},{224,1... | collective-permute-start | bytes 147464 | tf_op jit(solution)/shard_map/over_slides/ppermute | solution.py:588
  70.4 2.6 %collective-permute-done.9.other_ref = bf16[16,1536]{1,0:T(8,128)(2,1)S(1)} collective-permute-done((bf16[16,1536]{1,0:T(8,128)(2,1)S(1)}, bf16[16,1536]{1,0:T(8,128)(2,1)S(1)}, u32[]{:S(2)}, u32[]{:S(2)}) %collective-permute-start.9) | collective-permute-done | bytes 49184 | tf_op jit(solution)/shard_map/over_slides/ppermute | solution.py:588
  73.0 3.1 %collective-permute-start.12 = (bf16[16,1536]{1,0:T(8,128)(2,1)S(1)}, bf16[16,1536]{1,0:T(8,128)(2,1)S(1)}, u32[]{:S(2)}, u32[]{:S(2)}) collective-permute-start(bf16[16,1536]{1,0:T(8,128)(2,1)S(1)} %over_slides.2.own_ref), channel_id=1, source_target_pairs={{0,192},{32,224},{64,0},{96,32},{128,64},{160,96},{192,128},{224,1... | collective-permute-start | bytes 147464 | tf_op jit(solution)/shard_map/over_slides/ppermute | solution.py:591
  76.7 1.0 %collective-permute-start.10 = (bf16[16,1536]{1,0:T(8,128)(2,1)S(1)}, bf16[16,1536]{1,0:T(8,128)(2,1)S(1)}, u32[]{:S(2)}, u32[]{:S(2)}) collective-permute-start(bf16[16,1536]{1,0:T(8,128)(2,1)S(1)} %over_slides.2.own_ref), channel_id=1, source_target_pairs={{0,64},{32,96},{64,128},{96,160},{128,192},{160,224},{192,0},{224,... | collective-permute-start | bytes 147464 | tf_op jit(solution)/shard_map/over_slides/ppermute | solution.py:591
  77.8 3.9 %collective-permute-done.11.two_ref = bf16[16,1536]{1,0:T(8,128)(2,1)S(1)} collective-permute-done((bf16[16,1536]{1,0:T(8,128)(2,1)S(1)}, bf16[16,1536]{1,0:T(8,128)(2,1)S(1)}, u32[]{:S(2)}, u32[]{:S(2)}) %collective-permute-start.11) | collective-permute-done | bytes 49184 | tf_op jit(solution)/shard_map/over_slides/ppermute | solution.py:591
  (39 shorter events, 4.5 us)
Async XLA Ops:
  0.6 6.2 %copy-start.3 = (bf16[1,4,128,256]{3,2,1,0:T(8,128)(2,1)S(1)}, bf16[1,4,128,256]{3,2,1,0:T(8,128)(2,1)}, u32[]{:S(2)}) copy-start(bf16[1,4,128,256]{3,2,1,0:T(8,128)(2,1)} %param.12) | copy-start | bytes 786436
  0.6 6.2 %copy-start.10 = (f32[8]{0:T(128)S(1)}, f32[8]{0:T(128)}, u32[]{:S(2)}) copy-start(f32[8]{0:T(128)} %bias_ref.1) | copy-start | bytes 100
  0.7 6.2 %copy-start.9 = (f32[128]{0:T(128)S(1)}, f32[128]{0:T(128)}, u32[]{:S(2)}) copy-start(f32[128]{0:T(128)} %param.18) | copy-start | bytes 1540
  0.7 6.1 %copy-start.8 = (f32[128]{0:T(128)S(1)}, f32[128]{0:T(128)}, u32[]{:S(2)}) copy-start(f32[128]{0:T(128)} %param.17) | copy-start | bytes 1540
  0.7 6.1 %copy-start.7 = (f32[128]{0:T(128)S(1)}, f32[128]{0:T(128)}, u32[]{:S(2)}) copy-start(f32[128]{0:T(128)} %param.16) | copy-start | bytes 1540
  0.7 6.1 %copy-start.6 = (f32[128]{0:T(128)S(1)}, f32[128]{0:T(128)}, u32[]{:S(2)}) copy-start(f32[128]{0:T(128)} %param.15) | copy-start | bytes 1540
  0.7 6.1 %copy-start.1 = (bf16[256,9,128]{2,0,1:T(8,128)(2,1)S(1)}, bf16[256,9,128]{2,0,1:T(8,128)(2,1)}, u32[]{:S(2)}) copy-start(bf16[256,9,128]{2,0,1:T(8,128)(2,1)} %param.14) | copy-start | bytes 1769476
  0.7 6.1 %copy-start = (bf16[256,9,128]{2,0,1:T(8,128)(2,1)S(1)}, bf16[256,9,128]{2,0,1:T(8,128)(2,1)}, u32[]{:S(2)}) copy-start(bf16[256,9,128]{2,0,1:T(8,128)(2,1)} %param.13) | copy-start | bytes 1769476
  2.7 8.3 %collective-permute-start = (bf16[384,256]{1,0:T(8,128)(2,1)S(1)}, bf16[384,256]{1,0:T(8,128)(2,1)S(1)}, u32[]{:S(2)}, u32[]{:S(2)}) collective-permute-start(bf16[384,256]{1,0:T(8,128)(2,1)S(1)} %pad_maximum_fusion), channel_id=1, source_target_pairs={{1,2},{2,1},{3,4},{4,3},{5,6},{6,5},{7,8},{8,7},{9,10},{10,9},{11,... | collective-permute-start | bytes 589832 | tf_op jit(solution)/shard_map/halo/ppermute | solution.py:529
  4.7 6.4 %collective-permute-start.1 = (bf16[384,256]{1,0:T(8,128)(2,1)S(1)}, bf16[384,256]{1,0:T(8,128)(2,1)S(1)}, u32[]{:S(2)}, u32[]{:S(2)}) collective-permute-start(bf16[384,256]{1,0:T(8,128)(2,1)S(1)} %pad_maximum_fusion.1), channel_id=1, source_target_pairs={{0,1},{1,0},{2,3},{3,2},{4,5},{5,4},{6,7},{7,6},{8,9},{9,8},{10,11... | collective-permute-start | bytes 589832 | tf_op jit(solution)/shard_map/halo/ppermute | solution.py:530
  6.9 1.2 %copy-start.2 = (bf16[1,8,256,256]{3,2,1,0:T(8,128)(2,1)S(1)}, bf16[1,8,256,256]{3,2,1,0:T(8,128)(2,1)}, u32[]{:S(2)}) copy-start(bf16[1,8,256,256]{3,2,1,0:T(8,128)(2,1)} %param.11) | copy-start | bytes 3145732
  11.1 16.3 %copy-start.4 = (s32[1,8,256]{2,1,0:T(8,128)S(1)}, s32[1,8,256]{2,1,0:T(8,128)}, u32[]{:S(2)}) copy-start(s32[1,8,256]{2,1,0:T(8,128)} %param.21) | copy-start | bytes 24580
  11.1 16.3 %copy-start.5 = (bf16[8,128]{1,0:T(8,128)(2,1)S(1)}, bf16[8,128]{1,0:T(8,128)(2,1)}, u32[]{:S(2)}) copy-start(bf16[8,128]{1,0:T(8,128)(2,1)} %class_ref.1) | copy-start | bytes 6148
  43.5 2.1 %collective-permute-start.2 = (bf16[256,1152]{1,0:T(8,128)(2,1)S(1)}, bf16[256,1152]{1,0:T(8,128)(2,1)S(1)}, u32[]{:S(2)}, u32[]{:S(2)}) collective-permute-start(bf16[256,1152]{1,0:T(8,128)(2,1)S(1)} %get-tuple-element.34), channel_id=1, source_target_pairs={{0,1},{1,0},{2,3},{3,2},{4,5},{5,4},{6,7},{7,6},{8,9},{9,8},{10,11... | collective-permute-start | bytes 1769480 | tf_op jit(solution)/shard_map/over_tiles/ppermute | solution.py:573
  45.8 8.3 %collective-permute-start.3 = (bf16[64,1152]{1,0:T(8,128)(2,1)S(1)}, bf16[64,1152]{1,0:T(8,128)(2,1)S(1)}, u32[]{:S(2)}, u32[]{:S(2)}) collective-permute-start(bf16[64,1152]{1,0:T(8,128)(2,1)S(1)} %get-tuple-element.36), channel_id=1, source_target_pairs={{0,16},{1,17},{2,18},{3,19},{4,20},{5,21},{6,22},{7,23},{8,24},{9,... | collective-permute-start | bytes 442376 | tf_op jit(solution)/shard_map/over_tiles/ppermute | solution.py:578
  47.2 9.5 %collective-permute-start.4 = (bf16[64,1152]{1,0:T(8,128)(2,1)S(1)}, bf16[64,1152]{1,0:T(8,128)(2,1)S(1)}, u32[]{:S(2)}, u32[]{:S(2)}) collective-permute-start(bf16[64,1152]{1,0:T(8,128)(2,1)S(1)} %get-tuple-element.37), channel_id=1, source_target_pairs={{0,8},{1,9},{2,10},{3,11},{4,12},{5,13},{6,14},{7,15},{8,16},{9,17... | collective-permute-start | bytes 442376 | tf_op jit(solution)/shard_map/over_tiles/ppermute | solution.py:578
  47.8 8.8 %collective-permute-start.5 = (bf16[64,1152]{1,0:T(8,128)(2,1)S(1)}, bf16[64,1152]{1,0:T(8,128)(2,1)S(1)}, u32[]{:S(2)}, u32[]{:S(2)}) collective-permute-start(bf16[64,1152]{1,0:T(8,128)(2,1)S(1)} %get-tuple-element.38), channel_id=1, source_target_pairs={{0,24},{1,25},{2,26},{3,27},{4,28},{5,29},{6,30},{7,31},{8,0},{9,1... | collective-permute-start | bytes 442376 | tf_op jit(solution)/shard_map/over_tiles/ppermute | solution.py:578
  56.7 4.5 %collective-permute-start.6 = (bf16[16,1152]{1,0:T(8,128)(2,1)S(1)}, bf16[16,1152]{1,0:T(8,128)(2,1)S(1)}, u32[]{:S(2)}, u32[]{:S(2)}) collective-permute-start(bf16[16,1152]{1,0:T(8,128)(2,1)S(1)} %get-tuple-element.40), channel_id=1, source_target_pairs={{0,2},{1,3},{2,4},{3,5},{4,6},{5,7},{6,0},{7,1},{8,10},{9,11},{10,... | collective-permute-start | bytes 110600 | tf_op jit(solution)/shard_map/over_tiles/ppermute | solution.py:583
  57.5 6.0 %collective-permute-start.7 = (bf16[16,1152]{1,0:T(8,128)(2,1)S(1)}, bf16[16,1152]{1,0:T(8,128)(2,1)S(1)}, u32[]{:S(2)}, u32[]{:S(2)}) collective-permute-start(bf16[16,1152]{1,0:T(8,128)(2,1)S(1)} %get-tuple-element.41), channel_id=1, source_target_pairs={{0,4},{1,5},{2,6},{3,7},{4,0},{5,1},{6,2},{7,3},{8,12},{9,13},{10,... | collective-permute-start | bytes 110600 | tf_op jit(solution)/shard_map/over_tiles/ppermute | solution.py:583
  60.9 4.0 %collective-permute-start.8 = (bf16[16,1152]{1,0:T(8,128)(2,1)S(1)}, bf16[16,1152]{1,0:T(8,128)(2,1)S(1)}, u32[]{:S(2)}, u32[]{:S(2)}) collective-permute-start(bf16[16,1152]{1,0:T(8,128)(2,1)S(1)} %get-tuple-element.42), channel_id=1, source_target_pairs={{0,6},{1,7},{2,0},{3,1},{4,2},{5,3},{6,4},{7,5},{8,14},{9,15},{10,... | collective-permute-start | bytes 110600 | tf_op jit(solution)/shard_map/over_tiles/ppermute | solution.py:583
  64.9 8.1 %collective-permute-start.9 = (bf16[16,1536]{1,0:T(8,128)(2,1)S(1)}, bf16[16,1536]{1,0:T(8,128)(2,1)S(1)}, u32[]{:S(2)}, u32[]{:S(2)}) collective-permute-start(bf16[16,1536]{1,0:T(8,128)(2,1)S(1)} %over_tiles.5.own_ref), channel_id=1, source_target_pairs={{0,32},{32,0},{64,96},{96,64},{128,160},{160,128},{192,224},{224,1... | collective-permute-start | bytes 147464 | tf_op jit(solution)/shard_map/over_slides/ppermute | solution.py:588
  73.0 4.8 %collective-permute-start.12 = (bf16[16,1536]{1,0:T(8,128)(2,1)S(1)}, bf16[16,1536]{1,0:T(8,128)(2,1)S(1)}, u32[]{:S(2)}, u32[]{:S(2)}) collective-permute-start(bf16[16,1536]{1,0:T(8,128)(2,1)S(1)} %over_slides.2.own_ref), channel_id=1, source_target_pairs={{0,192},{32,224},{64,0},{96,32},{128,64},{160,96},{192,128},{224,1... | collective-permute-start | bytes 147464 | tf_op jit(solution)/shard_map/over_slides/ppermute | solution.py:591
  76.1 5.6 %collective-permute-start.11 = (bf16[16,1536]{1,0:T(8,128)(2,1)S(1)}, bf16[16,1536]{1,0:T(8,128)(2,1)S(1)}, u32[]{:S(2)}, u32[]{:S(2)}) collective-permute-start(bf16[16,1536]{1,0:T(8,128)(2,1)S(1)} %over_slides.2.own_ref), channel_id=1, source_target_pairs={{0,128},{32,160},{64,192},{96,224},{128,0},{160,32},{192,64},{224,... | collective-permute-start | bytes 147464 | tf_op jit(solution)/shard_map/over_slides/ppermute | solution.py:591
  76.7 5.5 %collective-permute-start.10 = (bf16[16,1536]{1,0:T(8,128)(2,1)S(1)}, bf16[16,1536]{1,0:T(8,128)(2,1)S(1)}, u32[]{:S(2)}, u32[]{:S(2)}) collective-permute-start(bf16[16,1536]{1,0:T(8,128)(2,1)S(1)} %over_slides.2.own_ref), channel_id=1, source_target_pairs={{0,64},{32,96},{64,128},{96,160},{128,192},{160,224},{192,0},{224,... | collective-permute-start | bytes 147464 | tf_op jit(solution)/shard_map/over_slides/ppermute | solution.py:591
